TPU v7x, 32 devices: a whole 2x2x4 slice. The times are simulated.
32 devices in a mesh: fsdp: 4 (over x, core), dp: 8 (over z, y).
Axes of the slice: x: 2, y: 2, z: 4, core: 2. Of those that a mesh axis runs over, the one named last changes fastest.
Arguments:
- tokens: bfloat16 [32, 1024, 768], P(('fsdp', 'dp')), may hold values from -6 to 6
- lengths: int32 [32], P(('fsdp', 'dp')), may hold values from 256 to 1024, as said below
- neighbours: bfloat16 [1024, 128, 768], P(('fsdp', 'dp')), may hold values from -6 to 6
- neighbour_ids: int32 [32, 16, 2], P(('fsdp', 'dp')), may hold values from 0 to 31
- neighbour_lengths: int32 [1024], P(('fsdp', 'dp')), may hold values from 32 to 128
- first_gain: bfloat16 [768], P(('fsdp', 'dp')), may hold values from 0.5 to 1.5
- first_shift: bfloat16 [768], P(('fsdp', 'dp')), may hold values from -3 to 3
- self_input: bfloat16 [768, 2304], P(('fsdp', 'dp')), may hold values from -0.21875 to 0.21875
- self_output: bfloat16 [768, 768], P(('fsdp', 'dp')), may hold values from -3.5 to 3.5
- second_gain: bfloat16 [768], P(('fsdp', 'dp')), may hold values from 0.5 to 1.5
- second_shift: bfloat16 [768], P(('fsdp', 'dp')), may hold values from -3 to 3
- cross_query: bfloat16 [768, 768], P(('fsdp', 'dp')), may hold values from -0.21875 to 0.21875
- cross_keyval: bfloat16 [768, 1536], P(('fsdp', 'dp')), may hold values from -0.21875 to 0.21875
- cross_output: bfloat16 [768, 768], P(('fsdp', 'dp')), may hold values from -2.5 to 2.5
- third_gain: bfloat16 [768], P(('fsdp', 'dp')), may hold values from 0.5 to 1.5
- third_shift: bfloat16 [768], P(('fsdp', 'dp')), may hold values from -3 to 3
- feed_up: bfloat16 [768, 3072], P(('fsdp', 'dp')), may hold values from -0.21875 to 0.21875
- feed_down: bfloat16 [3072, 768], P(('fsdp', 'dp')), may hold values from -0.109375 to 0.109375
- cotangent: bfloat16 [32, 1024, 768], P(('fsdp', 'dp')), may hold values from -6 to 6
Outputs:
- block_out: bfloat16 [32, 1024, 768], P(('fsdp', 'dp'))
- tokens_grad: float32 [32, 1024, 768], P(('fsdp', 'dp'))
- neighbours_grad: float32 [1024, 128, 768], P(('fsdp', 'dp'))
- firstgain_grad: float32 [768], P(('fsdp', 'dp'))
- firstshift_grad: float32 [768], P(('fsdp', 'dp'))
- selfinput_grad: float32 [768, 2304], P(('fsdp', 'dp'))
- selfoutput_grad: float32 [768, 768], P(('fsdp', 'dp'))
- secondgain_grad: float32 [768], P(('fsdp', 'dp'))
- secondshift_grad: float32 [768], P(('fsdp', 'dp'))
- crossquery_grad: float32 [768, 768], P(('fsdp', 'dp'))
- crosskeyval_grad: float32 [768, 1536], P(('fsdp', 'dp'))
- crossoutput_grad: float32 [768, 768], P(('fsdp', 'dp'))
- thirdgain_grad: float32 [768], P(('fsdp', 'dp'))
- thirdshift_grad: float32 [768], P(('fsdp', 'dp'))
- feedup_grad: float32 [768, 3072], P(('fsdp', 'dp'))
- feeddown_grad: float32 [3072, 768], P(('fsdp', 'dp'))
Inputs may be any that keep to these rules, and one draw needn't show every extreme that they name: `lengths`: positions at or past a sequence's length are padding; some sequence has all 1024 tokens. Slot j of span c of sequence s is filled by row (s) * 32 + neighbour_ids[s, c, j] of neighbours, held with the sequence; an encoded neighbour may fill several slots or none.
All inputs are finite; a program needn't handle non-finite values.
Results may differ from a plain program's by a relative error of at most 0.017.
Values may be sent and summed in bfloat16 or wider, within the bound.
No kernel may reach another device: no remote copies, remote signals or barrier semaphores. Data moves between devices by JAX's collectives and lax.ppermute only.
A program may use at most 384 MiB of HBM per device.

v0:
```python
import jax
import jax.numpy as jnp
from jax import lax
from jax.sharding import PartitionSpec as P

HEADS = 12
SPAN = 64
NEIGH = 2


EPSILON = 1e-05
SCALE = 0.125
NEGATIVE = -1e30


def norm_apply(values, gain, shift):
    centre = jnp.mean(values, axis=-1, keepdims=True)
    centred = values - centre
    spread = jnp.mean(centred * centred, axis=-1, keepdims=True)
    return centred * lax.rsqrt(spread + EPSILON) * gain + shift


def norm_back(values, gain, shift, upstream):
    result, pullback = jax.vjp(norm_apply, values, gain, shift)
    return pullback(upstream)


def gelu_tanh(values):
    return jax.nn.gelu(values, approximate=True)


def split_heads(matrix):
    return matrix.reshape(matrix.shape[:-1] + (HEADS, matrix.shape[-1] // HEADS))


def pack_terms(terms, owners):
    return jnp.concatenate([term.reshape(owners, -1) for term in terms], axis=1)


def unpack_terms(packed, terms, owners):
    results = []
    offset = 0
    for term in terms:
        width = term.size // owners
        piece = packed[0, offset : offset + width]
        results.append(piece.reshape((term.shape[0] // owners,) + term.shape[1:]))
        offset = offset + width
    return tuple(results)


def self_scores(query_block, key_heads, start, valid):
    raw = (
        jnp.einsum("sqhe,skhe->shqk", query_block, key_heads, preferred_element_type=jnp.float32)
        * SCALE
    )
    rows = start + jnp.arange(query_block.shape[1], dtype=jnp.int32)
    columns = jnp.arange(key_heads.shape[1], dtype=jnp.int32)
    allowed = (columns[None, :] <= rows[:, None])[None, None] & valid[:, None, None, :]
    return (raw, allowed)


def self_forward(query_heads, key_heads, value_heads, valid, block):
    count = query_heads.shape[1] // block

    def step(index):
        start = index * block
        query_block = lax.dynamic_slice_in_dim(query_heads, start, block, 1)
        raw, allowed = self_scores(query_block, key_heads, start, valid)
        masked = jnp.where(allowed, raw, NEGATIVE)
        top = jnp.max(masked, axis=-1, keepdims=True)
        expo = jnp.exp(masked - top)
        total = jnp.sum(expo, axis=-1, keepdims=True)
        soft = (expo / total).astype(jnp.bfloat16)
        mixed = jnp.einsum("shqk,skhe->sqhe", soft, value_heads, preferred_element_type=jnp.float32)
        return (mixed, (top + jnp.log(total))[..., 0])

    return lax.map(step, jnp.arange(count, dtype=jnp.int32))


def self_backward(query_heads, key_heads, value_heads, valid, grad_heads, logsum, block):
    count = query_heads.shape[1] // block

    def step(carry, item):
        key_grad, value_grad = carry
        index, block_logsum = item
        start = index * block
        query_block = lax.dynamic_slice_in_dim(query_heads, start, block, 1)
        grad_block = lax.dynamic_slice_in_dim(grad_heads, start, block, 1)
        raw, allowed = self_scores(query_block, key_heads, start, valid)
        soft = jnp.where(allowed, jnp.exp(raw - block_logsum[..., None]), 0.0)
        value_grad = value_grad + jnp.einsum(
            "shqk,sqhe->skhe",
            soft.astype(jnp.bfloat16),
            grad_block,
            preferred_element_type=jnp.float32,
        )
        prob_grad = jnp.einsum(
            "sqhe,skhe->shqk", grad_block, value_heads, preferred_element_type=jnp.float32
        )
        score_grad = (
            soft * (prob_grad - jnp.sum(soft * prob_grad, axis=-1, keepdims=True))
        ).astype(jnp.bfloat16)
        query_rows_gradient = (
            jnp.einsum("shqk,skhe->sqhe", score_grad, key_heads, preferred_element_type=jnp.float32)
            * SCALE
        )
        key_grad = (
            key_grad
            + jnp.einsum(
                "shqk,sqhe->skhe", score_grad, query_block, preferred_element_type=jnp.float32
            )
            * SCALE
        )
        return ((key_grad, value_grad), query_rows_gradient)

    zeroes = jnp.zeros(key_heads.shape, jnp.float32)
    carried, query_grads = lax.scan(
        step, (zeroes, zeroes), (jnp.arange(count, dtype=jnp.int32), logsum)
    )
    return (query_grads, carried[0], carried[1])


def cross_soft(query_spans, key_spans, valid):
    raw = (
        jnp.einsum("scqhe,sckhe->schqk", query_spans, key_spans, preferred_element_type=jnp.float32)
        * SCALE
    )
    masked = jnp.where(valid[:, :, None, None, :], raw, NEGATIVE)
    top = jnp.max(masked, axis=-1, keepdims=True)
    expo = jnp.exp(masked - top)
    return expo / jnp.sum(expo, axis=-1, keepdims=True)


def local(
    tokens,
    lengths,
    neighbours,
    neighbour_ids,
    neighbour_lengths,
    first_gain,
    first_shift,
    self_input,
    self_output,
    second_gain,
    second_shift,
    cross_query,
    cross_keyval,
    cross_output,
    third_gain,
    third_shift,
    feed_up,
    feed_down,
    cotangent,
):
    gathered = (
        lax.all_gather(first_gain, ("fsdp", "dp"), axis=0, tiled=True),
        lax.all_gather(first_shift, ("fsdp", "dp"), axis=0, tiled=True),
        lax.all_gather(self_input, ("fsdp", "dp"), axis=0, tiled=True),
        lax.all_gather(self_output, ("fsdp", "dp"), axis=0, tiled=True),
        lax.all_gather(second_gain, ("fsdp", "dp"), axis=0, tiled=True),
        lax.all_gather(second_shift, ("fsdp", "dp"), axis=0, tiled=True),
        lax.all_gather(cross_query, ("fsdp", "dp"), axis=0, tiled=True),
        lax.all_gather(cross_keyval, ("fsdp", "dp"), axis=0, tiled=True),
        lax.all_gather(cross_output, ("fsdp", "dp"), axis=0, tiled=True),
        lax.all_gather(third_gain, ("fsdp", "dp"), axis=0, tiled=True),
        lax.all_gather(third_shift, ("fsdp", "dp"), axis=0, tiled=True),
        lax.all_gather(feed_up, ("fsdp", "dp"), axis=0, tiled=True),
        lax.all_gather(feed_down, ("fsdp", "dp"), axis=0, tiled=True),
    )
    (
        gain_one,
        shift_one,
        self_attention_input,
        self_attention_output,
        gain_two,
        shift_two,
        cross_query_weight,
        keyval_cross,
        cross_attention_output,
        gain_three,
        shift_three,
        up_projection_weight,
        down_projection_weight,
    ) = gathered
    seq_count, seq_len, width = tokens.shape
    pool_count, neigh_len = (neighbours.shape[0], neighbours.shape[1])
    span_count = seq_len // SPAN
    block = min(512, seq_len)
    residual_stream = tokens.astype(jnp.float32)
    first_norm_input = norm_apply(
        residual_stream, gain_one.astype(jnp.float32), shift_one.astype(jnp.float32)
    ).astype(jnp.bfloat16)
    projected_rows = jnp.einsum(
        "zjx,xc->zjc", first_norm_input, self_attention_input, preferred_element_type=jnp.float32
    ).astype(jnp.bfloat16)
    query_heads = split_heads(projected_rows[..., :width])
    key_heads = split_heads(projected_rows[..., width : 2 * width])
    value_heads = split_heads(projected_rows[..., 2 * width :])
    valid = jnp.arange(seq_len, dtype=jnp.int32)[None, :] < lengths[:, None]
    mixed_blocks, logsum = self_forward(query_heads, key_heads, value_heads, valid, block)
    self_attended = (
        jnp.moveaxis(mixed_blocks, 0, 1).reshape(seq_count, seq_len, width).astype(jnp.bfloat16)
    )
    self_residual_sum = residual_stream + jnp.einsum(
        "zjx,xc->zjc", self_attended, self_attention_output, preferred_element_type=jnp.float32
    )
    second_norm_input = norm_apply(
        self_residual_sum, gain_two.astype(jnp.float32), shift_two.astype(jnp.float32)
    ).astype(jnp.bfloat16)
    pool_keyval = jnp.einsum(
        "pnd,de->pne", neighbours, keyval_cross, preferred_element_type=jnp.float32
    ).astype(jnp.bfloat16)
    matches = neighbour_ids[..., None] == jnp.arange(pool_count, dtype=jnp.int32)
    selector = matches.astype(jnp.bfloat16)
    span_keyval = jnp.einsum(
        "scjp,pne->scjne", selector, pool_keyval, preferred_element_type=jnp.float32
    ).astype(jnp.bfloat16)
    span_keyval = span_keyval.reshape(seq_count, span_count, NEIGH * neigh_len, 2 * width)
    span_keys = split_heads(span_keyval[..., :width])
    span_values = split_heads(span_keyval[..., width:])
    slot_lengths = jnp.sum(jnp.where(matches, neighbour_lengths, 0), axis=-1)
    span_valid = (jnp.arange(neigh_len, dtype=jnp.int32) < slot_lengths[..., None]).reshape(
        seq_count, span_count, NEIGH * neigh_len
    )
    cross_query_rows = jnp.einsum(
        "zjx,xc->zjc", second_norm_input, cross_query_weight, preferred_element_type=jnp.float32
    ).astype(jnp.bfloat16)
    cross_query_rows = split_heads(cross_query_rows.reshape(seq_count, span_count, SPAN, width))
    cross_probs = cross_soft(cross_query_rows, span_keys, span_valid)
    cross_weights = cross_probs.astype(jnp.bfloat16)
    cross_attended = jnp.einsum(
        "schqk,sckhe->scqhe", cross_weights, span_values, preferred_element_type=jnp.float32
    )
    cross_attended = cross_attended.reshape(seq_count, seq_len, width).astype(jnp.bfloat16)
    cross_residual_sum = self_residual_sum + jnp.einsum(
        "zjx,xc->zjc", cross_attended, cross_attention_output, preferred_element_type=jnp.float32
    )
    third_norm_input = norm_apply(
        cross_residual_sum, gain_three.astype(jnp.float32), shift_three.astype(jnp.float32)
    ).astype(jnp.bfloat16)
    hidden_preactivation = jnp.einsum(
        "vtc,cz->vtz", third_norm_input, up_projection_weight, preferred_element_type=jnp.float32
    )
    hidden_activations = gelu_tanh(hidden_preactivation).astype(jnp.bfloat16)
    block_out = (
        cross_residual_sum
        + jnp.einsum(
            "iew,wm->iem",
            hidden_activations,
            down_projection_weight,
            preferred_element_type=jnp.float32,
        )
    ).astype(jnp.bfloat16)
    regathered = (
        lax.all_gather(first_gain, ("fsdp", "dp"), axis=0, tiled=True),
        lax.all_gather(first_shift, ("fsdp", "dp"), axis=0, tiled=True),
        lax.all_gather(self_input, ("fsdp", "dp"), axis=0, tiled=True),
        lax.all_gather(self_output, ("fsdp", "dp"), axis=0, tiled=True),
        lax.all_gather(second_gain, ("fsdp", "dp"), axis=0, tiled=True),
        lax.all_gather(second_shift, ("fsdp", "dp"), axis=0, tiled=True),
        lax.all_gather(cross_query, ("fsdp", "dp"), axis=0, tiled=True),
        lax.all_gather(cross_keyval, ("fsdp", "dp"), axis=0, tiled=True),
        lax.all_gather(cross_output, ("fsdp", "dp"), axis=0, tiled=True),
        lax.all_gather(third_gain, ("fsdp", "dp"), axis=0, tiled=True),
        lax.all_gather(third_shift, ("fsdp", "dp"), axis=0, tiled=True),
        lax.all_gather(feed_up, ("fsdp", "dp"), axis=0, tiled=True),
        lax.all_gather(feed_down, ("fsdp", "dp"), axis=0, tiled=True),
    )
    (
        gain_one,
        shift_one,
        self_attention_input,
        self_attention_output,
        gain_two,
        shift_two,
        cross_query_weight,
        keyval_cross,
        cross_attention_output,
        gain_three,
        shift_three,
        up_projection_weight,
        down_projection_weight,
    ) = regathered
    upstream = cotangent.astype(jnp.float32)
    down_weight_contribution = jnp.einsum(
        "och,ocv->hv", hidden_activations, cotangent, preferred_element_type=jnp.float32
    )
    hidden_back = jnp.einsum(
        "pxh,kh->pxk", cotangent, down_projection_weight, preferred_element_type=jnp.float32
    )
    hidden_activation_gradient = jax.vjp(gelu_tanh, hidden_preactivation)[1](hidden_back)[0].astype(
        jnp.bfloat16
    )
    feedup_term = jnp.einsum(
        "mix,miq->xq",
        third_norm_input,
        hidden_activation_gradient,
        preferred_element_type=jnp.float32,
    )
    third_norm_backward = jnp.einsum(
        "bgx,mx->bgm",
        hidden_activation_gradient,
        up_projection_weight,
        preferred_element_type=jnp.float32,
    )
    cross_grad_in, gainthree_term, shiftthree_term = norm_back(
        cross_residual_sum,
        gain_three.astype(jnp.float32),
        shift_three.astype(jnp.float32),
        third_norm_backward,
    )
    after_cross_grad = upstream + cross_grad_in
    cross_projection_input = after_cross_grad.astype(jnp.bfloat16)
    crossout_term = jnp.einsum(
        "zfv,zfm->vm", cross_attended, cross_projection_input, preferred_element_type=jnp.float32
    )
    mixed_grad = jnp.einsum(
        "ymb,ib->ymi",
        cross_projection_input,
        cross_attention_output,
        preferred_element_type=jnp.float32,
    ).astype(jnp.bfloat16)
    mixed_grad = split_heads(mixed_grad.reshape(seq_count, span_count, SPAN, width))
    value_grad = jnp.einsum(
        "schqk,scqhe->sckhe", cross_weights, mixed_grad, preferred_element_type=jnp.float32
    )
    prob_grad = jnp.einsum(
        "scqhe,sckhe->schqk", mixed_grad, span_values, preferred_element_type=jnp.float32
    )
    score_grad = (
        cross_probs * (prob_grad - jnp.sum(cross_probs * prob_grad, axis=-1, keepdims=True))
    ).astype(jnp.bfloat16)
    query_rows_gradient = (
        jnp.einsum("schqk,sckhe->scqhe", score_grad, span_keys, preferred_element_type=jnp.float32)
        * SCALE
    )
    query_rows_gradient = query_rows_gradient.reshape(seq_count, seq_len, width).astype(
        jnp.bfloat16
    )
    key_grad = (
        jnp.einsum(
            "schqk,scqhe->sckhe", score_grad, cross_query_rows, preferred_element_type=jnp.float32
        )
        * SCALE
    )
    span_grad = jnp.concatenate(
        [
            key_grad.reshape(seq_count, span_count, NEIGH * neigh_len, width),
            value_grad.reshape(seq_count, span_count, NEIGH * neigh_len, width),
        ],
        axis=-1,
    )
    span_grad = span_grad.reshape(seq_count, span_count, NEIGH, neigh_len, 2 * width)
    pool_grad = jnp.einsum(
        "scjp,scjne->pne", matches.astype(jnp.float32), span_grad, precision=lax.Precision.HIGHEST
    ).astype(jnp.bfloat16)
    keyval_term = jnp.einsum(
        "pnd,pne->de", neighbours, pool_grad, preferred_element_type=jnp.float32
    )
    neighbours_grad = jnp.einsum(
        "pne,de->pnd", pool_grad, keyval_cross, preferred_element_type=jnp.float32
    )
    query_term = jnp.einsum(
        "zfv,zfm->vm", second_norm_input, query_rows_gradient, preferred_element_type=jnp.float32
    )
    second_back = jnp.einsum(
        "ymb,ib->ymi", query_rows_gradient, cross_query_weight, preferred_element_type=jnp.float32
    )
    self_grad_in, gaintwo_term, shifttwo_term = norm_back(
        self_residual_sum, gain_two.astype(jnp.float32), shift_two.astype(jnp.float32), second_back
    )
    after_self_grad = after_cross_grad + self_grad_in
    self_projection_input = after_self_grad.astype(jnp.bfloat16)
    selfout_term = jnp.einsum(
        "zfv,zfm->vm", self_attended, self_projection_input, preferred_element_type=jnp.float32
    )
    attend_grad = jnp.einsum(
        "ymb,ib->ymi",
        self_projection_input,
        self_attention_output,
        preferred_element_type=jnp.float32,
    ).astype(jnp.bfloat16)
    query_blocks, key_part, value_part = self_backward(
        query_heads, key_heads, value_heads, valid, split_heads(attend_grad), logsum, block
    )
    query_part = jnp.moveaxis(query_blocks, 0, 1).reshape(seq_count, seq_len, width)
    projected_rows_gradient = jnp.concatenate(
        [
            query_part,
            key_part.reshape(seq_count, seq_len, width),
            value_part.reshape(seq_count, seq_len, width),
        ],
        axis=-1,
    ).astype(jnp.bfloat16)
    selfin_term = jnp.einsum(
        "zfv,zfm->vm", first_norm_input, projected_rows_gradient, preferred_element_type=jnp.float32
    )
    first_back = jnp.einsum(
        "ymb,ib->ymi",
        projected_rows_gradient,
        self_attention_input,
        preferred_element_type=jnp.float32,
    )
    token_grad_in, gainone_term, shiftone_term = norm_back(
        residual_stream, gain_one.astype(jnp.float32), shift_one.astype(jnp.float32), first_back
    )
    tokens_grad = after_self_grad + token_grad_in
    partials = (
        gainone_term,
        shiftone_term,
        selfin_term,
        selfout_term,
        gaintwo_term,
        shifttwo_term,
        query_term,
        keyval_term,
        crossout_term,
        gainthree_term,
        shiftthree_term,
        feedup_term,
        down_weight_contribution,
    )
    owners = lax.axis_size("fsdp") * lax.axis_size("dp")
    packed = pack_terms(partials, owners)
    reduced = lax.psum_scatter(packed, ("fsdp", "dp"), scatter_dimension=0, tiled=True)
    summed = unpack_terms(reduced, partials, owners)
    (
        grad_gainone,
        grad_shiftone,
        grad_selfin,
        grad_selfout,
        grad_gaintwo,
        grad_shifttwo,
        grad_crossq,
        grad_crosskv,
        grad_crossout,
        grad_gainthree,
        grad_shiftthree,
        grad_feedup,
        grad_feeddown,
    ) = summed
    return (
        block_out,
        tokens_grad,
        neighbours_grad,
        grad_gainone,
        grad_shiftone,
        grad_selfin,
        grad_selfout,
        grad_gaintwo,
        grad_shifttwo,
        grad_crossq,
        grad_crosskv,
        grad_crossout,
        grad_gainthree,
        grad_shiftthree,
        grad_feedup,
        grad_feeddown,
    )


def solution(mesh):
    placed = (
        P(("fsdp", "dp"), None, None),
        P(("fsdp", "dp")),
        P(("fsdp", "dp"), None, None),
        P(("fsdp", "dp"), None, None),
        P(("fsdp", "dp")),
        P(("fsdp", "dp")),
        P(("fsdp", "dp")),
        P(("fsdp", "dp"), None),
        P(("fsdp", "dp"), None),
        P(("fsdp", "dp")),
        P(("fsdp", "dp")),
        P(("fsdp", "dp"), None),
        P(("fsdp", "dp"), None),
        P(("fsdp", "dp"), None),
        P(("fsdp", "dp")),
        P(("fsdp", "dp")),
        P(("fsdp", "dp"), None),
        P(("fsdp", "dp"), None),
        P(("fsdp", "dp"), None, None),
    )
    return jax.shard_map(
        local,
        mesh=mesh,
        in_specs=placed,
        out_specs=(
            P(("fsdp", "dp"), None, None),
            P(("fsdp", "dp"), None, None),
            P(("fsdp", "dp"), None, None),
            P(("fsdp", "dp")),
            P(("fsdp", "dp")),
            P(("fsdp", "dp"), None),
            P(("fsdp", "dp"), None),
            P(("fsdp", "dp")),
            P(("fsdp", "dp")),
            P(("fsdp", "dp"), None),
            P(("fsdp", "dp"), None),
            P(("fsdp", "dp"), None),
            P(("fsdp", "dp")),
            P(("fsdp", "dp")),
            P(("fsdp", "dp"), None),
            P(("fsdp", "dp"), None),
        ),
        check_vma=False,
    )
```

profile of v0, /device:TPU:0, one launch (start us, length us, event | category | flops | bytes accessed | tf_op | source)
XLA Modules:
  0.0 1620.7 jit_solution(10160456022927179055)
XLA Ops:
  17.0 42.3 %all-reduce.7 = (bf16[768]{0:T(1024)(128)(2,1)S(1)}, bf16[768]{0:T(1024)(128)(2,1)S(1)}, bf16[768]{0:T(1024)(128)(2,1)S(1)}, bf16[768]{0:T(1024)(128)(2,1)S(1)},...) all-reduce(bf16[768]{0:T(1024)(128)(2,1)S(1)} %dynamic-update-slice, ...), channel_id=1, replica_groups=mesh['fsdp'=4,'dp'=8] {'fsdp','dp'}, use_global_device_ids=true, to_apply=%add.1 | all-reduce | flops 4608 | bytes 18432
  71.1 22.9 %fusion.62 = bf16[16,2,128,1536]{3,0,2,1:T(8,128)(2,1)} fusion(bf16[32,128,768]{2,1,0:T(8,128)(2,1)} %param.25, bf16[768,1536]{1,0:T(8,128)(2,1)} %all-gather.12.cloned.1.call-done, s32[16,2]{0,1:T(2,128)S(1)} %bitcast.338), kind=kOutput, calls=%fused_computation.82 | convolution fusion | flops 10078913536 | bytes 21233792 | tf_op jit(solution)/shard_map/scjp,pne->scjne/dot_general | solution.py:215
  93.9 10.4 fusion.148
  104.3 9.1 copy.137
  113.4 9.3 copy.134
  122.7 10.5 all-gather.8.cloned.1.call-done
  133.2 6.7 fusion.72
  146.8 73.8 %while.28 = (s32[]{:T(128)}, bf16[2,1,512,12,64]{2,4,3,1,0:T(8,128)(2,1)}, f32[2,1,12,512]{3,2,1,0:T(8,128)S(1)}, s32[2]{0:T(128)S(1)}, bf16[1,1024,12,64]{1,3,2...) while((s32[]{:T(128)}, ...), condition=%wide.region_5.6_spmd.clone, body=%wide.region_2.5_spmd.clone.sunk | while | flops 1687154176 | bytes 190281984 | solution.py:77
  149.2 10.6 fusion.210
  159.8 12.3 fusion.211
  175.2 8.5 bitcast_dynamic-update-slice_fusion.6
  186.1 10.6 fusion.210
  196.7 12.3 fusion.211
  212.1 8.5 bitcast_dynamic-update-slice_fusion.6
  231.2 13.7 all-gather.14.cloned.1.call-done
  255.0 6.6 copy.149
  261.6 12.8 fusion.151
  274.5 7.5 convert_bitcast_fusion
  287.7 13.2 all-gather.16.cloned.1.call-done
  305.4 60.7 %all-gather.18.cloned.1.call-done = bf16[768,3072]{1,0:T(8,128)(2,1)} async-done(((bf16[24,3072]{1,0:T(8,128)(2,1)}), bf16[768,3072]{1,0:T(8,128)(2,1)}) %all-gather.18.cloned.1.call-update) | async-done | bytes 4718608 | tf_op jit(solution)/shard_map/all_gather | solution.py:167
  366.2 8.0 fusion.142
  378.7 9.1 fusion.115
  387.8 43.8 %all-gather.20.cloned.1.call-done = bf16[3072,768]{1,0:T(8,128)(2,1)} async-done(((bf16[96,768]{1,0:T(8,128)(2,1)}), bf16[3072,768]{1,0:T(8,128)(2,1)}) %all-gather.20.cloned.1.call-update) | async-done | bytes 4718608 | tf_op jit(solution)/shard_map/all_gather | solution.py:168
  431.6 15.3 fusion.57
  446.9 8.1 fusion.140
  455.0 9.1 fusion.155
  482.3 6.4 copy.150
  490.4 11.5 multiply_reduce_fusion.1
  501.9 9.7 convolution_bitcast_fusion
  511.6 10.3 multiply_convert_fusion.1
  525.4 8.2 multiply_bitcast_fusion
  533.6 8.1 reshape.804
  542.3 8.3 reshape.803
  560.4 16.1 concatenate.30
  576.6 15.5 copy.152
  625.1 170.1 %while.29 = (s32[]{:T(128)}, f32[1,1024,12,64]{1,3,2,0:T(8,128)}, f32[1,1024,12,64]{1,3,2,0:T(8,128)}, bf16[2,1,512,12,64]{2,4,3,1,0:T(8,128)(2,1)}, s32[2]{0:T(...) while((s32[]{:T(128)}, f32[1,1024,12,64]{1,3,2,0:T(8,128)}, ...), condition=%wide.region_20.21_spmd.clone, body=%wide.region_18.20_spmd.clone.sunk | while | flops 4126273024 | bytes 225630512 | solution.py:117
  627.6 11.4 fusion.220
  639.0 12.9 bitcast_add_fusion.7
  651.9 18.1 %multiply_reduce_fusion.5 = (f32[12,512]{1,0:T(8,128)S(1)}, f32[12,512,1024]{2,1,0:T(8,128)}) fusion(f32[12,512,1024]{2,1,0:T(8,128)} %fusion.220, f32[12,512]{1,0:T(8,128)S(1)} %dynamic-slice_bitcast_fusion.8, pred[512,1024]{1,0:T(8,128)(4,1)S(1)} %fusion.221, bf16[1,1024,12,64]{1,3,2,0:T(8,128)(2,1)} %get-tuple-element.549, ...), kind=kOutput, calls=%fused_computation.23.clone.1 | convolution fusion | flops 836757504 | bytes 53264388 | tf_op jit(solution)/shard_map/while/body/eval_jaxpr/sqhe,skhe->shqk/dot_general | solution.py:97
  670.0 21.2 %multiply_convert_fusion.7 = bf16[12,512,1024]{2,1,0:T(8,128)(2,1)} fusion(f32[12,512,1024]{2,1,0:T(8,128)} %get-tuple-element.472, f32[12,512,1024]{2,1,0:T(8,128)} %fusion.220, f32[12,512]{1,0:T(8,128)S(1)} %get-tuple-element.473, f32[12,512]{1,0:T(8,128)S(1)} %dynamic-slice_bitcast_fusion.8, pred[512,1024]{1,0:T(8,128)(4,1)S(1)} %fusion.221), kind=kLoop, calls=%fused_computation.22.clone.1 | loop fusion | flops 37748736 | bytes 63488000 | tf_op jit(solution)/shard_map/while/body/eval_jaxpr/convert_element_type | solution.py:102
  691.2 9.5 bitcast_dynamic-update-slice_fusion.8
  700.7 8.5 bitcast_add_fusion.6
  711.6 11.4 fusion.220
  722.9 13.8 bitcast_add_fusion.7
  736.7 18.1 %multiply_reduce_fusion.5 = (f32[12,512]{1,0:T(8,128)S(1)}, f32[12,512,1024]{2,1,0:T(8,128)}) fusion(f32[12,512,1024]{2,1,0:T(8,128)} %fusion.220, f32[12,512]{1,0:T(8,128)S(1)} %dynamic-slice_bitcast_fusion.8, pred[512,1024]{1,0:T(8,128)(4,1)S(1)} %fusion.221, bf16[1,1024,12,64]{1,3,2,0:T(8,128)(2,1)} %get-tuple-element.549, ...), kind=kOutput, calls=%fused_computation.23.clone.1 | convolution fusion | flops 836757504 | bytes 53264388 | tf_op jit(solution)/shard_map/while/body/eval_jaxpr/sqhe,skhe->shqk/dot_general | solution.py:97
  754.8 21.2 %multiply_convert_fusion.7 = bf16[12,512,1024]{2,1,0:T(8,128)(2,1)} fusion(f32[12,512,1024]{2,1,0:T(8,128)} %get-tuple-element.472, f32[12,512,1024]{2,1,0:T(8,128)} %fusion.220, f32[12,512]{1,0:T(8,128)S(1)} %get-tuple-element.473, f32[12,512]{1,0:T(8,128)S(1)} %dynamic-slice_bitcast_fusion.8, pred[512,1024]{1,0:T(8,128)(4,1)S(1)} %fusion.221), kind=kLoop, calls=%fused_computation.22.clone.1 | loop fusion | flops 37748736 | bytes 63488000 | tf_op jit(solution)/shard_map/while/body/eval_jaxpr/convert_element_type | solution.py:102
  776.0 9.5 bitcast_dynamic-update-slice_fusion.8
  785.5 9.5 bitcast_add_fusion.6
  805.9 7.1 fusion.106
  818.5 6.6 reshape.794
  833.3 15.8 concatenate.29
  849.1 15.5 copy.151
  864.5 19.1 %bitcast_convert_fusion = bf16[32,128,1536]{2,0,1:T(8,128)(2,1)} fusion(f32[1,16,2,128,768]{4,1,2,3,0:T(8,128)} %copy.152, f32[1,16,2,128,768]{4,1,2,3,0:T(8,128)} %copy.151, s32[16,2]{0,1:T(2,128)S(1)} %bitcast.339), kind=kOutput, calls=%fused_computation.61 | convolution fusion | flops 2428503040 | bytes 37748864 | tf_op jit(solution)/shard_map/scjp,scjne->pne/dot_general | solution.py:354
  883.6 18.6 %fusion.77 = f32[768,1536]{0,1:T(8,128)} fusion(bf16[32,128,1536]{2,0,1:T(8,128)(2,1)} %bitcast_convert_fusion, bf16[32,128,768]{2,1,0:T(8,128)(2,1)} %param.25), kind=kOutput, calls=%fused_computation.106 | convolution fusion | flops 9663676416 | bytes 23592960 | tf_op jit(solution)/shard_map/pnd,pne->de/dot_general | solution.py:357
  916.5 20.5 %dynamic-update-slice.8 = f32[32,295056]{1,0:T(8,128)} dynamic-update-slice(f32[32,295056]{1,0:T(8,128)} %dynamic-update-slice.7, f32[32,55296]{1,0:T(8,128)} %reshape.794, s32[]{} %constant.147, s32[]{} %constant.149) | dynamic-update-slice | bytes 14155780
  937.1 9.3 dynamic-update-slice.9
  949.4 9.3 dynamic-update-slice.12
  958.7 14.9 dynamic-update-slice.13
  973.6 9.3 dynamic-update-slice.14
  985.9 28.8 %dynamic-update-slice.17 = f32[32,295056]{1,0:T(8,128)} dynamic-update-slice(f32[32,295056]{1,0:T(8,128)} %dynamic-update-slice.16, f32[32,73728]{1,0:T(8,128)} %reshape.803, s32[]{} %constant.147, s32[]{} %constant.158) | dynamic-update-slice | bytes 18874372
  1014.7 28.3 %dynamic-update-slice.18 = f32[32,295056]{1,0:T(8,128)} dynamic-update-slice(f32[32,295056]{1,0:T(8,128)} %dynamic-update-slice.17, f32[32,73728]{1,0:T(8,128)} %reshape.804, s32[]{} %constant.147, s32[]{} %constant.159) | dynamic-update-slice | bytes 18874372 | tf_op jit(solution)/shard_map/concatenate | solution.py:37
  1043.1 11.2 fusion.96
  1065.3 30.2 %fusion.60 = f32[32,128,768]{2,1,0:T(8,128)} fusion(bf16[32,128,1536]{2,0,1:T(8,128)(2,1)} %bitcast_convert_fusion, bf16[768,1536]{1,0:T(8,128)(2,1)S(1)} %copy-done.62), kind=kOutput, calls=%fused_computation.74 | convolution fusion | flops 9663676416 | bytes 27525120 | tf_op jit(solution)/shard_map/pne,de->pnd/dot_general | solution.py:360
  1095.5 501.5 %all-reduce.10.cloned.1.call-done = f32[32,295056]{1,0:T(8,128)} async-done(((f32[32,295056]{1,0:T(8,128)}), f32[32,295056]{1,0:T(8,128)}) %all-reduce.10.cloned.1.call-update) | async-done | bytes 37767184
  (302 shorter events, 215.0 us)
Async XLA Ops:
  7.2 63.9 %all-gather.12.cloned.1.call-start = ((), (), s32[]{:S(2)}) async-start(), calls=%async_computation.2 | async-start | bytes 2433024 | tf_op jit(solution)/shard_map/all_gather | solution.py:163
  7.9 125.2 %all-gather.8.cloned.1.call-start = ((), (), s32[]{:S(2)}) async-start(), calls=%async_computation | async-start | bytes 3649536 | tf_op jit(solution)/shard_map/all_gather | solution.py:158
  8.7 217.8 %all-gather.10.cloned.1.call-start = ((), (), s32[]{:S(2)}) async-start(), calls=%async_computation.1 | async-start | bytes 1216512 | tf_op jit(solution)/shard_map/all_gather | solution.py:159
  9.4 235.6 %all-gather.14.cloned.1.call-start = ((), (), s32[]{:S(2)}) async-start(), calls=%async_computation.3 | async-start | bytes 1216512 | tf_op jit(solution)/shard_map/all_gather | solution.py:162
  10.0 290.8 %all-gather.16.cloned.1.call-start = ((), (), s32[]{:S(2)}) async-start(), calls=%async_computation.4 | async-start | bytes 1216512 | tf_op jit(solution)/shard_map/all_gather | solution.py:164
  10.6 355.6 %all-gather.18.cloned.1.call-start = ((), (), s32[]{:S(2)}) async-start(), calls=%async_computation.5 | async-start | bytes 4866048 | tf_op jit(solution)/shard_map/all_gather | solution.py:167
  11.1 420.4 %all-gather.20.cloned.1.call-start = ((), (), s32[]{:S(2)}) async-start(), calls=%async_computation.6 | async-start | bytes 4866048 | tf_op jit(solution)/shard_map/all_gather | solution.py:168
  11.9 1585.1 %all-reduce.10.cloned.1.call-start = ((), (), s32[]{:S(2)}) async-start(), calls=%async_computation.7 | async-start | bytes 75563008
  59.4 73.8 %copy-start.56 = (f32[768]{0:T(1024)}, f32[768]{0:T(1024)S(1)}, u32[]{:S(2)}) copy-start(f32[768]{0:T(1024)S(1)} %convert_element_type.159) | copy-start | bytes 9220
  59.4 73.8 %copy-start.40 = (f32[768]{0:T(1024)}, f32[768]{0:T(1024)S(1)}, u32[]{:S(2)}) copy-start(f32[768]{0:T(1024)S(1)} %convert_element_type.158) | copy-start | bytes 9220
  62.7 3.2 copy-start.25
  64.6 68.6 %copy-start.7 = (bf16[1,1024,768]{1,2,0:T(8,128)(2,1)}, bf16[1,1024,768]{1,2,0:T(8,128)(2,1)S(1)}, u32[]{:S(2)}) copy-start(bf16[1,1024,768]{1,2,0:T(8,128)(2,1)S(1)} %copy.128) | copy-start | bytes 4718596
  64.6 6.5 copy-start.54
  64.9 68.3 %copy-start.34 = (f32[1024]{0:T(1024)}, f32[1024]{0:T(1024)S(1)}, u32[]{:S(2)}) copy-start(f32[1024]{0:T(1024)S(1)} %broadcast_multiply_fusion.2) | copy-start | bytes 12292
  65.9 67.2 %copy-start.38 = (f32[1024]{0:T(1024)}, f32[1024]{0:T(1024)S(1)}, u32[]{:S(2)}) copy-start(f32[1024]{0:T(1024)S(1)} %fusion.129) | copy-start | bytes 12292
  149.2 23.0 %copy-start.6 = (bf16[1,1024,12,64]{1,3,2,0:T(8,128)(2,1)S(1)}, bf16[1,1024,12,64]{1,3,2,0:T(8,128)(2,1)}, u32[]{:S(2)}) copy-start(bf16[1,1024,12,64]{1,3,2,0:T(8,128)(2,1)} %get-tuple-element.504) | copy-start | bytes 4718596 | tf_op jit(solution)/shard_map/while
  159.8 15.4 copy-start
  186.1 22.9 %copy-start.6 = (bf16[1,1024,12,64]{1,3,2,0:T(8,128)(2,1)S(1)}, bf16[1,1024,12,64]{1,3,2,0:T(8,128)(2,1)}, u32[]{:S(2)}) copy-start(bf16[1,1024,12,64]{1,3,2,0:T(8,128)(2,1)} %get-tuple-element.504) | copy-start | bytes 4718596 | tf_op jit(solution)/shard_map/while
  196.7 15.4 copy-start
  220.7 5.8 copy-start.1
  220.7 5.8 copy-start.4
  220.7 5.8 copy-start.31
  230.2 18.9 %copy-start.10 = (f32[1,1024,768]{1,2,0:T(8,128)}, f32[1,1024,768]{1,2,0:T(8,128)S(1)}, u32[]{:S(2)}) copy-start(f32[1,1024,768]{1,2,0:T(8,128)S(1)} %get-tuple-element.337) | copy-start | bytes 9437188
  230.2 14.7 copy-start.48
  230.2 14.7 copy-start.58
  230.3 18.9 %copy-start.36 = (f32[1024]{0:T(1024)}, f32[1024]{0:T(1024)S(1)}, u32[]{:S(2)}) copy-start(f32[1024]{0:T(1024)S(1)} %broadcast_multiply_fusion.1) | copy-start | bytes 12292
  231.2 17.9 %copy-start.46 = (f32[1024]{0:T(1024)}, f32[1024]{0:T(1024)S(1)}, u32[]{:S(2)}) copy-start(f32[1024]{0:T(1024)S(1)} %fusion.130) | copy-start | bytes 12292
  255.0 6.6 copy-start.60
  261.6 12.8 copy-start.17
  305.0 165.6 %copy-start.9 = (f32[1,1024,768]{1,2,0:T(8,128)}, f32[1,1024,768]{1,2,0:T(8,128)S(1)}, u32[]{:S(2)}) copy-start(f32[1,1024,768]{1,2,0:T(8,128)S(1)} %get-tuple-element.341) | copy-start | bytes 9437188
  305.0 61.1 %copy-start.30 = (f32[768]{0:T(1024)S(1)}, f32[768]{0:T(1024)}, u32[]{:S(2)}) copy-start(f32[768]{0:T(1024)} %convert_element_type.176) | copy-start | bytes 9220
  305.0 61.1 %copy-start.33 = (f32[768]{0:T(1024)S(1)}, f32[768]{0:T(1024)}, u32[]{:S(2)}) copy-start(f32[768]{0:T(1024)} %convert_element_type.177) | copy-start | bytes 9220
  366.2 12.5 copy-start.26
  374.1 4.6 copy-start.20
  467.7 3.0 copy-start.14
  474.1 2.8 copy-start.65
  490.4 31.5 %slice-start = ((s8[6291456]{0:T(1024)(128)(4,1)}), s8[4194304]{0:T(1024)(128)(4,1)S(1)}, s32[]{:S(2)}) async-start(s8[6291456]{0:T(1024)(128)(4,1)} %bitcast.319), calls=%async_computation.8 | async-start | bytes 8388608
  501.9 20.0 %slice-start.1 = ((s8[6291456]{0:T(1024)(128)(4,1)}), s8[2097152]{0:T(1024)(128)(4,1)S(1)}, s32[]{:S(2)}) async-start(s8[6291456]{0:T(1024)(128)(4,1)} %bitcast.319), calls=%async_computation.9 | async-start | bytes 4194304
  542.3 9.0 copy-start.24
  576.6 15.5 copy-start.11
  576.6 15.5 copy-start.37
  576.6 15.5 copy-start.47
  576.6 15.5 copy-start.49
  576.6 15.5 copy-start.59
  592.1 4.6 copy-start.29
  592.1 4.6 copy-start.64
  606.8 2.8 copy-start.13
  615.8 5.4 copy-start.21
  615.8 5.4 copy-start.63
  621.2 3.9 copy-start.2
  621.2 3.9 copy-start.32
  627.6 11.4 copy-start.22
  691.2 9.5 copy-start.5
  711.6 11.4 copy-start.22
  776.0 9.5 copy-start.5
  799.8 3.0 copy-start.3
  805.9 7.1 copy-start.61
  829.0 2.8 copy-start.12
  849.1 15.5 copy-start.55
  937.1 9.3 copy-start.45
  937.1 10.8 copy-start.44
  973.6 9.3 copy-start.43
  973.6 10.8 copy-start.42
  1061.5 3.7 copy-start.62
  (16 other events, 33.7 us)
Sparse Core Ops, SparseCore 0:
  10.9 60.0 all-gather.11
  74.0 59.1 all-gather.7
  136.1 52.9 all-gather.9
  191.8 53.0 all-gather.13
  247.7 53.0 all-gather.15
  303.6 62.5 all-gather.17
  369.1 62.4 all-gather.19
  1043.2 553.7 all-reduce.9
where the time goes:
time: 1640 us; the launch traced here: 1620 us
  waiting for transfers between devices  650 us (40%)
  matrix products  417 us (25%)
  local copies, waits for them, and re-layouts  382 us (23%)
  other arithmetic  110 us (7%)
  blocking collectives  42.3 us (3%)
    unnamed x9, waiting for transfers between devices  506 us
    unnamed x158, local copies, waits for them, and re-layouts  130 us
    concatenate x4, local copies, waits for them, and re-layouts, local(): jnp.concatenate([key_grad.reshape(seq_count, span_count, NEIGH * neigh_le...  62.8 us
    all_gather x1, waiting for transfers between devices, local(): lax.all_gather(feed_up, ('fsdp', 'dp'), axis=0, tiled=True)  60.7 us
    dot_general x4, matrix products, self_scores(): jnp.einsum('sqhe,skhe->shqk', query_block, key_heads, preferred_element_t...  43.9 us
    all_gather x1, waiting for transfers between devices, local(): lax.all_gather(feed_down, ('fsdp', 'dp'), axis=0, tiled=True)  43.8 us
    unnamed x1, blocking collectives  42.3 us
    convert_element_type x2, other arithmetic, step(): score_grad = (soft * (prob_grad - jnp.sum(soft * prob_grad, axis=-1, keep...  42.3 us
  transfers between devices with their start and end apart: 8, of which 7 were waited for; matrix products, arithmetic and copies ran while one was open for 17% of the time, Pallas kernels for 0%

commit v1 on v0

v1 whole, which is shorter than its diff:
```python
import functools

import jax
import jax.numpy as jnp
from jax import lax
from jax.experimental import pallas as pl
from jax.experimental.pallas import tpu as pltpu
from jax.sharding import PartitionSpec as P

HEADS = 12
SPAN = 64
NEIGH = 2
LANES = 128
WIDE = 256
QBLOCK = 256

EPSILON = 1e-05
SCALE = 0.125
NEGATIVE = -1e30
BF16 = jnp.bfloat16
F32 = jnp.float32
NT = (((1,), (1,)), ((), ()))
NN = (((1,), (0,)), ((), ()))
TN = (((0,), (0,)), ((), ()))


def dot(left, right, dims=NN):
    return lax.dot_general(left, right, dims, preferred_element_type=F32)


def iota(shape, axis):
    return lax.broadcasted_iota(jnp.int32, shape, axis)


def split_three(values):
    high = values.astype(BF16)
    rest = values - high.astype(F32)
    middle = rest.astype(BF16)
    low = (rest - middle.astype(F32)).astype(BF16)
    return (high, middle, low)


def self_forward_kernel(length_ref, query_ref, key_ref, value_ref, mixed_ref, exact_ref, logsum_ref):
    seq_len = query_ref.shape[0]
    length = length_ref[0]
    lane = iota((1, LANES), 1)
    first = lane < 64
    padded = jnp.where(iota((seq_len, 1), 0) < length, 0.0, NEGATIVE).astype(BF16)
    keys = key_ref[...]
    values = value_ref[...]
    one = jnp.ones((), BF16)
    keys_by_head = (
        jnp.where(first, keys, jnp.where(lane == 64, padded, 0)),
        jnp.where(first, jnp.where(lane == 0, padded, 0), keys),
    )
    values_by_head = (jnp.where(first, values, one), jnp.where(first, one, values))
    causal = iota((QBLOCK, QBLOCK), 1) <= iota((QBLOCK, QBLOCK), 0)
    for block in range(seq_len // QBLOCK):
        start = block * QBLOCK
        query = query_ref[start : start + QBLOCK] * jnp.asarray(SCALE, BF16)
        queries = (
            jnp.where(first, query, jnp.where(lane == 64, one, 0)),
            jnp.where(first, jnp.where(lane == 0, one, 0), query),
        )
        outs = []
        tops = []
        for head in range(2):
            diagonal = dot(queries[head], keys_by_head[head][start : start + QBLOCK], NT)
            diagonal = jnp.where(causal, diagonal, NEGATIVE)
            top = jnp.max(diagonal, axis=-1, keepdims=True)
            if block:
                before = dot(queries[head], keys_by_head[head][:start], NT)
                top = jnp.maximum(top, jnp.max(before, axis=-1, keepdims=True))
            out = dot(
                jnp.exp(diagonal - top).astype(BF16),
                values_by_head[head][start : start + QBLOCK],
            )
            if block:
                out = out + dot(jnp.exp(before - top).astype(BF16), values_by_head[head][:start])
            outs.append(out)
            tops.append(top)
        total = pltpu.roll(jnp.where(first, outs[1], outs[0]), 64, 1)
        mixed = jnp.where(first, outs[0], outs[1]) / total
        mixed_ref[start : start + QBLOCK] = mixed.astype(BF16)
        exact_ref[start : start + QBLOCK] = mixed
        logsum = (jnp.where(first, tops[0], tops[1]) + jnp.log(total)).T
        logsum_ref[0, 0:1, start : start + QBLOCK] = logsum[0:1]
        logsum_ref[0, 1:2, start : start + QBLOCK] = logsum[64:65]


def self_forward(projected, lengths):
    seq_len = projected.shape[0]
    width = projected.shape[1] // 3
    pairs = width // LANES
    column = lambda offset: pl.BlockSpec((seq_len, LANES), lambda p: (0, p + offset))
    return pl.pallas_call(
        self_forward_kernel,
        grid=(pairs,),
        in_specs=[
            pl.BlockSpec(memory_space=pltpu.SMEM),
            column(0),
            column(pairs),
            column(2 * pairs),
        ],
        out_specs=[
            column(0),
            column(0),
            pl.BlockSpec((1, 8, seq_len), lambda p: (p, 0, 0)),
        ],
        out_shape=[
            jax.ShapeDtypeStruct((seq_len, width), BF16),
            jax.ShapeDtypeStruct((seq_len, width), F32),
            jax.ShapeDtypeStruct((pairs, 8, seq_len), F32),
        ],
        compiler_params=pltpu.CompilerParams(vmem_limit_bytes=48 * 2**20),
        name="self_forward",
    )(lengths, projected, projected, projected)


def self_backward_kernel(
    length_ref,
    query_ref,
    key_ref,
    value_ref,
    grad_ref,
    exact_ref,
    logsum_ref,
    out_ref,
    key_grad_ref,
    value_grad_ref,
):
    seq_len = query_ref.shape[0]
    length = length_ref[0]
    lane = iota((1, LANES), 1)
    first = lane < 64
    row = iota((LANES, 1), 0)
    top_rows = row < 64
    padded = jnp.where(iota((seq_len, 1), 0) < length, 0.0, NEGATIVE).astype(BF16)
    keys = key_ref[...]
    values = value_ref[...]
    zero = jnp.zeros((), BF16)
    minus = -jnp.ones((), BF16)

    def beside(offset, head_lane):
        kept = (lane > head_lane) & (lane < head_lane + 4)
        return jnp.where(lane == head_lane, offset, jnp.where(kept, minus, zero))

    keys_by_head = (
        jnp.where(first, keys, beside(padded, 64)),
        jnp.where(first, beside(padded, 0), keys),
    )
    values_by_head = (
        jnp.where(first, values, beside(zero, 64)),
        jnp.where(first, beside(zero, 0), values),
    )
    keys_turned = keys.T
    turned_by_head = (
        jnp.where(top_rows, keys_turned, zero),
        jnp.where(top_rows, zero, keys_turned),
    )
    causal = iota((QBLOCK, QBLOCK), 0) <= iota((QBLOCK, QBLOCK), 1)

    def fill(turned, head, lead, parts):
        base = 64 if head == 0 else 0
        other = jnp.where(row == base, lead, zero)
        for place, part in enumerate(parts):
            other = jnp.where(row == base + 1 + place, part, other)
        own = top_rows if head == 0 else ~top_rows
        return jnp.where(own, turned, other)

    count = seq_len // QBLOCK
    for block in reversed(range(count)):
        start = block * QBLOCK
        stop = start + QBLOCK
        query = query_ref[start:stop] * jnp.asarray(SCALE, BF16)
        grad = grad_ref[start:stop]
        query_turned = query.T
        grad_turned = grad.T
        weighted = (grad.astype(F32) * exact_ref[start:stop]).T
        probs_all = []
        scores_all = []
        query_grad = None
        for head in range(2):
            delta = jnp.sum(weighted[head * 64 : head * 64 + 64], axis=0, keepdims=True)
            logsum = logsum_ref[0, head : head + 1, start:stop]
            score = dot(
                keys_by_head[head][:stop],
                fill(query_turned, head, jnp.ones((), BF16), split_three(logsum)),
            )
            prob = jnp.exp(score)
            last = jnp.where(causal, prob[start:], 0.0)
            prob = jnp.concatenate([prob[:start], last], axis=0) if block else last
            centred = dot(
                values_by_head[head][:stop], fill(grad_turned, head, zero, split_three(delta))
            )
            score_grad = (prob * centred).astype(BF16)
            scores_all.append(score_grad)
            probs_all.append(prob.astype(BF16))
            part = dot(turned_by_head[head][:, :stop], score_grad)
            query_grad = part if query_grad is None else query_grad + part
        out_ref[0, start:stop] = (query_grad.T * SCALE).astype(BF16)
        own_query = jnp.concatenate(
            [jnp.where(first, query, zero), jnp.where(first, zero, query)], axis=0
        )
        own_grad = jnp.concatenate(
            [jnp.where(first, grad, zero), jnp.where(first, zero, grad)], axis=0
        )
        key_part = dot(jnp.concatenate(scores_all, axis=1), own_query)
        value_part = dot(jnp.concatenate(probs_all, axis=1), own_grad)
        if block == count - 1:
            key_grad_ref[...] = key_part
            value_grad_ref[...] = value_part
        else:
            key_grad_ref[:stop] += key_part
            value_grad_ref[:stop] += value_part
    out_ref[1] = key_grad_ref[...].astype(BF16)
    out_ref[2] = value_grad_ref[...].astype(BF16)


def self_backward(projected, lengths, grad, exact, logsum):
    seq_len = projected.shape[0]
    width = projected.shape[1] // 3
    pairs = width // LANES
    column = lambda offset: pl.BlockSpec((seq_len, LANES), lambda p: (0, p + offset))
    return pl.pallas_call(
        self_backward_kernel,
        grid=(pairs,),
        in_specs=[
            pl.BlockSpec(memory_space=pltpu.SMEM),
            column(0),
            column(pairs),
            column(2 * pairs),
            column(0),
            column(0),
            pl.BlockSpec((1, 8, seq_len), lambda p: (p, 0, 0)),
        ],
        out_specs=pl.BlockSpec((3, seq_len, LANES), lambda p: (0, 0, p)),
        out_shape=jax.ShapeDtypeStruct((3, seq_len, width), BF16),
        scratch_shapes=[pltpu.VMEM((seq_len, LANES), F32), pltpu.VMEM((seq_len, LANES), F32)],
        compiler_params=pltpu.CompilerParams(vmem_limit_bytes=48 * 2**20),
        name="self_backward",
    )(lengths, projected, projected, projected, grad, exact, logsum)


def block_diagonal(rows):
    lane = iota((1, WIDE), 1)
    return jnp.concatenate(
        [jnp.where((lane >= h * 64) & (lane < h * 64 + 64), rows, 0) for h in range(4)], axis=0
    )


def take_diagonal(stacked):
    lane = iota((1, WIDE), 1)
    result = stacked[:SPAN]
    for h in range(1, 4):
        result = jnp.where(lane >= h * 64, stacked[h * SPAN : (h + 1) * SPAN], result)
    return result


def slot_bias(ids_ref, neighbour_lengths_ref, span, neigh_len, axis):
    shape = (1, NEIGH * neigh_len) if axis else (NEIGH * neigh_len, 1)
    place = iota(shape, axis)
    first = neighbour_lengths_ref[ids_ref[span * NEIGH]]
    second = neighbour_lengths_ref[ids_ref[span * NEIGH + 1]]
    limit = jnp.where(place < neigh_len, first, neigh_len + second)
    return jnp.where(place < limit, 0.0, NEGATIVE)


def cross_forward_kernel(
    ids_ref, neighbour_lengths_ref, query_ref, first_ref, second_ref, mixed_ref
):
    span = pl.program_id(0)
    neigh_len = first_ref.shape[1]
    width = query_ref.shape[1]
    bias = slot_bias(ids_ref, neighbour_lengths_ref, span, neigh_len, 1)
    for group in range(width // WIDE):
        place = slice(group * WIDE, (group + 1) * WIDE)
        value_place = slice(width + group * WIDE, width + (group + 1) * WIDE)
        queries = block_diagonal(query_ref[:, place] * jnp.asarray(SCALE, BF16))
        keys = jnp.concatenate([first_ref[0, :, place], second_ref[0, :, place]], axis=0)
        values = jnp.concatenate(
            [first_ref[0, :, value_place], second_ref[0, :, value_place]], axis=0
        )
        score = dot(queries, keys, NT) + bias
        expo = jnp.exp(score - jnp.max(score, axis=-1, keepdims=True))
        total = jnp.sum(expo, axis=-1, keepdims=True)
        out = dot(expo.astype(BF16), values) / total
        mixed_ref[:, place] = take_diagonal(out).astype(BF16)


def cross_forward(queries, pool_keyval, ids, neighbour_lengths):
    seq_len, width = queries.shape
    neigh_len, both = pool_keyval.shape[1:]
    spans = seq_len // SPAN
    rows = pl.BlockSpec((SPAN, width), lambda c, ids, lens: (c, 0))
    slot = lambda j: pl.BlockSpec(
        (1, neigh_len, both), lambda c, ids, lens: (ids[c * NEIGH + j], 0, 0)
    )
    return pl.pallas_call(
        cross_forward_kernel,
        grid_spec=pltpu.PrefetchScalarGridSpec(
            num_scalar_prefetch=2,
            grid=(spans,),
            in_specs=[rows, slot(0), slot(1)],
            out_specs=rows,
        ),
        out_shape=jax.ShapeDtypeStruct((seq_len, width), BF16),
        compiler_params=pltpu.CompilerParams(vmem_limit_bytes=48 * 2**20),
        name="cross_forward",
    )(ids, neighbour_lengths, queries, pool_keyval, pool_keyval)


def cross_backward_kernel(
    ids_ref,
    neighbour_lengths_ref,
    query_ref,
    grad_ref,
    first_key_ref,
    second_key_ref,
    first_value_ref,
    second_value_ref,
    query_grad_ref,
    key_out_ref,
    value_out_ref,
    key_total,
    value_total,
):
    span = pl.program_id(1)
    spans = pl.num_programs(1)
    neigh_len = first_key_ref.shape[1]

    @pl.when(span == 0)
    def _():
        key_total[...] = jnp.zeros_like(key_total)
        value_total[...] = jnp.zeros_like(value_total)

    bias = slot_bias(ids_ref, neighbour_lengths_ref, span, neigh_len, 0)
    queries = block_diagonal(query_ref[...] * jnp.asarray(SCALE, BF16))
    grads = block_diagonal(grad_ref[...])
    keys = jnp.concatenate([first_key_ref[0], second_key_ref[0]], axis=0)
    values = jnp.concatenate([first_value_ref[0], second_value_ref[0]], axis=0)
    score = dot(keys, queries, NT) + bias
    expo = jnp.exp(score - jnp.max(score, axis=0, keepdims=True))
    prob = expo * (1.0 / jnp.sum(expo, axis=0, keepdims=True))
    prob_grad = dot(values, grads, NT)
    centred = prob_grad - jnp.sum(prob * prob_grad, axis=0, keepdims=True)
    score_grad = (prob * centred).astype(BF16)
    value_part = dot(prob.astype(BF16), grads)
    key_part = dot(score_grad, queries)
    query_part = dot(score_grad, keys, TN)
    query_grad_ref[...] = (take_diagonal(query_part) * SCALE).astype(BF16)
    for slot in range(NEIGH):
        ident = ids_ref[span * NEIGH + slot]
        rows = slice(slot * neigh_len, (slot + 1) * neigh_len)
        key_total[ident] += key_part[rows]
        value_total[ident] += value_part[rows]

    @pl.when(span == spans - 1)
    def _():
        key_out_ref[...] = key_total[...].astype(BF16)
        value_out_ref[...] = value_total[...].astype(BF16)


def cross_backward(queries, grads, pool_keyval, ids, neighbour_lengths):
    seq_len, width = queries.shape
    pool_count, neigh_len, _ = pool_keyval.shape
    spans = seq_len // SPAN
    groups = width // WIDE
    rows = pl.BlockSpec((SPAN, WIDE), lambda g, c, ids, lens: (c, g))
    slot = lambda j, offset: pl.BlockSpec(
        (1, neigh_len, WIDE), lambda g, c, ids, lens: (ids[c * NEIGH + j], 0, g + offset)
    )
    pool = pl.BlockSpec((pool_count, neigh_len, WIDE), lambda g, c, ids, lens: (0, 0, g))
    pool_shape = jax.ShapeDtypeStruct((pool_count, neigh_len, width), BF16)
    return pl.pallas_call(
        cross_backward_kernel,
        grid_spec=pltpu.PrefetchScalarGridSpec(
            num_scalar_prefetch=2,
            grid=(groups, spans),
            in_specs=[rows, rows, slot(0, 0), slot(1, 0), slot(0, groups), slot(1, groups)],
            out_specs=[rows, pool, pool],
            scratch_shapes=[
                pltpu.VMEM((pool_count, neigh_len, WIDE), F32),
                pltpu.VMEM((pool_count, neigh_len, WIDE), F32),
            ],
        ),
        out_shape=[jax.ShapeDtypeStruct((seq_len, width), BF16), pool_shape, pool_shape],
        compiler_params=pltpu.CompilerParams(vmem_limit_bytes=56 * 2**20),
        name="cross_backward",
    )(ids, neighbour_lengths, queries, grads, pool_keyval, pool_keyval, pool_keyval, pool_keyval)


def norm_parts(values):
    centre = jnp.mean(values, axis=-1, keepdims=True)
    centred = values - centre
    spread = jnp.mean(centred * centred, axis=-1, keepdims=True)
    inverse = lax.rsqrt(spread + EPSILON)
    return (centred * inverse, inverse)


def norm_apply(values, gain, shift):
    return norm_parts(values)[0] * gain + shift


def norm_back(values, gain, upstream):
    unit, inverse = norm_parts(values)
    gain_term = jnp.sum(upstream * unit, axis=0)
    shift_term = jnp.sum(upstream, axis=0)
    inner = upstream * gain
    mean_inner = jnp.mean(inner, axis=-1, keepdims=True)
    mean_both = jnp.mean(inner * unit, axis=-1, keepdims=True)
    return (inverse * (inner - mean_inner - unit * mean_both), gain_term, shift_term)


def gelu_tanh(values):
    return jax.nn.gelu(values, approximate=True)


AXES = ("fsdp", "dp")


def local(
    tokens,
    lengths,
    neighbours,
    neighbour_ids,
    neighbour_lengths,
    first_gain,
    first_shift,
    self_input,
    self_output,
    second_gain,
    second_shift,
    cross_query,
    cross_keyval,
    cross_output,
    third_gain,
    third_shift,
    feed_up,
    feed_down,
    cotangent,
):
    _, seq_len, width = tokens.shape
    pool_count, neigh_len = neighbours.shape[:2]
    rows = self_input.shape[0]
    vectors = (first_gain, first_shift, second_gain, second_shift, third_gain, third_shift)
    vector_pack = jnp.pad(jnp.stack(vectors, axis=1), ((0, 0), (0, LANES - len(vectors))))
    packed = jnp.concatenate(
        [cross_keyval, self_input, self_output, cross_query, cross_output, vector_pack], axis=1
    )
    gathered = lax.all_gather(packed, AXES, axis=0, tiled=True)
    sizes = (2 * width, 3 * width, width, width, width)
    weights = []
    offset = 0
    for size in sizes:
        weights.append(gathered[:, offset : offset + size])
        offset = offset + size
    w_keyval, w_self_in, w_self_out, w_query, w_cross_out = weights
    gains = gathered[:, offset : offset + len(vectors)].astype(F32).T
    w_up = lax.all_gather(feed_up, AXES, axis=0, tiled=True)
    w_down = lax.all_gather(feed_down, AXES, axis=0, tiled=True)

    stream = tokens[0].astype(F32)
    encoded = neighbours.reshape(pool_count * neigh_len, width)
    ids = neighbour_ids.reshape(-1)
    pool_keyval = dot(encoded, w_keyval).astype(BF16).reshape(pool_count, neigh_len, 2 * width)
    first_in = norm_apply(stream, gains[0], gains[1]).astype(BF16)
    projected = dot(first_in, w_self_in).astype(BF16)
    self_mixed, self_exact, logsum = self_forward(projected, lengths)
    after_self = stream + dot(self_mixed, w_self_out)
    second_in = norm_apply(after_self, gains[2], gains[3]).astype(BF16)
    cross_queries = dot(second_in, w_query).astype(BF16)
    cross_mixed = cross_forward(cross_queries, pool_keyval, ids, neighbour_lengths)
    after_cross = after_self + dot(cross_mixed, w_cross_out)
    third_in = norm_apply(after_cross, gains[4], gains[5]).astype(BF16)
    hidden_pre = dot(third_in, w_up)
    hidden, gelu_back = jax.vjp(gelu_tanh, hidden_pre)
    hidden = hidden.astype(BF16)
    block_out = (after_cross + dot(hidden, w_down)).astype(BF16)

    down_in = cotangent[0]
    feeddown_term = dot(hidden, down_in, TN).astype(BF16)
    hidden_grad = gelu_back(dot(down_in, w_down, NT))[0].astype(BF16)
    feedup_term = dot(third_in, hidden_grad, TN).astype(BF16)
    third_back = dot(hidden_grad, w_up, NT)
    back, gain_three, shift_three = norm_back(after_cross, gains[4], third_back)
    after_cross_grad = down_in.astype(F32) + back
    cross_out_in = after_cross_grad.astype(BF16)
    crossout_term = dot(cross_mixed, cross_out_in, TN)
    mixed_grad = dot(cross_out_in, w_cross_out, NT).astype(BF16)
    query_grad, pool_key_grad, pool_value_grad = cross_backward(
        cross_queries, mixed_grad, pool_keyval, ids, neighbour_lengths
    )
    query_term = dot(second_in, query_grad, TN)
    second_back = dot(query_grad, w_query, NT)
    back, gain_two, shift_two = norm_back(after_self, gains[2], second_back)
    after_self_grad = after_cross_grad + back
    self_out_in = after_self_grad.astype(BF16)
    selfout_term = dot(self_mixed, self_out_in, TN)
    attend_grad = dot(self_out_in, w_self_out, NT).astype(BF16)
    projected_grad = self_backward(projected, lengths, attend_grad, self_exact, logsum)
    projected_grad = jnp.concatenate([projected_grad[i] for i in range(3)], axis=1)
    selfin_term = dot(first_in, projected_grad, TN)
    first_back = dot(projected_grad, w_self_in, NT)
    back, gain_one, shift_one = norm_back(stream, gains[0], first_back)
    tokens_grad = after_self_grad + back

    pool_grad = jnp.concatenate([pool_key_grad, pool_value_grad], axis=-1)
    pool_grad = pool_grad.reshape(pool_count * neigh_len, 2 * width)
    keyval_term = dot(encoded, pool_grad, TN)
    neighbours_grad = dot(pool_grad, w_keyval, NT).reshape(neighbours.shape)

    vector_terms = jnp.stack([gain_one, shift_one, gain_two, shift_two, gain_three, shift_three], axis=1)
    vector_terms = jnp.pad(vector_terms, ((0, 0), (0, LANES - len(vectors))))
    packed_terms = jnp.concatenate(
        [
            term.astype(BF16)
            for term in (keyval_term, selfin_term, selfout_term, query_term, crossout_term, vector_terms)
        ],
        axis=1,
    )

    def scatter(term):
        return lax.psum_scatter(term, AXES, scatter_dimension=0, tiled=True).astype(F32)

    feeddown_grad = scatter(feeddown_term)
    feedup_grad = scatter(feedup_term)
    summed = scatter(packed_terms)
    pieces = []
    offset = 0
    for size in sizes:
        pieces.append(summed[:, offset : offset + size])
        offset = offset + size
    vector_grads = [summed[:, offset + i] for i in range(len(vectors))]
    return (
        block_out[None],
        tokens_grad[None],
        neighbours_grad,
        vector_grads[0],
        vector_grads[1],
        pieces[1],
        pieces[2],
        vector_grads[2],
        vector_grads[3],
        pieces[3],
        pieces[0],
        pieces[4],
        vector_grads[4],
        vector_grads[5],
        feedup_grad,
        feeddown_grad,
    )


def solution(mesh):
    placed = (
        P(("fsdp", "dp"), None, None),
        P(("fsdp", "dp")),
        P(("fsdp", "dp"), None, None),
        P(("fsdp", "dp"), None, None),
        P(("fsdp", "dp")),
        P(("fsdp", "dp")),
        P(("fsdp", "dp")),
        P(("fsdp", "dp"), None),
        P(("fsdp", "dp"), None),
        P(("fsdp", "dp")),
        P(("fsdp", "dp")),
        P(("fsdp", "dp"), None),
        P(("fsdp", "dp"), None),
        P(("fsdp", "dp"), None),
        P(("fsdp", "dp")),
        P(("fsdp", "dp")),
        P(("fsdp", "dp"), None),
        P(("fsdp", "dp"), None),
        P(("fsdp", "dp"), None, None),
    )
    return jax.shard_map(
        local,
        mesh=mesh,
        in_specs=placed,
        out_specs=(
            P(("fsdp", "dp"), None, None),
            P(("fsdp", "dp"), None, None),
            P(("fsdp", "dp"), None, None),
            P(("fsdp", "dp")),
            P(("fsdp", "dp")),
            P(("fsdp", "dp"), None),
            P(("fsdp", "dp"), None),
            P(("fsdp", "dp")),
            P(("fsdp", "dp")),
            P(("fsdp", "dp"), None),
            P(("fsdp", "dp"), None),
            P(("fsdp", "dp"), None),
            P(("fsdp", "dp")),
            P(("fsdp", "dp")),
            P(("fsdp", "dp"), None),
            P(("fsdp", "dp"), None),
        ),
        check_vma=False,
    )
```

time: 1640 us -> 648 us (0.40)
  waiting for transfers between devices: 650 us -> 232 us
  local copies, waits for them, and re-layouts: 382 us -> 84.8 us
  matrix products: 417 us -> 163 us
  Pallas kernels: 0 us -> 114 us
  other arithmetic: 110 us -> 26.8 us
  blocking collectives: 42.3 us -> 0 us
    unnamed x9 -> x7, waiting for transfers between devices: 506 us -> 138 us
    dot_general x41 -> x21, matrix products: 404 us -> 163 us  [dot(): return lax.dot_general(left, right, dims, preferred_element_type=F32)]
    pallas_call x0 -> x4, Pallas kernels: none -> 114 us  [the longest x1 48.8 us: cross_backward(): pl.pallas_call(cross_backward_kernel, grid_spec=pltpu.PrefetchScalarGridS...]
    unnamed x158 -> x88, local copies, waits for them, and re-layouts: 130 us -> 35.4 us
    concatenate x5 -> x3, local copies, waits for them, and re-layouts: 91.1 us -> 4.85 us  [the longest x1 4.09 us: local(): pool_grad = jnp.concatenate([pool_key_grad, pool_value_grad], axis=-1)]
    all_gather x7 -> x3, waiting for transfers between devices: 145 us -> 93.6 us  [the longest x1 78.3 us: local(): gathered = lax.all_gather(packed, AXES, axis=0, tiled=True)]
    convert_element_type x9 -> x3, other arithmetic: 55 us -> 4.29 us  [scatter(): lax.psum_scatter(term, AXES, scatter_dimension=0, tiled=True).astype(F32)]
    unnamed x1 -> x0, blocking collectives: 42.3 us -> none
  transfers between devices with their start and end apart: 8 -> 6, of which waited for: 7 -> 3; matrix products, arithmetic and copies ran while one was open for 17% -> 39% of each run, Pallas kernels for 0% -> 18%
where the time goes in v1:
time: 648 us; the launch traced here: 636 us
  waiting for transfers between devices  232 us (36%)
  matrix products  163 us (25%)
  Pallas kernels  114 us (18%)
  local copies, waits for them, and re-layouts  84.8 us (13%)
  other arithmetic  26.8 us (4%)
  between operations  15.6 us (2%)
    dot_general x21, matrix products, dot(): return lax.dot_general(left, right, dims, preferred_element_type=F32)  163 us
    unnamed x7, waiting for transfers between devices  138 us
    all_gather x1, waiting for transfers between devices, local(): gathered = lax.all_gather(packed, AXES, axis=0, tiled=True)  78.3 us
    pallas_call x1, Pallas kernels, cross_backward(): pl.pallas_call(cross_backward_kernel, grid_spec=pltpu.PrefetchScalarGridS...  48.8 us
    unnamed x88, local copies, waits for them, and re-layouts  35.4 us
    pallas_call x1, Pallas kernels, self_backward(): pl.pallas_call(self_backward_kernel, grid=(pairs,), in_specs=[pl.BlockSpe...  26.1 us
    pallas_call x1, Pallas kernels, self_forward(): pl.pallas_call(self_forward_kernel, grid=(pairs,), in_specs=[pl.BlockSpec...  22.2 us
    pallas_call x1, Pallas kernels, cross_forward(): pl.pallas_call(cross_forward_kernel, grid_spec=pltpu.PrefetchScalarGridSp...  17.2 us
  transfers between devices with their start and end apart: 6, of which 3 were waited for; matrix products, arithmetic and copies ran while one was open for 39% of the time, Pallas kernels for 18%

profile of v1, /device:TPU:0, one launch (start us, length us, event | category | flops | bytes accessed | tf_op | source)
XLA Modules:
  0.0 636.1 jit_solution(1403523342789492421)
XLA Ops:
  8.1 0.9 constant_dynamic-update-slice_fusion.5
  9.0 0.9 constant_dynamic-update-slice_fusion.4
  9.9 0.8 constant_dynamic-update-slice_fusion.3
  10.7 0.8 constant_dynamic-update-slice_fusion.2
  16.0 1.8 copy.89
  18.6 1.6 copy.94
  20.2 78.3 %all-gather.4.cloned.1.call-done = bf16[768,6272]{1,0:T(8,128)(2,1)} async-done(((bf16[24,6272]{1,0:T(8,128)(2,1)}), bf16[768,6272]{1,0:T(8,128)(2,1)}) %all-gather.4.cloned.1.call-update) | async-done | bytes 9633808 | tf_op jit(solution)/shard_map/all_gather | solution.py:451
  98.5 15.6 %fusion = bf16[4096,1536]{0,1:T(8,128)(2,1)} fusion(bf16[4096,768]{1,0:T(8,128)(2,1)} %bitcast.105, bf16[768,6272]{1,0:T(8,128)(2,1)} %all-gather.4.cloned.1.call-done), kind=kOutput, calls=%fused_computation.3 | convolution fusion | flops 9669967872 | bytes 21233664 | tf_op jit(solution)/shard_map/dot_general | solution.py:28
  114.1 16.7 %copy.92 = bf16[4096,1536]{1,0:T(8,128)(2,1)} copy(bf16[4096,1536]{0,1:T(8,128)(2,1)} %fusion) | data formatting | bytes 25165824 | tf_op jit(solution)/shard_map/convert_element_type | solution.py:466
  130.8 1.0 convert_bitcast_fusion.1
  131.8 1.2 slice_reduce_fusion.1
  133.0 7.8 %convolution_convert_fusion.1.query_ref.key_ref.value_ref = bf16[1024,2304]{1,0:T(8,128)(2,1)} fusion(bf16[768,6272]{1,0:T(8,128)(2,1)} %all-gather.4.cloned.1.call-done, bf16[1,1024,768]{1,2,0:T(8,128)(2,1)S(1)} %copy.89, f32[768]{0:T(1024)S(1)} %get-tuple-element.95, f32[768]{0:T(1024)S(1)} %get-tuple-element.96, f32[1024]{0:T(1024)S(1)} %add_rsqrt_fusion.2, ...), kind=kOutput, calls=%fused_computation.12 | convolution fusion | flops 3630956544 | bytes 9844736 | tf_op jit(solution)/shard_map/dot_general | solution.py:28
  140.8 22.2 %self_forward.1 = (bf16[1024,768]{1,0:T(8,128)(2,1)S(1)}, f32[1024,768]{1,0:T(8,128)S(1)}, f32[6,8,1024]{2,1,0:T(8,128)S(1)}) custom-call(s32[1]{0:T(128)S(6)} %copy.125.length_ref, bf16[1024,2304]{1,0:T(8,128)(2,1)} %convolution_convert_fusion.1.query_ref.key_ref.value_ref, bf16[1024,2304]{1,0:T(8,128)(2,1)} %convolution_convert_fusion.1.query_ref.key_ref.value_ref, ...), custom_call_target="tpu_custom_call" | custom-call | tf_op jit(solution)/shard_map/self_forward/pallas_call | solution.py:96
  163.1 3.7 fusion.57
  167.3 3.7 convolution_convert_fusion.7.query_ref
  171.0 17.2 %cross_forward.1 = bf16[1024,768]{1,0:T(8,128)(2,1)S(1)} custom-call(s32[32]{0:T(128)S(1)} %reshape.106.ids_ref, s32[32]{0:T(128)S(1)} %copy-done.6, bf16[1024,768]{1,0:T(8,128)(2,1)S(1)} %convolution_convert_fusion.7.query_ref, bf16[32,128,1536]{2,1,0:T(8,128)(2,1)} %bitcast.93, bf16[32,128,1536]{2,1,0:T(8,128)(2,1)} %bitcast.94), custom_call_target="tpu_custom_call" | custom-call | tf_op jit(solution)/shard_map/cross_forward/pallas_call | solution.py:299
  188.2 3.3 fusion.58
  191.9 7.8 %fusion.55 = f32[1024,3072]{1,0:T(8,128)S(1)} fusion(bf16[768,3072]{1,0:T(8,128)(2,1)} %all-gather.6.cloned.1.call-done, f32[1024,768]{0,1:T(8,128)S(1)} %get-tuple-element.106, f32[768]{0:T(1024)S(1)} %get-tuple-element.92, f32[768]{0:T(1024)S(1)} %get-tuple-element.91, f32[1024]{0:T(1024)S(1)} %add_rsqrt_fusion, f32[1024]{0:T(1024)S(1)} %broadcast_multiply_fusion.6), kind=kOutput, calls=%fused_computation.126 | convolution fusion | flops 4835770368 | bytes 20461568 | tf_op jit(solution)/shard_map/dot_general | solution.py:28
  199.7 4.8 copy-done.18
  204.5 9.4 %convolution_convert_fusion.2 = bf16[3072,768]{1,0:T(8,128)(2,1)} fusion(bf16[1,1024,768]{2,1,0:T(8,128)(2,1)S(1)} %copy-done.28, f32[1024,3072]{1,0:T(8,128)S(1)} %fusion.55), kind=kOutput, calls=%fused_computation.13 | convolution fusion | flops 4862509056 | bytes 18874368 | tf_op jit(solution)/shard_map/dot_general | solution.py:28
  213.9 15.3 %all-gather.8.cloned.1.call-done = bf16[3072,768]{1,0:T(8,128)(2,1)} async-done(((bf16[96,768]{1,0:T(8,128)(2,1)}), bf16[3072,768]{1,0:T(8,128)(2,1)}) %all-gather.8.cloned.1.call-update) | async-done | bytes 4718608 | tf_op jit(solution)/shard_map/all_gather | solution.py:461
  229.2 15.3 %fusion.7 = bf16[1024,3072]{1,0:T(8,128)(2,1)S(1)} fusion(f32[1024,3072]{1,0:T(8,128)} %copy-done.18, bf16[3072,768]{1,0:T(8,128)(2,1)} %all-gather.8.cloned.1.call-done, bf16[1,1024,768]{2,1,0:T(8,128)(2,1)} %param.37), kind=kOutput, calls=%fused_computation.10 | convolution fusion | flops 4894752768 | bytes 25165824 | tf_op jit(solution)/shard_map/dot_general | solution.py:28
  244.5 11.5 %fusion.61 = (bf16[768]{0:T(1024)(128)(2,1)S(1)}, f32[1024,768]{1,0:T(8,128)}) fusion(bf16[1024,3072]{1,0:T(8,128)(2,1)S(1)} %fusion.7, bf16[768,3072]{1,0:T(8,128)(2,1)} %all-gather.6.cloned.1.call-done), kind=kOutput, calls=%fused_computation.132 | convolution fusion | flops 4832623616 | bytes 14157312 | tf_op jit(solution)/shard_map/dot_general | solution.py:28
  256.1 3.8 copy.95
  259.9 3.1 multiply_reduce_fusion
  263.4 1.0 multiply_add_fusion.1
  264.4 1.7 copy-done.19
  266.1 3.9 convolution_convert_fusion.6.grad_ref
  270.0 48.8 %cross_backward.1 = (bf16[1024,768]{1,0:T(8,128)(2,1)}, bf16[32,128,768]{2,1,0:T(8,128)(2,1)}, bf16[32,128,768]{2,1,0:T(8,128)(2,1)}) custom-call(s32[32]{0:T(128)} %copy-done.5, s32[32]{0:T(128)} %neighbour_lengths_ref.3, bf16[1024,768]{1,0:T(8,128)(2,1)} %copy-done, bf16[1024,768]{1,0:T(8,128)(2,1)} %convolution_convert_fusion.6.grad_ref, ...), custom_call_target="tpu_custom_call" | custom-call | tf_op jit(solution)/shard_map/cross_backward/pallas_call | solution.py:375
  318.7 4.9 fusion.60
  323.7 3.5 copy.96
  327.2 4.0 multiply_reduce_fusion.1
  331.9 2.8 multiply_add_fusion
  334.8 3.8 convolution_convert_fusion.5.grad_ref
  338.6 26.1 %self_backward.1 = bf16[3,1024,768]{2,1,0:T(8,128)(2,1)} custom-call(s32[1]{0:T(128)S(6)} %copy.125.length_ref, bf16[1024,2304]{1,0:T(8,128)(2,1)} %convolution_convert_fusion.1.query_ref.key_ref.value_ref, bf16[1024,2304]{1,0:T(8,128)(2,1)} %convolution_convert_fusion.1.query_ref.key_ref.value_ref, ...), custom_call_target="tpu_custom_call" | custom-call | tf_op jit(solution)/shard_map/self_backward/pallas_call | solution.py:225
  364.7 4.6 slice_bitcast_fusion.2
  369.4 6.9 %convolution_convert_fusion.3 = bf16[768,3072]{1,0:T(8,128)(2,1)} fusion(bf16[1024,3072]{1,0:T(8,128)(2,1)S(1)} %bitcast.107, f32[1024,768]{0,1:T(8,128)S(1)} %get-tuple-element.106, f32[768]{0:T(1024)S(1)} %get-tuple-element.92, f32[768]{0:T(1024)S(1)} %get-tuple-element.91, f32[1024]{0:T(1024)S(1)} %add_rsqrt_fusion, f32[1024]{0:T(1024)S(1)} %broadcast_multiply_fusion.6), kind=kOutput, calls=%fused_computation.14 | convolution fusion | flops 4838129664 | bytes 14170112 | tf_op jit(solution)/shard_map/dot_general | solution.py:28
  376.4 9.0 %fusion.59 = (bf16[768]{0:T(1024)(128)(2,1)S(1)}, f32[1024,768]{1,0:T(8,128)}) fusion(bf16[768,6272]{1,0:T(8,128)(2,1)} %all-gather.4.cloned.1.call-done, bf16[1024,768]{1,0:T(8,128)(2,1)} %get-tuple-element.98, bf16[1024,768]{1,0:T(8,128)(2,1)} %get-tuple-element.99, bf16[1024,768]{1,0:T(8,128)(2,1)} %get-tuple-element.97), kind=kOutput, calls=%fused_computation.130 | convolution fusion | flops 3638820096 | bytes 11404800 | tf_op jit(solution)/shard_map/dot_general | solution.py:28
  385.4 3.6 copy.97
  389.0 3.5 fusion.24
  392.7 3.5 constant_dynamic-update-slice_fusion.7
  396.3 4.1 constant_dynamic-update-slice_fusion.6
  400.4 4.5 copy-done.24
  404.9 13.0 %fusion.29 = bf16[768,1536]{0,1:T(8,128)(2,1)} fusion(bf16[32,128,1536]{2,1,0:T(8,128)(2,1)S(1)} %constant_dynamic-update-slice_fusion.6, bf16[32,128,768]{2,1,0:T(8,128)(2,1)} %param.21), kind=kOutput, calls=%fused_computation.52 | convolution fusion | flops 9664856064 | bytes 21233664 | tf_op jit(solution)/shard_map/dot_general | solution.py:28
  417.9 4.4 copy.106
  422.4 3.5 constant_dynamic-update-slice_fusion.8
  425.9 0.8 copy-done.26
  426.7 7.4 %fusion.8 = bf16[768,6272]{1,0:T(8,128)(2,1)} fusion(bf16[768,6272]{1,0:T(8,128)(2,1)} %constant_dynamic-update-slice_fusion.8, bf16[1024,768]{1,0:T(8,128)(2,1)S(1)} %copy-done.26, bf16[1024,768]{1,0:T(8,128)(2,1)} %get-tuple-element.99, bf16[1024,768]{1,0:T(8,128)(2,1)S(1)} %copy-done.25, bf16[1,1024,768]{1,2,0:T(8,128)(2,1)S(1)} %copy-done.14, ...), kind=kOutput, calls=%fused_computation.16 | convolution fusion | flops 3644522496 | bytes 9844736 | tf_op jit(solution)/shard_map/dot_general | solution.py:28
  434.2 2.5 fusion.38
  436.8 2.6 fusion.37
  439.4 2.5 fusion.36
  442.7 11.3 %fusion.39 = bf16[1,1024,768]{1,2,0:T(8,128)(2,1)} fusion(f32[1024,768]{0,1:T(8,128)S(1)} %get-tuple-element.106, bf16[3072,768]{1,0:T(8,128)(2,1)} %all-gather.8.cloned.1.call-done, f32[1024,3072]{1,0:T(8,128)} %copy-done.18), kind=kOutput, calls=%fused_computation.77 | convolution fusion | flops 4861722624 | bytes 22020096 | tf_op jit(solution)/shard_map/dot_general | solution.py:28
  453.9 2.9 copy.107
  456.9 5.5 fusion.23
  462.4 3.5 copy.108
  466.0 16.5 %fusion.30 = f32[32,128,768]{2,1,0:T(8,128)} fusion(bf16[32,128,1536]{2,1,0:T(8,128)(2,1)} %copy-done.24, bf16[768,6272]{1,0:T(8,128)(2,1)} %all-gather.4.cloned.1.call-done), kind=kOutput, calls=%fused_computation.58 | convolution fusion | flops 9663676416 | bytes 27525120 | tf_op jit(solution)/shard_map/dot_general | solution.py:28
  482.4 1.6 convert_element_type.117
  484.1 1.6 convert_element_type.115
  485.7 136.9 %reduce-scatter.10.cloned.1.call-done = bf16[24,6272]{1,0:T(8,128)(2,1)} async-done(((bf16[768,6272]{1,0:T(8,128)(2,1)}), bf16[24,6272]{1,0:T(8,128)(2,1)}) %reduce-scatter.10.cloned.1.call-update) | async-done | bytes 301072
  622.6 1.0 convert_element_type.113
  623.6 0.8 slice_reduce_fusion.6
  624.4 1.6 slice.129
  626.0 1.6 slice.124
  627.6 1.5 fusion.56
  (118 shorter events, 8.7 us)
Async XLA Ops:
  7.2 91.4 %all-gather.4.cloned.1.call-start = ((), (), s32[]{:S(2)}) async-start(), calls=%async_computation.3 | async-start | bytes 9934848 | tf_op jit(solution)/shard_map/all_gather | solution.py:451
  12.2 0.7 copy-start.29
  13.0 179.0 %all-gather.6.cloned.1.call-start = ((), (), s32[]{:S(2)}) async-start(), calls=%async_computation.4 | async-start | bytes 4866048 | tf_op jit(solution)/shard_map/all_gather | solution.py:460
  13.7 215.5 %all-gather.8.cloned.1.call-start = ((), (), s32[]{:S(2)}) async-start(), calls=%async_computation.5 | async-start | bytes 4866048 | tf_op jit(solution)/shard_map/all_gather | solution.py:461
  14.4 468.0 %reduce-scatter.8.cloned.1.call-start = ((), (), s32[]{:S(2)}) async-start(), calls=%async_computation.7 | async-start | bytes 4866048 | tf_op jit(solution)/shard_map/reduce_scatter | solution.py:524
  16.0 155.0 %copy-start.5 = (s32[32]{0:T(128)}, s32[32]{0:T(128)S(1)}, u32[]{:S(2)}) copy-start(s32[32]{0:T(128)S(1)} %reshape.106.ids_ref) | copy-start | bytes 388
  16.0 2.6 copy-start.27
  17.8 115.2 %copy-start.12 = (bf16[1,1024,768]{1,2,0:T(8,128)(2,1)}, bf16[1,1024,768]{1,2,0:T(8,128)(2,1)S(1)}, u32[]{:S(2)}) copy-start(bf16[1,1024,768]{1,2,0:T(8,128)(2,1)S(1)} %copy.89) | copy-start | bytes 4718596
  133.0 7.9 %copy-start.32 = (f32[768]{0:T(1024)}, f32[768]{0:T(1024)S(1)}, u32[]{:S(2)}) copy-start(f32[768]{0:T(1024)S(1)} %get-tuple-element.95) | copy-start | bytes 9220
  133.0 34.2 %copy-start.30 = (f32[768]{0:T(1024)}, f32[768]{0:T(1024)S(1)}, u32[]{:S(2)}) copy-start(f32[768]{0:T(1024)S(1)} %get-tuple-element.93) | copy-start | bytes 9220
  140.8 22.3 %copy-start.13 = (bf16[1,1024,768]{1,2,0:T(8,128)(2,1)S(1)}, bf16[1,1024,768]{1,2,0:T(8,128)(2,1)}, u32[]{:S(2)}) copy-start(bf16[1,1024,768]{1,2,0:T(8,128)(2,1)} %copy-done.12) | copy-start | bytes 4718596
  163.1 3.7 copy-start.3
  163.1 3.7 copy-start.7
  166.8 21.4 %copy-start.9 = (f32[1024,768]{0,1:T(8,128)}, f32[1024,768]{0,1:T(8,128)S(1)}, u32[]{:S(2)}) copy-start(f32[1024,768]{0,1:T(8,128)S(1)} %get-tuple-element.104) | copy-start | bytes 9437188
  167.2 3.7 copy-start.6
  170.9 17.2 %copy-start = (bf16[1024,768]{1,0:T(8,128)(2,1)}, bf16[1024,768]{1,0:T(8,128)(2,1)S(1)}, u32[]{:S(2)}) copy-start(bf16[1024,768]{1,0:T(8,128)(2,1)S(1)} %convolution_convert_fusion.7.query_ref) | copy-start | bytes 4718596
  188.2 3.3 copy-start.1
  191.9 12.6 %copy-start.28 = (bf16[1,1024,768]{2,1,0:T(8,128)(2,1)S(1)}, bf16[1,1024,768]{2,1,0:T(8,128)(2,1)}, u32[]{:S(2)}) copy-start(bf16[1,1024,768]{2,1,0:T(8,128)(2,1)} %param.37) | copy-start | bytes 4718596
  199.7 4.8 copy-start.18
  213.9 270.2 %reduce-scatter.6.cloned.1.call-start = ((), (), s32[]{:S(2)}) async-start(), calls=%async_computation.6 | async-start | bytes 4866048 | tf_op jit(solution)/shard_map/reduce_scatter | solution.py:524
  244.5 11.5 %copy-start.35 = (bf16[1024,3072]{1,0:T(8,128)(2,1)}, bf16[1024,3072]{1,0:T(8,128)(2,1)S(1)}, u32[]{:S(2)}) copy-start(bf16[1024,3072]{1,0:T(8,128)(2,1)S(1)} %fusion.7) | copy-start | bytes 18874372
  259.9 3.1 copy-start.16
  259.9 3.5 copy-start.23
  264.4 1.7 copy-start.19
  327.2 4.0 copy-start.10
  327.2 4.7 copy-start.17
  334.7 3.9 copy-start.21
  334.7 3.9 copy-start.4
  334.8 34.6 %slice-start = ((s8[6291456]{0:T(1024)(128)(4,1)}), s8[4194304]{0:T(1024)(128)(4,1)S(1)}, s32[]{:S(2)}) async-start(s8[6291456]{0:T(1024)(128)(4,1)} %bitcast.106), calls=%async_computation.9 | async-start | bytes 8388608
  338.6 30.8 %slice-start.1 = ((s8[6291456]{0:T(1024)(128)(4,1)}), s8[2097152]{0:T(1024)(128)(4,1)S(1)}, s32[]{:S(2)}) async-start(s8[6291456]{0:T(1024)(128)(4,1)} %bitcast.106), calls=%async_computation.10 | async-start | bytes 4194304
  376.3 246.3 %reduce-scatter.10.cloned.1.call-start = ((), (), s32[]{:S(2)}) async-start(), calls=%async_computation.8 | async-start | bytes 9934848
  400.4 4.5 copy-start.24
  404.9 21.0 %copy-start.33 = (f32[768]{0:T(1024)S(1)}, f32[768]{0:T(1024)}, u32[]{:S(2)}) copy-start(f32[768]{0:T(1024)} %copy-done.32) | copy-start | bytes 9220
  422.3 3.6 copy-start.14
  422.4 3.5 copy-start.25
  422.4 4.4 copy-start.26
  426.7 7.5 %copy-start.8 = (bf16[1024,768]{1,0:T(8,128)(2,1)S(1)}, bf16[1024,768]{1,0:T(8,128)(2,1)}, u32[]{:S(2)}) copy-start(bf16[1024,768]{1,0:T(8,128)(2,1)} %copy-done.7) | copy-start | bytes 4718596
  426.7 7.5 %copy-start.22 = (f32[1024,768]{0,1:T(8,128)S(1)}, f32[1024,768]{0,1:T(8,128)}, u32[]{:S(2)}) copy-start(f32[1024,768]{0,1:T(8,128)} %copy-done.21) | copy-start | bytes 9437188
  434.2 2.6 copy-start.11
  434.2 2.6 copy-start.31
  434.2 2.6 copy-start.34
  436.8 2.6 copy-start.2
  436.8 2.6 copy-start.20
  453.9 2.9 copy-start.15
Sparse Core Ops, SparseCore 0:
  13.1 85.4 all-gather.3
  101.5 62.2 all-gather.5
  166.7 62.4 all-gather.7
  234.5 105.7 reduce-scatter.7
  376.5 105.8 reduce-scatter.5
  488.3 134.3 reduce-scatter.9

commit v2 on v1

--- a/solution.py
+++ b/solution.py
@@ -389,6 +389,194 @@
         name="cross_backward",
     )(ids, neighbour_lengths, queries, grads, pool_keyval, pool_keyval, pool_keyval, pool_keyval)
 
+AXES = ("fsdp", "dp")
+
+
+def bits_of(size):
+    return [1 << i for i in range(size.bit_length() - 1)]
+
+
+def index_bits(count):
+    return [1 << i for i in range(count.bit_length() - 2, -1, -1)]
+
+
+def place(side, own, other):
+    return jnp.stack([jnp.where(side == 0, own, other), jnp.where(side == 0, other, own)])
+
+
+class Plan:
+    def __init__(self, rows):
+        self.inner = lax.axis_size("dp")
+        self.outer = lax.axis_size("fsdp")
+        self.count = self.inner * self.outer
+        self.rows = rows
+        self.core = [self.inner] if self.outer > 1 else []
+        self.halves = 2 if self.core else 1
+        self.across = self.outer // self.halves
+        self.stripe = self.inner * rows
+        self.half_rows = self.across * self.stripe
+        self.me = lax.axis_index(AXES)
+        across = [bit * self.inner for bit in bits_of(self.outer)[1:]]
+        along = bits_of(self.inner)
+        near, far = along[: len(across)], along[len(across) :]
+        self.orders = (far + near + across, far + across + near)
+        self.natural = [mask for mask in index_bits(self.count) if mask not in self.core]
+        self.odd = self.bit(self.core[0]) if self.core else jnp.zeros((), jnp.int32)
+        self.odd_word = self.odd.reshape(1)
+
+    def steps(self):
+        return list(zip(*self.orders))
+
+    def bit(self, mask):
+        return (self.me // mask) % 2
+
+    def side(self, masks):
+        even, odd = masks
+        return jnp.where(self.odd == 0, self.bit(even), self.bit(odd))
+
+    def exchange(self, values, masks):
+        even, odd = masks
+        pairs = []
+        for index in range(self.count):
+            is_odd = bool(self.core) and (index // self.core[0]) % 2 == 1
+            pairs.append((index, index ^ (odd if is_odd else even)))
+        return lax.ppermute(values, AXES, pairs)
+
+    def swap(self, values):
+        return self.exchange(values, (self.core[0], self.core[0])) if self.core else values
+
+
+def reorder_kernel(moves, odd_ref, in_ref, out_ref, buffer, sems):
+    for parity, pairs in enumerate(moves):
+
+        @pl.when(odd_ref[0] == parity)
+        def _():
+            for source, target in pairs:
+                pltpu.make_async_copy(
+                    in_ref.at[source], buffer.at[target], sems.at[source]
+                ).start()
+            for source, target in pairs:
+                pltpu.make_async_copy(
+                    in_ref.at[source], buffer.at[target], sems.at[source]
+                ).wait()
+
+    pltpu.sync_copy(buffer, out_ref)
+
+
+def reorder(plan, held):
+    blocks = held.shape[0]
+    moves = []
+    for order in plan.orders[: plan.halves]:
+        pairs = []
+        for source in range(blocks):
+            target = 0
+            for place_at, mask in enumerate(order):
+                if (source >> place_at) & 1:
+                    target += 1 << (len(plan.natural) - 1 - plan.natural.index(mask))
+            pairs.append((source, target))
+        moves.append(pairs)
+    return pl.pallas_call(
+        functools.partial(reorder_kernel, moves),
+        in_specs=[pl.BlockSpec(memory_space=pltpu.SMEM), pl.BlockSpec(memory_space=pl.ANY)],
+        out_specs=pl.BlockSpec(memory_space=pl.ANY),
+        out_shape=jax.ShapeDtypeStruct(held.shape, held.dtype),
+        scratch_shapes=[pltpu.VMEM(held.shape, held.dtype), pltpu.SemaphoreType.DMA((blocks,))],
+        compiler_params=pltpu.CompilerParams(vmem_limit_bytes=32 * 2**20),
+        name="reorder_blocks",
+    )(plan.odd_word, held)
+
+
+def gather_halves(plan, shard):
+    columns = shard.shape[1]
+    held = shard
+    for masks in plan.steps():
+        other = plan.exchange(held, masks)
+        held = place(plan.side(masks), held, other)
+    held = reorder(plan, held.reshape((-1,) + shard.shape))
+    other = plan.swap(held)
+    shape = (plan.half_rows, columns)
+    return (held.reshape(shape), other.reshape(shape))
+
+
+def scatter_halves(plan, keep, send):
+    columns = keep.shape[1]
+    shape = (2,) * len(plan.natural) + (plan.rows, columns)
+    blocks = [keep.reshape(shape)]
+    if plan.core:
+        blocks.append(plan.swap(send).reshape(shape))
+
+    def add(parts):
+        total = parts[0].astype(F32)
+        for part in parts[1:]:
+            total = total + part.astype(F32)
+        return total.astype(BF16)
+
+    def pick(parts, axes, index):
+        chosen = []
+        for part in parts:
+            even, odd = [lax.dynamic_index_in_dim(part, index, axis, False) for axis in axes]
+            chosen.append(even if axes[0] == axes[1] else jnp.where(plan.odd == 0, even, odd))
+        return add(chosen)
+
+    layouts = [list(plan.natural), list(plan.natural)]
+    for masks in plan.steps()[::-1]:
+        axes = tuple(layouts[parity].index(masks[parity]) for parity in range(2))
+        side = plan.side(masks)
+        sent = pick(blocks, axes, 1 - side)
+        kept = pick(blocks, axes, side)
+        blocks = [kept, plan.exchange(sent, masks)]
+        for parity in range(2):
+            layouts[parity].pop(axes[parity])
+    total = blocks[0].astype(F32)
+    for part in blocks[1:]:
+        total = total + part.astype(F32)
+    return total.reshape(plan.rows, columns)
+
+
+def column_copies(plan, odd, held_ref, other_ref, target, sems, start, width):
+    copies = []
+    for across in range(plan.across):
+        source_rows = pl.ds(across * plan.stripe, plan.stripe)
+        for turn, ref in enumerate((held_ref, other_ref)[: plan.halves]):
+            half = odd if turn == 0 else 1 - odd
+            first = across * plan.halves * plan.stripe + half * plan.stripe
+            if plan.halves == 1:
+                first = across * plan.stripe
+            elif plan.stripe % 16 == 0:
+                first = pl.multiple_of(first, 16)
+            copies.append(
+                pltpu.make_async_copy(
+                    ref.at[source_rows, pl.ds(start, width)],
+                    target.at[pl.ds(first, plan.stripe), :],
+                    sems.at[across * plan.halves + turn],
+                )
+            )
+    return copies
+
+
+def store_halves(plan, odd, result, keep_ref, send_ref, columns):
+    for across in range(plan.across):
+        rows = slice(across * plan.stripe, (across + 1) * plan.stripe)
+        for half in range(plan.halves):
+            first = (across * plan.halves + half) * plan.stripe
+            part = result[first : first + plan.stripe]
+            if plan.halves == 1:
+                keep_ref[rows, columns] = part
+                continue
+
+            @pl.when(odd == half)
+            def _():
+                keep_ref[rows, columns] = part
+
+            @pl.when(odd != half)
+            def _():
+                send_ref[rows, columns] = part
+
+ROWS = 256
+MEBI = 2**20
+ANYWHERE = pl.BlockSpec(memory_space=pl.ANY)
+SCALAR = pl.BlockSpec(memory_space=pltpu.SMEM)
+
 
 def norm_parts(values):
     centre = jnp.mean(values, axis=-1, keepdims=True)
@@ -398,26 +586,632 @@
     return (centred * inverse, inverse)
 
 
-def norm_apply(values, gain, shift):
-    return norm_parts(values)[0] * gain + shift
-
-
 def norm_back(values, gain, upstream):
     unit, inverse = norm_parts(values)
-    gain_term = jnp.sum(upstream * unit, axis=0)
-    shift_term = jnp.sum(upstream, axis=0)
+    gain_term = jnp.sum(upstream * unit, axis=0, keepdims=True)
+    shift_term = jnp.sum(upstream, axis=0, keepdims=True)
     inner = upstream * gain
     mean_inner = jnp.mean(inner, axis=-1, keepdims=True)
     mean_both = jnp.mean(inner * unit, axis=-1, keepdims=True)
     return (inverse * (inner - mean_inner - unit * mean_both), gain_term, shift_term)
 
 
-def gelu_tanh(values):
-    return jax.nn.gelu(values, approximate=True)
-
-
-AXES = ("fsdp", "dp")
-
+def add_terms(step, target_ref, gain_term, shift_term):
+    @pl.when(step == 0)
+    def _():
+        target_ref[...] = jnp.zeros_like(target_ref)
+
+    target_ref[0:1] += gain_term
+    target_ref[1:2] += shift_term
+
+
+def start_all(copies):
+    for copy in copies:
+        copy.start()
+
+
+def wait_all(copies):
+    for copy in copies:
+        copy.wait()
+
+
+def row_block(columns, last=None):
+    if last is None:
+        return pl.BlockSpec((ROWS, columns), lambda i: (i, 0))
+    return pl.BlockSpec((ROWS, columns), lambda i: (jnp.minimum(i, last), 0))
+
+
+def params(megabytes):
+    return pltpu.CompilerParams(vmem_limit_bytes=megabytes * MEBI)
+
+
+def copy_sems(plan, *sets):
+    return pltpu.SemaphoreType.DMA(sets + (plan.across * plan.halves,))
+
+
+def pool_kernel(plan, odd_ref, rows_ref, held_ref, other_ref, out_ref, weight, sems):
+    width = weight.shape[1]
+
+    @pl.when(pl.program_id(0) == 0)
+    def _():
+        copies = column_copies(plan, odd_ref[0], held_ref, other_ref, weight, sems, 0, width)
+        start_all(copies)
+        wait_all(copies)
+
+    out_ref[...] = dot(rows_ref[...], weight[...]).astype(BF16)
+
+
+def pool_project(plan, encoded, halves):
+    rows, width = encoded.shape
+    block = 512
+    return pl.pallas_call(
+        functools.partial(pool_kernel, plan),
+        grid=(rows // block,),
+        in_specs=[SCALAR, pl.BlockSpec((block, width), lambda i: (i, 0)), ANYWHERE, ANYWHERE],
+        out_specs=pl.BlockSpec((block, 2 * width), lambda i: (i, 0)),
+        out_shape=jax.ShapeDtypeStruct((rows, 2 * width), BF16),
+        scratch_shapes=[pltpu.VMEM((width, 2 * width), BF16), copy_sems(plan)],
+        compiler_params=params(40),
+        name="pool_project",
+    )(plan.odd_word, encoded, *halves)
+
+
+def project_kernel(
+    plan,
+    odd_ref,
+    tokens_ref,
+    held_ref,
+    other_ref,
+    first_in_ref,
+    projected_ref,
+    vectors_ref,
+    weight,
+    pack,
+    sems,
+):
+    width = tokens_ref.shape[1]
+
+    @pl.when(pl.program_id(0) == 0)
+    def _():
+        copies = column_copies(plan, odd_ref[0], held_ref, other_ref, weight, sems.at[0], 0, 3 * width)
+        copies += column_copies(
+            plan, odd_ref[0], held_ref, other_ref, pack, sems.at[1], 3 * width, LANES
+        )
+        start_all(copies)
+        wait_all(copies)
+        vectors_ref[...] = pack[...].astype(F32).T[:8]
+
+    unit = norm_parts(tokens_ref[...].astype(F32))[0]
+    first_in = (unit * vectors_ref[0:1] + vectors_ref[1:2]).astype(BF16)
+    first_in_ref[...] = first_in
+    projected_ref[...] = dot(first_in, weight[...]).astype(BF16)
+
+
+def project(plan, tokens, halves):
+    rows, width = tokens.shape
+    return pl.pallas_call(
+        functools.partial(project_kernel, plan),
+        grid=(rows // ROWS,),
+        in_specs=[SCALAR, row_block(width), ANYWHERE, ANYWHERE],
+        out_specs=[
+            row_block(width),
+            row_block(3 * width),
+            pl.BlockSpec((8, width), lambda i: (0, 0)),
+        ],
+        out_shape=[
+            jax.ShapeDtypeStruct((rows, width), BF16),
+            jax.ShapeDtypeStruct((rows, 3 * width), BF16),
+            jax.ShapeDtypeStruct((8, width), F32),
+        ],
+        scratch_shapes=[
+            pltpu.VMEM((width, 3 * width), BF16),
+            pltpu.VMEM((width, LANES), BF16),
+            copy_sems(plan, 2),
+        ],
+        compiler_params=params(40),
+        name="project",
+    )(plan.odd_word, tokens, *halves)
+
+
+def middle_kernel(
+    plan,
+    starts,
+    odd_ref,
+    tokens_ref,
+    mixed_ref,
+    vectors_ref,
+    held_ref,
+    other_ref,
+    after_ref,
+    second_in_ref,
+    queries_ref,
+    out_weight,
+    query_weight,
+    sems,
+):
+    width = tokens_ref.shape[1]
+
+    @pl.when(pl.program_id(0) == 0)
+    def _():
+        copies = []
+        for place_at, target in enumerate((out_weight, query_weight)):
+            copies += column_copies(
+                plan, odd_ref[0], held_ref, other_ref, target, sems.at[place_at], starts[place_at], width
+            )
+        start_all(copies)
+        wait_all(copies)
+
+    after = tokens_ref[...].astype(F32) + dot(mixed_ref[...], out_weight[...])
+    after_ref[...] = after
+    unit = norm_parts(after)[0]
+    second_in = (unit * vectors_ref[2:3] + vectors_ref[3:4]).astype(BF16)
+    second_in_ref[...] = second_in
+    queries_ref[...] = dot(second_in, query_weight[...]).astype(BF16)
+
+
+def middle(plan, starts, tokens, mixed, vectors, halves):
+    rows, width = tokens.shape
+    return pl.pallas_call(
+        functools.partial(middle_kernel, plan, starts),
+        grid=(rows // ROWS,),
+        in_specs=[
+            SCALAR,
+            row_block(width),
+            row_block(width),
+            pl.BlockSpec((8, width), lambda i: (0, 0)),
+            ANYWHERE,
+            ANYWHERE,
+        ],
+        out_specs=[row_block(width)] * 3,
+        out_shape=[
+            jax.ShapeDtypeStruct((rows, width), F32),
+            jax.ShapeDtypeStruct((rows, width), BF16),
+            jax.ShapeDtypeStruct((rows, width), BF16),
+        ],
+        scratch_shapes=[
+            pltpu.VMEM((width, width), BF16),
+            pltpu.VMEM((width, width), BF16),
+            copy_sems(plan, 2),
+        ],
+        compiler_params=params(40),
+        name="middle",
+    )(plan.odd_word, tokens, mixed, vectors, *halves)
+
+
+GELU_SCALE = 0.7978845608028654
+GELU_CUBE = 0.044715
+
+
+def gelu_both(values):
+    square = values * values
+    bent = jnp.tanh(values * (GELU_SCALE + (GELU_SCALE * GELU_CUBE) * square))
+    half = 0.5 + 0.5 * bent
+    slope = GELU_SCALE + (3.0 * GELU_SCALE * GELU_CUBE) * square
+    return (values * half, half + (0.5 * values) * (1.0 - bent * bent) * slope)
+
+
+def feed_kernel(
+    plan,
+    out_start,
+    row_steps,
+    odd_ref,
+    after_ref,
+    mixed_ref,
+    cotangent_ref,
+    vectors_ref,
+    feed_held_ref,
+    feed_other_ref,
+    held_ref,
+    other_ref,
+    block_ref,
+    grad_ref,
+    mixed_grad_ref,
+    terms_ref,
+    keep_ref,
+    send_ref,
+    weights,
+    lefts,
+    rights,
+    sems,
+):
+    step = pl.program_id(0)
+    width = after_ref.shape[1]
+    parts = (weights.shape[0] - 1) // 2
+
+    def copies(index):
+        if index == 2 * parts:
+            return column_copies(
+                plan, odd_ref[0], held_ref, other_ref, weights.at[index], sems.at[index], out_start, width
+            )
+        return column_copies(
+            plan,
+            odd_ref[0],
+            feed_held_ref,
+            feed_other_ref,
+            weights.at[index],
+            sems.at[index],
+            index * width,
+            width,
+        )
+
+    @pl.when(step == 0)
+    def _():
+        order = [2 * parts]
+        for part in range(parts):
+            order += [part, parts + part]
+        for index in order:
+            start_all(copies(index))
+
+    def ready(index):
+        @pl.when(step == 0)
+        def _():
+            wait_all(copies(index))
+
+        return weights[index]
+
+    @pl.when(step < row_steps)
+    def _():
+        place_at = pl.ds(pl.multiple_of(step * ROWS, ROWS), ROWS)
+        mixed = mixed_ref[...]
+        cotangent = cotangent_ref[...]
+        out_weight = ready(2 * parts)
+        after_cross = after_ref[...] + dot(mixed, out_weight)
+        unit, inverse = norm_parts(after_cross)
+        gain = vectors_ref[4:5]
+        third_in = (unit * gain + vectors_ref[5:6]).astype(BF16)
+        lefts[parts, :, place_at] = third_in.T
+        lefts[parts + 1, :, place_at] = mixed.T
+        rights[0, place_at] = cotangent
+        result = after_cross
+        upstream = jnp.zeros_like(after_cross)
+        for part in range(parts):
+            up = ready(part)
+            hidden, slope = gelu_both(dot(third_in, up))
+            hidden = hidden.astype(BF16)
+            lefts[part, :, place_at] = hidden.T
+            down = ready(parts + part)
+            result = result + dot(hidden, down)
+            hidden_grad = (slope * dot(cotangent, down, NT)).astype(BF16)
+            rights[1 + part, place_at] = hidden_grad
+            upstream = upstream + dot(hidden_grad, up, NT)
+        block_ref[...] = result.astype(BF16)
+        inner = upstream * gain
+        mean_inner = jnp.mean(inner, axis=-1, keepdims=True)
+        mean_both = jnp.mean(inner * unit, axis=-1, keepdims=True)
+        grad = cotangent.astype(F32) + inverse * (inner - mean_inner - unit * mean_both)
+        add_terms(
+            step,
+            terms_ref,
+            jnp.sum(upstream * unit, axis=0, keepdims=True),
+            jnp.sum(upstream, axis=0, keepdims=True),
+        )
+        grad_ref[...] = grad
+        rounded = grad.astype(BF16)
+        rights[parts + 1, place_at] = rounded
+        mixed_grad_ref[...] = dot(rounded, out_weight, NT).astype(BF16)
+
+    @pl.when(step >= row_steps)
+    def _():
+        term = step - row_steps
+        left = jnp.where(term < parts, term, jnp.where(term < 2 * parts, parts, parts + 1))
+        right = jnp.where(term < parts, 0, term - parts + 1)
+        result = dot(lefts[left], rights[right]).astype(BF16)
+        store_halves(plan, odd_ref[0], result, keep_ref, send_ref, slice(0, width))
+
+
+def feed(plan, out_start, after, mixed, cotangent, vectors, feed_halves, halves):
+    rows, width = after.shape
+    parts = feed_halves[0].shape[1] // width // 2
+    terms = 2 * parts + 1
+    steps = rows // ROWS
+    last = steps - 1
+    rows_in = row_block(width, last)
+    whole = pl.BlockSpec((8, width), lambda i: (0, 0))
+    slab = pl.BlockSpec((plan.half_rows, width), lambda i: (0, jnp.maximum(i - steps, 0)))
+    slab_shape = jax.ShapeDtypeStruct((plan.half_rows, terms * width), BF16)
+    return pl.pallas_call(
+        functools.partial(feed_kernel, plan, out_start, steps),
+        grid=(steps + terms,),
+        in_specs=[SCALAR, rows_in, rows_in, rows_in, whole] + [ANYWHERE] * 4,
+        out_specs=[rows_in, rows_in, rows_in, whole, slab, slab],
+        out_shape=[
+            jax.ShapeDtypeStruct((rows, width), BF16),
+            jax.ShapeDtypeStruct((rows, width), F32),
+            jax.ShapeDtypeStruct((rows, width), BF16),
+            jax.ShapeDtypeStruct((8, width), F32),
+            slab_shape,
+            slab_shape,
+        ],
+        scratch_shapes=[
+            pltpu.VMEM((terms, width, width), BF16),
+            pltpu.VMEM((parts + 2, width, rows), BF16),
+            pltpu.VMEM((parts + 2, rows, width), BF16),
+            copy_sems(plan, terms),
+        ],
+        compiler_params=params(60),
+        name="feed_forward",
+    )(plan.odd_word, after, mixed, cotangent, vectors, *feed_halves, *halves)
+
+
+def second_kernel(
+    plan,
+    starts,
+    row_steps,
+    odd_ref,
+    after_ref,
+    grad_in_ref,
+    query_grad_ref,
+    second_in_ref,
+    mixed_ref,
+    vectors_ref,
+    held_ref,
+    other_ref,
+    grad_ref,
+    attend_ref,
+    terms_ref,
+    keep_ref,
+    send_ref,
+    out_weight,
+    query_weight,
+    lefts,
+    rights,
+    sems,
+):
+    step = pl.program_id(0)
+    width = after_ref.shape[1]
+
+    @pl.when(step == 0)
+    def _():
+        copies = []
+        for place_at, target in enumerate((out_weight, query_weight)):
+            copies += column_copies(
+                plan, odd_ref[0], held_ref, other_ref, target, sems.at[place_at], starts[place_at], width
+            )
+        start_all(copies)
+        wait_all(copies)
+
+    @pl.when(step < row_steps)
+    def _():
+        place_at = pl.ds(pl.multiple_of(step * ROWS, ROWS), ROWS)
+        query_grad = query_grad_ref[...]
+        back, gain_term, shift_term = norm_back(
+            after_ref[...], vectors_ref[2:3], dot(query_grad, query_weight[...], NT)
+        )
+        add_terms(step, terms_ref, gain_term, shift_term)
+        grad = grad_in_ref[...] + back
+        grad_ref[...] = grad
+        rounded = grad.astype(BF16)
+        attend_ref[...] = dot(rounded, out_weight[...], NT).astype(BF16)
+        lefts[0, :, place_at] = second_in_ref[...].T
+        lefts[1, :, place_at] = mixed_ref[...].T
+        rights[0, place_at] = query_grad
+        rights[1, place_at] = rounded
+
+    @pl.when(step >= row_steps)
+    def _():
+        term = step - row_steps
+        result = dot(lefts[term], rights[term]).astype(BF16)
+        store_halves(plan, odd_ref[0], result, keep_ref, send_ref, slice(0, width))
+
+
+def second_back(plan, starts, after, grad_in, query_grad, second_in, mixed, vectors, halves):
+    rows, width = after.shape
+    steps = rows // ROWS
+    rows_in = row_block(width, steps - 1)
+    whole = pl.BlockSpec((8, width), lambda i: (0, 0))
+    slab = pl.BlockSpec((plan.half_rows, width), lambda i: (0, jnp.maximum(i - steps, 0)))
+    slab_shape = jax.ShapeDtypeStruct((plan.half_rows, 2 * width), BF16)
+    return pl.pallas_call(
+        functools.partial(second_kernel, plan, starts, steps),
+        grid=(steps + 2,),
+        in_specs=[SCALAR] + [rows_in] * 5 + [whole, ANYWHERE, ANYWHERE],
+        out_specs=[rows_in, rows_in, whole, slab, slab],
+        out_shape=[
+            jax.ShapeDtypeStruct((rows, width), F32),
+            jax.ShapeDtypeStruct((rows, width), BF16),
+            jax.ShapeDtypeStruct((8, width), F32),
+            slab_shape,
+            slab_shape,
+        ],
+        scratch_shapes=[
+            pltpu.VMEM((width, width), BF16),
+            pltpu.VMEM((width, width), BF16),
+            pltpu.VMEM((2, width, rows), BF16),
+            pltpu.VMEM((2, rows, width), BF16),
+            copy_sems(plan, 2),
+        ],
+        compiler_params=params(48),
+        name="second_back",
+    )(plan.odd_word, after, grad_in, query_grad, second_in, mixed, vectors, *halves)
+
+
+def first_kernel(
+    plan,
+    row_steps,
+    odd_ref,
+    tokens_ref,
+    grad_in_ref,
+    projected_grad_ref,
+    first_in_ref,
+    vectors_ref,
+    second_terms_ref,
+    third_terms_ref,
+    held_ref,
+    other_ref,
+    grad_ref,
+    keep_ref,
+    send_ref,
+    weight,
+    terms,
+    left,
+    rights,
+    sems,
+):
+    step = pl.program_id(0)
+    width = tokens_ref.shape[1]
+
+    @pl.when(step == 0)
+    def _():
+        copies = column_copies(plan, odd_ref[0], held_ref, other_ref, weight, sems, 0, 3 * width)
+        start_all(copies)
+        wait_all(copies)
+
+    place_at = pl.ds(pl.multiple_of(step * ROWS, ROWS), ROWS)
+    upstream = None
+    for part in range(3):
+        grads = projected_grad_ref[part]
+        rights[part, place_at] = grads
+        product = dot(grads, weight[:, part * width : (part + 1) * width], NT)
+        upstream = product if upstream is None else upstream + product
+    back, gain_term, shift_term = norm_back(
+        tokens_ref[...].astype(F32), vectors_ref[0:1], upstream
+    )
+    add_terms(step, terms, gain_term, shift_term)
+    grad_ref[...] = grad_in_ref[...] + back
+    left[:, place_at] = first_in_ref[...].T
+
+    @pl.when(step == row_steps - 1)
+    def _():
+        for part in range(3):
+            result = dot(left[...], rights[part]).astype(BF16)
+            columns = slice(part * width, (part + 1) * width)
+            store_halves(plan, odd_ref[0], result, keep_ref, send_ref, columns)
+        rows = jnp.concatenate(
+            [
+                terms[0:2],
+                second_terms_ref[0:2],
+                third_terms_ref[0:2],
+                jnp.zeros((LANES - 6, width), F32),
+            ],
+            axis=0,
+        )
+        columns = slice(3 * width, 3 * width + LANES)
+        store_halves(plan, odd_ref[0], rows.T.astype(BF16), keep_ref, send_ref, columns)
+
+
+def first_back(
+    plan, tokens, grad_in, projected_grad, first_in, vectors, second_terms, third_terms, halves
+):
+    rows, width = tokens.shape
+    steps = rows // ROWS
+    rows_in = row_block(width)
+    whole = pl.BlockSpec((8, width), lambda i: (0, 0))
+    columns = 3 * width + LANES
+    slab = pl.BlockSpec((plan.half_rows, columns), lambda i: (0, 0))
+    slab_shape = jax.ShapeDtypeStruct((plan.half_rows, columns), BF16)
+    return pl.pallas_call(
+        functools.partial(first_kernel, plan, steps),
+        grid=(steps,),
+        in_specs=[
+            SCALAR,
+            rows_in,
+            rows_in,
+            pl.BlockSpec((3, ROWS, width), lambda i: (0, i, 0)),
+            rows_in,
+            whole,
+            whole,
+            whole,
+            ANYWHERE,
+            ANYWHERE,
+        ],
+        out_specs=[rows_in, slab, slab],
+        out_shape=[jax.ShapeDtypeStruct((rows, width), F32), slab_shape, slab_shape],
+        scratch_shapes=[
+            pltpu.VMEM((width, 3 * width), BF16),
+            pltpu.VMEM((8, width), F32),
+            pltpu.VMEM((width, rows), BF16),
+            pltpu.VMEM((3, rows, width), BF16),
+            copy_sems(plan),
+        ],
+        compiler_params=params(56),
+        name="first_back",
+    )(
+        plan.odd_word,
+        tokens,
+        grad_in,
+        projected_grad,
+        first_in,
+        vectors,
+        second_terms,
+        third_terms,
+        *halves,
+    )
+
+
+def keyval_kernel(
+    plan, odd_ref, rows_ref, key_ref, value_ref, keep_ref, send_ref, key_total, value_total
+):
+    step = pl.program_id(0)
+    width = rows_ref.shape[1]
+    turned = rows_ref[...].T
+    key_part = dot(turned, key_ref[...])
+    value_part = dot(turned, value_ref[...])
+
+    @pl.when(step == 0)
+    def _():
+        key_total[...] = key_part
+        value_total[...] = value_part
+
+    @pl.when(step > 0)
+    def _():
+        key_total[...] += key_part
+        value_total[...] += value_part
+
+    @pl.when(step == pl.num_programs(0) - 1)
+    def _():
+        for place_at, total in enumerate((key_total, value_total)):
+            columns = slice(place_at * width, (place_at + 1) * width)
+            store_halves(plan, odd_ref[0], total[...].astype(BF16), keep_ref, send_ref, columns)
+
+
+def keyval_terms(plan, encoded, pool_keys, pool_values):
+    rows, width = encoded.shape
+    block = 1024
+    rows_in = pl.BlockSpec((block, width), lambda i: (i, 0))
+    slab = pl.BlockSpec((plan.half_rows, 2 * width), lambda i: (0, 0))
+    slab_shape = jax.ShapeDtypeStruct((plan.half_rows, 2 * width), BF16)
+    return pl.pallas_call(
+        functools.partial(keyval_kernel, plan),
+        grid=(rows // block,),
+        in_specs=[SCALAR, rows_in, rows_in, rows_in],
+        out_specs=[slab, slab],
+        out_shape=[slab_shape, slab_shape],
+        scratch_shapes=[pltpu.VMEM((width, width), F32), pltpu.VMEM((width, width), F32)],
+        compiler_params=params(48),
+        name="keyval_terms",
+    )(plan.odd_word, encoded, pool_keys, pool_values)
+
+
+def neighbours_kernel(
+    plan, odd_ref, key_ref, value_ref, held_ref, other_ref, out_ref, weight, sems
+):
+    width = key_ref.shape[1]
+
+    @pl.when(pl.program_id(0) == 0)
+    def _():
+        copies = column_copies(plan, odd_ref[0], held_ref, other_ref, weight, sems, 0, 2 * width)
+        start_all(copies)
+        wait_all(copies)
+
+    out_ref[...] = dot(key_ref[...], weight[:, :width], NT) + dot(
+        value_ref[...], weight[:, width:], NT
+    )
+
+
+def neighbours_back(plan, pool_keys, pool_values, halves):
+    rows, width = pool_keys.shape
+    block = 512
+    rows_in = pl.BlockSpec((block, width), lambda i: (i, 0))
+    return pl.pallas_call(
+        functools.partial(neighbours_kernel, plan),
+        grid=(rows // block,),
+        in_specs=[SCALAR, rows_in, rows_in, ANYWHERE, ANYWHERE],
+        out_specs=rows_in,
+        out_shape=jax.ShapeDtypeStruct((rows, width), F32),
+        scratch_shapes=[pltpu.VMEM((width, 2 * width), BF16), copy_sems(plan)],
+        compiler_params=params(40),
+        name="neighbours_back",
+    )(plan.odd_word, pool_keys, pool_values, *halves)
 
 def local(
     tokens,
@@ -440,115 +1234,103 @@
     feed_down,
     cotangent,
 ):
-    _, seq_len, width = tokens.shape
+    rows, width = cross_query.shape
+    plan = Plan(rows)
+    parts = feed_down.shape[0] // rows
     pool_count, neigh_len = neighbours.shape[:2]
-    rows = self_input.shape[0]
     vectors = (first_gain, first_shift, second_gain, second_shift, third_gain, third_shift)
     vector_pack = jnp.pad(jnp.stack(vectors, axis=1), ((0, 0), (0, LANES - len(vectors))))
-    packed = jnp.concatenate(
-        [cross_keyval, self_input, self_output, cross_query, cross_output, vector_pack], axis=1
-    )
-    gathered = lax.all_gather(packed, AXES, axis=0, tiled=True)
-    sizes = (2 * width, 3 * width, width, width, width)
-    weights = []
-    offset = 0
-    for size in sizes:
-        weights.append(gathered[:, offset : offset + size])
-        offset = offset + size
-    w_keyval, w_self_in, w_self_out, w_query, w_cross_out = weights
-    gains = gathered[:, offset : offset + len(vectors)].astype(F32).T
-    w_up = lax.all_gather(feed_up, AXES, axis=0, tiled=True)
-    w_down = lax.all_gather(feed_down, AXES, axis=0, tiled=True)
-
-    stream = tokens[0].astype(F32)
+    up_shard = feed_up.reshape(rows, plan.count, parts, rows).swapaxes(1, 2).reshape(feed_up.shape)
+    down_shard = feed_down.reshape(parts, rows, width).swapaxes(0, 1).reshape(rows, parts * width)
+
+    keyval_halves = gather_halves(plan, cross_keyval)
+    project_halves = gather_halves(plan, jnp.concatenate([self_input, vector_pack], axis=1))
+    middle_halves = gather_halves(
+        plan, jnp.concatenate([self_output, cross_query, cross_output], axis=1)
+    )
+    feed_halves = gather_halves(plan, jnp.concatenate([up_shard, down_shard], axis=1))
+
+    rows_in = tokens[0]
     encoded = neighbours.reshape(pool_count * neigh_len, width)
     ids = neighbour_ids.reshape(-1)
-    pool_keyval = dot(encoded, w_keyval).astype(BF16).reshape(pool_count, neigh_len, 2 * width)
-    first_in = norm_apply(stream, gains[0], gains[1]).astype(BF16)
-    projected = dot(first_in, w_self_in).astype(BF16)
+    pool_keyval = pool_project(plan, encoded, keyval_halves)
+    pool_keyval = pool_keyval.reshape(pool_count, neigh_len, 2 * width)
+    first_in, projected, vector_rows = project(plan, rows_in, project_halves)
     self_mixed, self_exact, logsum = self_forward(projected, lengths)
-    after_self = stream + dot(self_mixed, w_self_out)
-    second_in = norm_apply(after_self, gains[2], gains[3]).astype(BF16)
-    cross_queries = dot(second_in, w_query).astype(BF16)
+    after_self, second_in, cross_queries = middle(
+        plan, (0, width), rows_in, self_mixed, vector_rows, middle_halves
+    )
     cross_mixed = cross_forward(cross_queries, pool_keyval, ids, neighbour_lengths)
-    after_cross = after_self + dot(cross_mixed, w_cross_out)
-    third_in = norm_apply(after_cross, gains[4], gains[5]).astype(BF16)
-    hidden_pre = dot(third_in, w_up)
-    hidden, gelu_back = jax.vjp(gelu_tanh, hidden_pre)
-    hidden = hidden.astype(BF16)
-    block_out = (after_cross + dot(hidden, w_down)).astype(BF16)
-
-    down_in = cotangent[0]
-    feeddown_term = dot(hidden, down_in, TN).astype(BF16)
-    hidden_grad = gelu_back(dot(down_in, w_down, NT))[0].astype(BF16)
-    feedup_term = dot(third_in, hidden_grad, TN).astype(BF16)
-    third_back = dot(hidden_grad, w_up, NT)
-    back, gain_three, shift_three = norm_back(after_cross, gains[4], third_back)
-    after_cross_grad = down_in.astype(F32) + back
-    cross_out_in = after_cross_grad.astype(BF16)
-    crossout_term = dot(cross_mixed, cross_out_in, TN)
-    mixed_grad = dot(cross_out_in, w_cross_out, NT).astype(BF16)
-    query_grad, pool_key_grad, pool_value_grad = cross_backward(
+    block_out, after_cross_grad, mixed_grad, third_terms, feed_keep, feed_send = feed(
+        plan,
+        2 * width,
+        after_self,
+        cross_mixed,
+        cotangent[0],
+        vector_rows,
+        feed_halves,
+        middle_halves,
+    )
+    feed_sum = scatter_halves(plan, feed_keep, feed_send)
+
+    query_grad, pool_keys, pool_values = cross_backward(
         cross_queries, mixed_grad, pool_keyval, ids, neighbour_lengths
     )
-    query_term = dot(second_in, query_grad, TN)
-    second_back = dot(query_grad, w_query, NT)
-    back, gain_two, shift_two = norm_back(after_self, gains[2], second_back)
-    after_self_grad = after_cross_grad + back
-    self_out_in = after_self_grad.astype(BF16)
-    selfout_term = dot(self_mixed, self_out_in, TN)
-    attend_grad = dot(self_out_in, w_self_out, NT).astype(BF16)
+    pool_keys = pool_keys.reshape(pool_count * neigh_len, width)
+    pool_values = pool_values.reshape(pool_count * neigh_len, width)
+    keyval_keep, keyval_send = keyval_terms(plan, encoded, pool_keys, pool_values)
+    after_self_grad, attend_grad, second_terms, second_keep, second_send = second_back(
+        plan,
+        (0, width),
+        after_self,
+        after_cross_grad,
+        query_grad,
+        second_in,
+        self_mixed,
+        vector_rows,
+        middle_halves,
+    )
+    middle_sum = scatter_halves(
+        plan,
+        jnp.concatenate([keyval_keep, second_keep], axis=1),
+        jnp.concatenate([keyval_send, second_send], axis=1),
+    )
     projected_grad = self_backward(projected, lengths, attend_grad, self_exact, logsum)
-    projected_grad = jnp.concatenate([projected_grad[i] for i in range(3)], axis=1)
-    selfin_term = dot(first_in, projected_grad, TN)
-    first_back = dot(projected_grad, w_self_in, NT)
-    back, gain_one, shift_one = norm_back(stream, gains[0], first_back)
-    tokens_grad = after_self_grad + back
-
-    pool_grad = jnp.concatenate([pool_key_grad, pool_value_grad], axis=-1)
-    pool_grad = pool_grad.reshape(pool_count * neigh_len, 2 * width)
-    keyval_term = dot(encoded, pool_grad, TN)
-    neighbours_grad = dot(pool_grad, w_keyval, NT).reshape(neighbours.shape)
-
-    vector_terms = jnp.stack([gain_one, shift_one, gain_two, shift_two, gain_three, shift_three], axis=1)
-    vector_terms = jnp.pad(vector_terms, ((0, 0), (0, LANES - len(vectors))))
-    packed_terms = jnp.concatenate(
-        [
-            term.astype(BF16)
-            for term in (keyval_term, selfin_term, selfout_term, query_term, crossout_term, vector_terms)
-        ],
-        axis=1,
-    )
-
-    def scatter(term):
-        return lax.psum_scatter(term, AXES, scatter_dimension=0, tiled=True).astype(F32)
-
-    feeddown_grad = scatter(feeddown_term)
-    feedup_grad = scatter(feedup_term)
-    summed = scatter(packed_terms)
-    pieces = []
-    offset = 0
-    for size in sizes:
-        pieces.append(summed[:, offset : offset + size])
-        offset = offset + size
-    vector_grads = [summed[:, offset + i] for i in range(len(vectors))]
+    tokens_grad, first_keep, first_send = first_back(
+        plan,
+        rows_in,
+        after_self_grad,
+        projected_grad,
+        first_in,
+        vector_rows,
+        second_terms,
+        third_terms,
+        project_halves,
+    )
+    first_sum = scatter_halves(plan, first_keep, first_send)
+    neighbours_grad = neighbours_back(plan, pool_keys, pool_values, keyval_halves)
+
+    down_grad = feed_sum[:, : parts * width].reshape(rows, parts, width).swapaxes(0, 1)
+    up_grad = feed_sum[:, parts * width : 2 * parts * width]
+    up_grad = up_grad.reshape(rows, parts, plan.count, rows).swapaxes(1, 2)
+    vector_grads = [first_sum[:, 3 * width + i] for i in range(len(vectors))]
     return (
         block_out[None],
         tokens_grad[None],
-        neighbours_grad,
+        neighbours_grad.reshape(neighbours.shape),
         vector_grads[0],
         vector_grads[1],
-        pieces[1],
-        pieces[2],
+        first_sum[:, : 3 * width],
+        middle_sum[:, 3 * width :],
         vector_grads[2],
         vector_grads[3],
-        pieces[3],
-        pieces[0],
-        pieces[4],
+        middle_sum[:, 2 * width : 3 * width],
+        middle_sum[:, : 2 * width],
+        feed_sum[:, 2 * parts * width :],
         vector_grads[4],
         vector_grads[5],
-        feedup_grad,
-        feeddown_grad,
+        up_grad.reshape(feed_up.shape),
+        down_grad.reshape(feed_down.shape),
     )
 
 

time: 648 us -> 592 us (0.914)
  matrix products: 163 us -> 0 us
  Pallas kernels: 114 us -> 277 us
  local copies, waits for them, and re-layouts: 84.8 us -> 27.4 us
  starting transfers between devices: 0.24 us -> 57.6 us
  waiting for transfers between devices: 232 us -> 181 us
  between operations: 15.6 us -> 2.71 us
  other arithmetic: 26.8 us -> 35.6 us
    ppermute x0 -> x35, waiting for transfers between devices: none -> 181 us  [exchange(): return lax.ppermute(values, AXES, pairs)]
    pallas_call x0 -> x12, Pallas kernels: none -> 163 us  [the longest x1 58.7 us: feed(): pl.pallas_call(functools.partial(feed_kernel, plan, out_start, steps), gr...]
    dot_general x21 -> x0, matrix products: 163 us -> none  [dot(): return lax.dot_general(left, right, dims, preferred_element_type=F32)]
    unnamed x7 -> x0, waiting for transfers between devices: 138 us -> none
    all_gather x3 -> x0, waiting for transfers between devices: 93.6 us -> none  [the longest x1 78.3 us: local(): gathered = lax.all_gather(packed, AXES, axis=0, tiled=True)]
    ppermute x0 -> x35, starting transfers between devices: none -> 57.6 us  [exchange(): return lax.ppermute(values, AXES, pairs)]
    convert_element_type x3 -> x12, other arithmetic: 4.29 us -> 29.3 us  [add(): return total.astype(BF16)]
    convert_element_type x2 -> x0, local copies, waits for them, and re-layouts: 21.1 us -> none  [the longest x1 16.7 us: local(): dot(encoded, w_keyval).astype(BF16)]
  transfers between devices with their start and end apart: 6 -> 35, of which waited for: 3 -> 18; matrix products, arithmetic and copies ran while one was open for 39% -> 7% of each run, Pallas kernels for 18% -> 38%
where the time goes in v2:
time: 592 us; the launch traced here: 582 us
  Pallas kernels  277 us (47%)
  waiting for transfers between devices  181 us (31%)
  starting transfers between devices  57.6 us (10%)
  other arithmetic  35.6 us (6%)
  local copies, waits for them, and re-layouts  27.4 us (5%)
    ppermute x35, waiting for transfers between devices, exchange(): return lax.ppermute(values, AXES, pairs)  181 us
    pallas_call x1, Pallas kernels, feed(): pl.pallas_call(functools.partial(feed_kernel, plan, out_start, steps), gr...  58.7 us
    ppermute x35, starting transfers between devices, exchange(): return lax.ppermute(values, AXES, pairs)  57.6 us
    pallas_call x1, Pallas kernels, cross_backward(): pl.pallas_call(cross_backward_kernel, grid_spec=pltpu.PrefetchScalarGridS...  48.5 us
    convert_element_type x12, other arithmetic, add(): return total.astype(BF16)  29.3 us
    pallas_call x1, Pallas kernels, self_backward(): pl.pallas_call(self_backward_kernel, grid=(pairs,), in_specs=[pl.BlockSpe...  25.4 us
    pallas_call x1, Pallas kernels, self_forward(): pl.pallas_call(self_forward_kernel, grid=(pairs,), in_specs=[pl.BlockSpec...  21.9 us
    pallas_call x1, Pallas kernels, first_back(): pl.pallas_call(functools.partial(first_kernel, plan, steps), grid=(steps,...  18.6 us
  transfers between devices with their start and end apart: 35, of which 18 were waited for; matrix products, arithmetic and copies ran while one was open for 7% of the time, Pallas kernels for 38%

profile of v2, /device:TPU:0, one launch (start us, length us, event | category | flops | bytes accessed | tf_op | source)
XLA Modules:
  0.0 581.5 jit_solution(7342153402347527734)
XLA Ops:
  0.7 2.2 reshape.216
  4.5 3.1 collective-permute-start.15
  7.7 2.0 collective-permute-start.5
  10.1 6.9 %collective-permute-done.10 = bf16[24,1536]{1,0:T(8,128)(2,1)S(1)} collective-permute-done((bf16[24,1536]{1,0:T(8,128)(2,1)S(1)}, bf16[24,1536]{1,0:T(8,128)(2,1)S(1)}, u32[]{:S(2)}, u32[]{:S(2)}) %collective-permute-start.10) | collective-permute-done | bytes 73760 | tf_op jit(solution)/shard_map/ppermute | solution.py:443
  17.1 3.1 collective-permute-start.11
  21.0 2.0 collective-permute-start.6
  25.2 2.6 collective-permute-start.1
  27.8 22.6 %collective-permute-done.11 = bf16[2,24,1536]{2,1,0:T(8,128)(2,1)S(1)} collective-permute-done((bf16[2,24,1536]{2,1,0:T(8,128)(2,1)S(1)}, bf16[2,24,1536]{2,1,0:T(8,128)(2,1)S(1)}, u32[]{:S(2)}, u32[]{:S(2)}) %collective-permute-start.11) | collective-permute-done | bytes 147488 | tf_op jit(solution)/shard_map/ppermute | solution.py:443
  50.5 17.4 %collective-permute-done.16 = bf16[2,24,6144]{2,1,0:T(8,128)(2,1)S(1)} collective-permute-done((bf16[2,24,6144]{2,1,0:T(8,128)(2,1)S(1)}, bf16[2,24,6144]{2,1,0:T(8,128)(2,1)S(1)}, u32[]{:S(2)}, u32[]{:S(2)}) %collective-permute-start.16) | collective-permute-done | bytes 589856 | tf_op jit(solution)/shard_map/ppermute | solution.py:443
  68.0 1.9 collective-permute-start.17
  70.3 1.9 collective-permute-start.7
  72.2 13.6 %collective-permute-done.17 = bf16[2,2,24,6144]{3,2,1,0:T(8,128)(2,1)S(1)} collective-permute-done((bf16[2,2,24,6144]{3,2,1,0:T(8,128)(2,1)S(1)}, bf16[2,2,24,6144]{3,2,1,0:T(8,128)(2,1)S(1)}, u32[]{:S(2)}, u32[]{:S(2)}) %collective-permute-start.17) | collective-permute-done | bytes 1179680 | tf_op jit(solution)/shard_map/ppermute | solution.py:443
  86.1 2.5 collective-permute-start.18
  90.4 1.7 collective-permute-done.12
  92.2 2.5 collective-permute-start.13
  94.7 6.8 %collective-permute-done.7 = bf16[2,2,24,2304]{3,2,1,0:T(8,128)(2,1)S(1)} collective-permute-done((bf16[2,2,24,2304]{3,2,1,0:T(8,128)(2,1)S(1)}, bf16[2,2,24,2304]{3,2,1,0:T(8,128)(2,1)S(1)}, u32[]{:S(2)}, u32[]{:S(2)}) %collective-permute-start.7) | collective-permute-done | bytes 442400 | tf_op jit(solution)/shard_map/ppermute | solution.py:443
  101.7 2.5 collective-permute-start.8
  104.2 13.6 %collective-permute-done.18 = bf16[2,2,2,24,6144]{4,3,2,1,0:T(8,128)(2,1)S(1)} collective-permute-done((bf16[2,2,2,24,6144]{4,3,2,1,0:T(8,128)(2,1)S(1)}, bf16[2,2,2,24,6144]{4,3,2,1,0:T(8,128)(2,1)S(1)}, u32[]{:S(2)}, u32[]{:S(2)}) %collective-permute-start.18) | collective-permute-done | bytes 2359328 | tf_op jit(solution)/shard_map/ppermute | solution.py:443
  118.6 3.2 reorder_blocks.7
  121.9 4.8 collective-permute-start.19
  126.9 1.8 collective-permute-start.3
  128.7 5.0 collective-permute-done.8
  134.0 2.8 reorder_blocks.5
  136.8 4.8 collective-permute-start.9
  141.6 2.1 collective-permute-done.3
  144.1 3.8 reorder_blocks.4
  147.9 4.5 collective-permute-start.4
  152.6 2.9 reorder_blocks.6
  156.5 2.3 collective-permute-done.14
  158.8 2.8 copy-done.2
  161.6 14.2 %pool_project.1 = bf16[4096,1536]{1,0:T(8,128)(2,1)} custom-call(s32[1]{0:T(128)} %bitcast.odd_ref, bf16[4096,768]{1,0:T(8,128)(2,1)S(1)} %bitcast.306, bf16[384,1536]{1,0:T(8,128)(2,1)} %bitcast.40.held_ref, bf16[384,1536]{1,0:T(8,128)(2,1)} %bitcast.41.other_ref), custom_call_target="tpu_custom_call" | custom-call | tf_op jit(solution)/shard_map/pool_project/pallas_call | solution.py:647
  175.8 7.4 %project.1 = (bf16[1024,768]{1,0:T(8,128)(2,1)S(1)}, bf16[1024,2304]{1,0:T(8,128)(2,1)S(1)}, f32[8,768]{1,0:T(8,128)S(1)}) custom-call(s32[1]{0:T(128)} %bitcast.odd_ref, bf16[1024,768]{1,0:T(8,128)(2,1)S(1)} %bitcast.314, bf16[384,2432]{1,0:T(8,128)(2,1)} %bitcast.17.held_ref, bf16[384,2432]{1,0:T(8,128)(2,1)} %bitcast.18.other_ref), custom_call_target="tpu_custom_call" | custom-call | tf_op jit(solution)/shard_map/project/pallas_call | solution.py:692
  183.2 2.2 copy-done
  186.6 21.9 %self_forward.1 = (bf16[1024,768]{1,0:T(8,128)(2,1)S(1)}, f32[1024,768]{1,0:T(8,128)S(1)}, f32[6,8,1024]{2,1,0:T(8,128)S(1)}) custom-call(s32[1]{0:T(128)S(6)} %copy.55.length_ref, bf16[1024,2304]{1,0:T(8,128)(2,1)} %copy-done, bf16[1024,2304]{1,0:T(8,128)(2,1)} %copy-done, bf16[1024,2304]{1,0:T(8,128)(2,1)} %copy-done), custom_call_target="tpu_custom_call" | custom-call | tf_op jit(solution)/shard_map/self_forward/pallas_call | solution.py:96
  208.5 1.7 copy-done.10
  210.2 5.6 middle.1
  217.1 17.7 %cross_forward.1.mixed_ref = bf16[1024,768]{1,0:T(8,128)(2,1)S(1)} custom-call(s32[32]{0:T(128)S(1)} %reshape.210.ids_ref, s32[32]{0:T(128)S(1)} %copy-done.21, bf16[1024,768]{1,0:T(8,128)(2,1)S(1)} %get-tuple-element.48.query_ref, bf16[32,128,1536]{2,1,0:T(8,128)(2,1)} %bitcast.319, bf16[32,128,1536]{2,1,0:T(8,128)(2,1)} %bitcast.320), custom_call_target="tpu_custom_call" | custom-call | tf_op jit(solution)/shard_map/cross_forward/pallas_call | solution.py:299
  236.0 58.7 %feed_forward.1 = (bf16[1024,768]{1,0:T(8,128)(2,1)}, f32[1024,768]{1,0:T(8,128)}, bf16[1024,768]{1,0:T(8,128)(2,1)}, f32[8,768]{1,0:T(8,128)}, bf16[384,6912]{1,0:T(8,128)(2,1)}, /*index=5*/bf16[384,6912]{1,0:T(8,128)(2,1)}) custom-call(s32[1]{0:T(128)} %bitcast.odd_ref, f32[1024,768]{1,0:T(8,128)} %copy-done.6, bf16[1024,768]{1,0:T(8,128)(2,1)} %copy-done.8, ...), custom_call_target="tpu_custom_call" | custom-call | tf_op jit(solution)/shard_map/feed_forward/pallas_call | solution.py:912
  294.9 48.5 %cross_backward.1 = (bf16[1024,768]{1,0:T(8,128)(2,1)}, bf16[32,128,768]{2,1,0:T(8,128)(2,1)}, bf16[32,128,768]{2,1,0:T(8,128)(2,1)}) custom-call(s32[32]{0:T(128)} %copy-done.20, s32[32]{0:T(128)} %neighbour_lengths_ref.3, bf16[1024,768]{1,0:T(8,128)(2,1)} %copy-done.7, bf16[1024,768]{1,0:T(8,128)(2,1)} %get-tuple-element.51.grad_ref, ...), custom_call_target="tpu_custom_call" | custom-call | tf_op jit(solution)/shard_map/cross_backward/pallas_call | solution.py:375
  343.4 15.4 %keyval_terms.1 = (bf16[384,1536]{1,0:T(8,128)(2,1)S(1)}, bf16[384,1536]{1,0:T(8,128)(2,1)S(1)}) custom-call(s32[1]{0:T(128)} %bitcast.odd_ref, bf16[4096,768]{1,0:T(8,128)(2,1)} %bitcast.305, bf16[4096,768]{1,0:T(8,128)(2,1)} %bitcast.307, bf16[4096,768]{1,0:T(8,128)(2,1)} %bitcast.325), custom_call_target="tpu_custom_call" | custom-call | tf_op jit(solution)/shard_map/keyval_terms/pallas_call | solution.py:1173
  358.9 14.0 %second_back.1 = (f32[1024,768]{1,0:T(8,128)}, bf16[1024,768]{1,0:T(8,128)(2,1)S(1)}, f32[8,768]{1,0:T(8,128)S(1)}, bf16[384,1536]{1,0:T(8,128)(2,1)S(1)}, bf16[384,1536]{1,0:T(8,128)(2,1)S(1)}) custom-call(s32[1]{0:T(128)} %bitcast.odd_ref, f32[1024,768]{1,0:T(8,128)} %copy-done.6, f32[1024,768]{1,0:T(8,128)} %get-tuple-element.50.grad_in_ref, ...), custom_call_target="tpu_custom_call" | custom-call | tf_op jit(solution)/shard_map/second_back/pallas_call | solution.py:1004
  373.5 1.7 pad_maximum_fusion.3
  376.2 25.4 %self_backward.1.projected_grad_ref = bf16[3,1024,768]{2,1,0:T(8,128)(2,1)} custom-call(s32[1]{0:T(128)S(6)} %copy.55.length_ref, bf16[1024,2304]{1,0:T(8,128)(2,1)} %copy-done, bf16[1024,2304]{1,0:T(8,128)(2,1)} %copy-done, bf16[1024,2304]{1,0:T(8,128)(2,1)} %copy-done, bf16[1024,768]{1,0:T(8,128)(2,1)S(1)} %get-tuple-element.55.grad_ref, ...), custom_call_target="tpu_custom_call" | custom-call | tf_op jit(solution)/shard_map/self_backward/pallas_call | solution.py:225
  401.7 18.6 %first_back.1 = (f32[1024,768]{1,0:T(8,128)}, bf16[384,2432]{1,0:T(8,128)(2,1)}, bf16[384,2432]{1,0:T(8,128)(2,1)}) custom-call(s32[1]{0:T(128)} %bitcast.odd_ref, bf16[1024,768]{1,0:T(8,128)(2,1)} %bitcast.313, f32[1024,768]{1,0:T(8,128)} %get-tuple-element.54.grad_in_ref, bf16[3,1024,768]{2,1,0:T(8,128)(2,1)} %self_backward.1.projected_grad_ref, ...), custom_call_target="tpu_custom_call" | custom-call | tf_op jit(solution)/shard_map/first_back/pallas_call | solution.py:1102
  420.8 11.2 %add_convert_fusion.1 = (bf16[2,2,2,24,6912]{4,3,2,1,0:T(8,128)(2,1)}, bf16[2,2,2,24,6912]{4,3,2,1,0:T(8,128)(2,1)}) fusion(bf16[2,2,2,2,24,6912]{5,4,3,2,1,0:T(8,128)(2,1)} %bitcast.112, s32[]{:T(128)S(6)} %select_n.700, bf16[2,2,2,2,24,6912]{5,4,3,2,1,0:T(8,128)(2,1)} %bitcast.328, pred[]{:T(512)S(6)} %eq.68, s32[]{:T(128)S(6)} %select_n.705), kind=kLoop, calls=%fused_computation.1 | loop fusion | flops 15925248 | bytes 26542088 | tf_op jit(solution)/shard_map/convert_element_type | solution.py:512
  433.6 1.9 add_convert_fusion.7
  436.3 4.1 add_convert_fusion.5
  440.4 1.6 collective-permute-start.26
  442.0 32.4 %collective-permute-done.21 = bf16[2,2,2,24,2432]{4,3,2,1,0:T(8,128)(2,1)} collective-permute-done((bf16[2,2,2,24,2432]{4,3,2,1,0:T(8,128)(2,1)}, bf16[2,2,2,24,2432]{4,3,2,1,0:T(8,128)(2,1)}, u32[]{:S(2)}, u32[]{:S(2)}) %collective-permute-start.21) | collective-permute-done | bytes 933920 | tf_op jit(solution)/shard_map/ppermute | solution.py:443
  474.4 2.1 add_convert_fusion.13
  476.5 1.8 collective-permute-start.22
  478.3 5.0 add_convert_fusion.3
  483.6 11.8 %collective-permute-done.26 = bf16[2,2,2,24,3072]{4,3,2,1,0:T(8,128)(2,1)S(1)} collective-permute-done((bf16[2,2,2,24,3072]{4,3,2,1,0:T(8,128)(2,1)S(1)}, bf16[2,2,2,24,3072]{4,3,2,1,0:T(8,128)(2,1)S(1)}, u32[]{:S(2)}, u32[]{:S(2)}) %collective-permute-start.26) | collective-permute-done | bytes 1179680 | tf_op jit(solution)/shard_map/ppermute | solution.py:443
  495.4 1.6 add_convert_fusion.11
  497.0 1.8 collective-permute-start.27
  499.6 2.8 copy-done.3
  502.4 16.6 %neighbours_back.1 = f32[4096,768]{1,0:T(8,128)} custom-call(s32[1]{0:T(128)} %bitcast.odd_ref, bf16[4096,768]{1,0:T(8,128)(2,1)S(1)} %bitcast.308, bf16[4096,768]{1,0:T(8,128)(2,1)} %bitcast.326, bf16[384,1536]{1,0:T(8,128)(2,1)} %bitcast.40.held_ref, bf16[384,1536]{1,0:T(8,128)(2,1)} %bitcast.41.other_ref), custom_call_target="tpu_custom_call" | custom-call | tf_op jit(solution)/shard_map/neighbours_back/pallas_call | solution.py:1205
  520.0 3.2 collective-permute-start.24
  524.8 3.0 collective-permute-start.33
  530.2 21.2 %collective-permute-done.28 = bf16[2,24,3072]{2,1,0:T(8,128)(2,1)S(1)} collective-permute-done((bf16[2,24,3072]{2,1,0:T(8,128)(2,1)S(1)}, bf16[2,24,3072]{2,1,0:T(8,128)(2,1)S(1)}, u32[]{:S(2)}, u32[]{:S(2)}) %collective-permute-start.28) | collective-permute-done | bytes 294944 | tf_op jit(solution)/shard_map/ppermute | solution.py:443
  551.5 12.8 %collective-permute-done.33 = bf16[2,24,6912]{2,1,0:T(8,128)(2,1)S(1)} collective-permute-done((bf16[2,24,6912]{2,1,0:T(8,128)(2,1)S(1)}, bf16[2,24,6912]{2,1,0:T(8,128)(2,1)S(1)}, u32[]{:S(2)}, u32[]{:S(2)}) %collective-permute-start.33) | collective-permute-done | bytes 663584 | tf_op jit(solution)/shard_map/ppermute | solution.py:443
  564.5 3.0 collective-permute-done.29
  568.9 5.6 collective-permute-done.34
  577.7 2.6 reshape.233
  (170 shorter events, 29.8 us)
Async XLA Ops:
  0.6 3.7 copy-start.25
  2.8 4.8 copy-start.26
  2.8 4.9 copy-start.27
  2.8 4.9 copy-start.28
  2.9 4.9 copy-start.29
  2.9 6.9 %copy-start.31 = (bf16[24]{0:T(256)(128)(2,1)S(1)}, bf16[24]{0:T(256)(128)(2,1)}, u32[]{:S(2)}) copy-start(bf16[24]{0:T(256)(128)(2,1)} %param.24) | copy-start | bytes 148
  2.9 6.9 %copy-start.32 = (bf16[24]{0:T(256)(128)(2,1)S(1)}, bf16[24]{0:T(256)(128)(2,1)}, u32[]{:S(2)}) copy-start(bf16[24]{0:T(256)(128)(2,1)} %param.25) | copy-start | bytes 148
  2.9 6.9 %copy-start.33 = (bf16[24]{0:T(256)(128)(2,1)S(1)}, bf16[24]{0:T(256)(128)(2,1)}, u32[]{:S(2)}) copy-start(bf16[24]{0:T(256)(128)(2,1)} %param.28) | copy-start | bytes 148
  2.9 6.9 %copy-start.34 = (bf16[24]{0:T(256)(128)(2,1)S(1)}, bf16[24]{0:T(256)(128)(2,1)}, u32[]{:S(2)}) copy-start(bf16[24]{0:T(256)(128)(2,1)} %param.29) | copy-start | bytes 148
  2.9 6.8 %copy-start.35 = (bf16[24]{0:T(256)(128)(2,1)S(1)}, bf16[24]{0:T(256)(128)(2,1)}, u32[]{:S(2)}) copy-start(bf16[24]{0:T(256)(128)(2,1)} %param.33) | copy-start | bytes 148
  2.9 6.8 %copy-start.36 = (bf16[24]{0:T(256)(128)(2,1)S(1)}, bf16[24]{0:T(256)(128)(2,1)}, u32[]{:S(2)}) copy-start(bf16[24]{0:T(256)(128)(2,1)} %param.34) | copy-start | bytes 148
  2.9 7.0 %copy-start.24 = (bf16[24,2304]{1,0:T(8,128)(2,1)S(1)}, bf16[24,2304]{1,0:T(8,128)(2,1)}, u32[]{:S(2)}) copy-start(bf16[24,2304]{1,0:T(8,128)(2,1)} %param.26) | copy-start | bytes 331780
  4.5 20.1 %collective-permute-start.15 = (bf16[24,6144]{1,0:T(8,128)(2,1)S(1)}, bf16[24,6144]{1,0:T(8,128)(2,1)S(1)}, u32[]{:S(2)}, u32[]{:S(2)}) collective-permute-start(bf16[24,6144]{1,0:T(8,128)(2,1)S(1)} %constant_dynamic-update-slice_fusion.3), channel_id=1, source_target_pairs={{0,2},{1,3},{2,0},{3,1},{4,6},{5,7},{6,4},{7,5},{8,10},{9,11},{10,... | collective-permute-start | bytes 884744 | tf_op jit(solution)/shard_map/ppermute | solution.py:443
  7.6 9.4 %collective-permute-start.10 = (bf16[24,1536]{1,0:T(8,128)(2,1)S(1)}, bf16[24,1536]{1,0:T(8,128)(2,1)S(1)}, u32[]{:S(2)}, u32[]{:S(2)}) collective-permute-start(bf16[24,1536]{1,0:T(8,128)(2,1)S(1)} %copy-done.26), channel_id=1, source_target_pairs={{0,2},{1,3},{2,0},{3,1},{4,6},{5,7},{6,4},{7,5},{8,10},{9,11},{10,... | collective-permute-start | bytes 221192 | tf_op jit(solution)/shard_map/ppermute | solution.py:443
  7.7 13.2 %collective-permute-start.5 = (bf16[24,2304]{1,0:T(8,128)(2,1)S(1)}, bf16[24,2304]{1,0:T(8,128)(2,1)S(1)}, u32[]{:S(2)}, u32[]{:S(2)}) collective-permute-start(bf16[24,2304]{1,0:T(8,128)(2,1)S(1)} %constant_dynamic-update-slice_fusion), channel_id=1, source_target_pairs={{0,2},{1,3},{2,0},{3,1},{4,6},{5,7},{6,4},{7,5},{8,10},{9,11},{10,... | collective-permute-start | bytes 331784 | tf_op jit(solution)/shard_map/ppermute | solution.py:443
  9.9 14.6 %collective-permute-start = (bf16[24,2432]{1,0:T(8,128)(2,1)S(1)}, bf16[24,2432]{1,0:T(8,128)(2,1)S(1)}, u32[]{:S(2)}, u32[]{:S(2)}) collective-permute-start(bf16[24,2432]{1,0:T(8,128)(2,1)S(1)} %fusion.14), channel_id=1, source_target_pairs={{0,2},{1,3},{2,0},{3,1},{4,6},{5,7},{6,4},{7,5},{8,10},{9,11},{10,... | collective-permute-start | bytes 350216 | tf_op jit(solution)/shard_map/ppermute | solution.py:443
  17.1 33.4 %collective-permute-start.11 = (bf16[2,24,1536]{2,1,0:T(8,128)(2,1)S(1)}, bf16[2,24,1536]{2,1,0:T(8,128)(2,1)S(1)}, u32[]{:S(2)}, u32[]{:S(2)}) collective-permute-start(bf16[2,24,1536]{2,1,0:T(8,128)(2,1)S(1)} %pad_maximum_fusion.17), channel_id=1, source_target_pairs={{0,4},{1,5},{2,6},{3,7},{4,0},{5,1},{6,2},{7,3},{8,12},{9,13},{10,... | collective-permute-start | bytes 442376 | tf_op jit(solution)/shard_map/ppermute | solution.py:443
  21.0 49.2 %collective-permute-start.6 = (bf16[2,24,2304]{2,1,0:T(8,128)(2,1)S(1)}, bf16[2,24,2304]{2,1,0:T(8,128)(2,1)S(1)}, u32[]{:S(2)}, u32[]{:S(2)}) collective-permute-start(bf16[2,24,2304]{2,1,0:T(8,128)(2,1)S(1)} %pad_maximum_fusion.16), channel_id=1, source_target_pairs={{0,4},{1,5},{2,6},{3,7},{4,0},{5,1},{6,2},{7,3},{8,12},{9,13},{10,... | collective-permute-start | bytes 663560 | tf_op jit(solution)/shard_map/ppermute | solution.py:443
  24.7 43.1 %collective-permute-start.16 = (bf16[2,24,6144]{2,1,0:T(8,128)(2,1)S(1)}, bf16[2,24,6144]{2,1,0:T(8,128)(2,1)S(1)}, u32[]{:S(2)}, u32[]{:S(2)}) collective-permute-start(bf16[2,24,6144]{2,1,0:T(8,128)(2,1)S(1)} %pad_maximum_fusion.11), channel_id=1, source_target_pairs={{0,4},{1,5},{2,6},{3,7},{4,0},{5,1},{6,2},{7,3},{8,12},{9,13},{10,... | collective-permute-start | bytes 1769480 | tf_op jit(solution)/shard_map/ppermute | solution.py:443
  25.2 63.4 %collective-permute-start.1 = (bf16[2,24,2432]{2,1,0:T(8,128)(2,1)S(1)}, bf16[2,24,2432]{2,1,0:T(8,128)(2,1)S(1)}, u32[]{:S(2)}, u32[]{:S(2)}) collective-permute-start(bf16[2,24,2432]{2,1,0:T(8,128)(2,1)S(1)} %pad_maximum_fusion.15), channel_id=1, source_target_pairs={{0,4},{1,5},{2,6},{3,7},{4,0},{5,1},{6,2},{7,3},{8,12},{9,13},{10,... | collective-permute-start | bytes 700424 | tf_op jit(solution)/shard_map/ppermute | solution.py:443
  68.0 17.7 %collective-permute-start.17 = (bf16[2,2,24,6144]{3,2,1,0:T(8,128)(2,1)S(1)}, bf16[2,2,24,6144]{3,2,1,0:T(8,128)(2,1)S(1)}, u32[]{:S(2)}, u32[]{:S(2)}) collective-permute-start(bf16[2,2,24,6144]{3,2,1,0:T(8,128)(2,1)S(1)} %pad_maximum_fusion.7), channel_id=1, source_target_pairs={{0,1},{1,0},{2,3},{3,2},{4,5},{5,4},{6,7},{7,6},{8,24},{9,25},{10,... | collective-permute-start | bytes 3538952 | tf_op jit(solution)/shard_map/ppermute | solution.py:443
  69.9 22.1 %collective-permute-start.12 = (bf16[2,2,24,1536]{3,2,1,0:T(8,128)(2,1)S(1)}, bf16[2,2,24,1536]{3,2,1,0:T(8,128)(2,1)S(1)}, u32[]{:S(2)}, u32[]{:S(2)}) collective-permute-start(bf16[2,2,24,1536]{3,2,1,0:T(8,128)(2,1)S(1)} %pad_maximum_fusion.14), channel_id=1, source_target_pairs={{0,1},{1,0},{2,3},{3,2},{4,5},{5,4},{6,7},{7,6},{8,24},{9,25},{10,... | collective-permute-start | bytes 884744 | tf_op jit(solution)/shard_map/ppermute | solution.py:443
  70.3 31.2 %collective-permute-start.7 = (bf16[2,2,24,2304]{3,2,1,0:T(8,128)(2,1)S(1)}, bf16[2,2,24,2304]{3,2,1,0:T(8,128)(2,1)S(1)}, u32[]{:S(2)}, u32[]{:S(2)}) collective-permute-start(bf16[2,2,24,2304]{3,2,1,0:T(8,128)(2,1)S(1)} %pad_maximum_fusion.13), channel_id=1, source_target_pairs={{0,1},{1,0},{2,3},{3,2},{4,5},{5,4},{6,7},{7,6},{8,24},{9,25},{10,... | collective-permute-start | bytes 1327112 | tf_op jit(solution)/shard_map/ppermute | solution.py:443
  86.1 31.7 %collective-permute-start.18 = (bf16[2,2,2,24,6144]{4,3,2,1,0:T(8,128)(2,1)S(1)}, bf16[2,2,2,24,6144]{4,3,2,1,0:T(8,128)(2,1)S(1)}, u32[]{:S(2)}, u32[]{:S(2)}) collective-permute-start(bf16[2,2,2,24,6144]{4,3,2,1,0:T(8,128)(2,1)S(1)} %pad_maximum_fusion.1), channel_id=1, source_target_pairs={{0,16},{1,17},{2,18},{3,19},{4,20},{5,21},{6,22},{7,23},{8,9},{9,8... | collective-permute-start | bytes 7077896 | tf_op jit(solution)/shard_map/ppermute | solution.py:443
  88.8 37.9 %collective-permute-start.2 = (bf16[2,2,24,2432]{3,2,1,0:T(8,128)(2,1)S(1)}, bf16[2,2,24,2432]{3,2,1,0:T(8,128)(2,1)S(1)}, u32[]{:S(2)}, u32[]{:S(2)}) collective-permute-start(bf16[2,2,24,2432]{3,2,1,0:T(8,128)(2,1)S(1)} %pad_maximum_fusion.12), channel_id=1, source_target_pairs={{0,1},{1,0},{2,3},{3,2},{4,5},{5,4},{6,7},{7,6},{8,24},{9,25},{10,... | collective-permute-start | bytes 1400840 | tf_op jit(solution)/shard_map/ppermute | solution.py:443
  92.2 60.2 %collective-permute-start.13 = (bf16[2,2,2,24,1536]{4,3,2,1,0:T(8,128)(2,1)S(1)}, bf16[2,2,2,24,1536]{4,3,2,1,0:T(8,128)(2,1)S(1)}, u32[]{:S(2)}, u32[]{:S(2)}) collective-permute-start(bf16[2,2,2,24,1536]{4,3,2,1,0:T(8,128)(2,1)S(1)} %pad_maximum_fusion.10), channel_id=1, source_target_pairs={{0,16},{1,17},{2,18},{3,19},{4,20},{5,21},{6,22},{7,23},{8,9},{9,8... | collective-permute-start | bytes 1769480 | tf_op jit(solution)/shard_map/ppermute | solution.py:443
  101.7 32.0 %collective-permute-start.8 = (bf16[2,2,2,24,2304]{4,3,2,1,0:T(8,128)(2,1)S(1)}, bf16[2,2,2,24,2304]{4,3,2,1,0:T(8,128)(2,1)S(1)}, u32[]{:S(2)}, u32[]{:S(2)}) collective-permute-start(bf16[2,2,2,24,2304]{4,3,2,1,0:T(8,128)(2,1)S(1)} %pad_maximum_fusion.9), channel_id=1, source_target_pairs={{0,16},{1,17},{2,18},{3,19},{4,20},{5,21},{6,22},{7,23},{8,9},{9,8... | collective-permute-start | bytes 2654216 | tf_op jit(solution)/shard_map/ppermute | solution.py:443
  121.9 114.2 %collective-permute-start.19 = (bf16[16,24,6144]{2,1,0:T(8,128)(2,1)}, bf16[16,24,6144]{2,1,0:T(8,128)(2,1)}, u32[]{:S(2)}, u32[]{:S(2)}) collective-permute-start(bf16[16,24,6144]{2,1,0:T(8,128)(2,1)} %reorder_blocks.7), channel_id=1, source_target_pairs={{0,8},{1,9},{2,10},{3,11},{4,12},{5,13},{6,14},{7,15},{8,0},{9,1},... | collective-permute-start | bytes 14155784 | tf_op jit(solution)/shard_map/ppermute | solution.py:443
  126.9 16.8 %collective-permute-start.3 = (bf16[2,2,2,24,2432]{4,3,2,1,0:T(8,128)(2,1)S(1)}, bf16[2,2,2,24,2432]{4,3,2,1,0:T(8,128)(2,1)S(1)}, u32[]{:S(2)}, u32[]{:S(2)}) collective-permute-start(bf16[2,2,2,24,2432]{4,3,2,1,0:T(8,128)(2,1)S(1)} %pad_maximum_fusion.8), channel_id=1, source_target_pairs={{0,16},{1,17},{2,18},{3,19},{4,20},{5,21},{6,22},{7,23},{8,9},{9,8... | collective-permute-start | bytes 2801672 | tf_op jit(solution)/shard_map/ppermute | solution.py:443
  136.8 73.4 %copy-start.1 = (bf16[16,24,2304]{2,1,0:T(8,128)(2,1)}, bf16[16,24,2304]{2,1,0:T(8,128)(2,1)S(1)}, u32[]{:S(2)}) copy-start(bf16[16,24,2304]{2,1,0:T(8,128)(2,1)S(1)} %reorder_blocks.5) | copy-start | bytes 5308420
  136.8 73.3 %collective-permute-start.9 = (bf16[16,24,2304]{2,1,0:T(8,128)(2,1)S(1)}, bf16[16,24,2304]{2,1,0:T(8,128)(2,1)S(1)}, u32[]{:S(2)}, u32[]{:S(2)}) collective-permute-start(bf16[16,24,2304]{2,1,0:T(8,128)(2,1)S(1)} %reorder_blocks.5), channel_id=1, source_target_pairs={{0,8},{1,9},{2,10},{3,11},{4,12},{5,13},{6,14},{7,15},{8,0},{9,1},... | collective-permute-start | bytes 5308424 | tf_op jit(solution)/shard_map/ppermute | solution.py:443
  147.9 27.9 %collective-permute-start.4 = (bf16[16,24,2432]{2,1,0:T(8,128)(2,1)}, bf16[16,24,2432]{2,1,0:T(8,128)(2,1)}, u32[]{:S(2)}, u32[]{:S(2)}) collective-permute-start(bf16[16,24,2432]{2,1,0:T(8,128)(2,1)} %reorder_blocks.4), channel_id=1, source_target_pairs={{0,8},{1,9},{2,10},{3,11},{4,12},{5,13},{6,14},{7,15},{8,0},{9,1},... | collective-permute-start | bytes 5603336 | tf_op jit(solution)/shard_map/ppermute | solution.py:443
  152.5 3.8 copy-start.30
  155.5 3.3 collective-permute-start.14
  156.5 60.6 %copy-start.20 = (s32[32]{0:T(128)}, s32[32]{0:T(128)S(1)}, u32[]{:S(2)}) copy-start(s32[32]{0:T(128)S(1)} %reshape.210.ids_ref) | copy-start | bytes 388
  158.8 2.8 copy-start.2
  161.6 14.2 %copy-start.5 = (bf16[1,1024,768]{2,1,0:T(8,128)(2,1)S(1)}, bf16[1,1024,768]{2,1,0:T(8,128)(2,1)}, u32[]{:S(2)}) copy-start(bf16[1,1024,768]{2,1,0:T(8,128)(2,1)} %param.19) | copy-start | bytes 4718596
  186.6 23.6 %copy-start.15 = (f32[8,768]{1,0:T(8,128)}, f32[8,768]{1,0:T(8,128)S(1)}, u32[]{:S(2)}) copy-start(f32[8,768]{1,0:T(8,128)S(1)} %get-tuple-element.46.vectors_ref) | copy-start | bytes 73732
  210.2 5.7 copy-start.9
  210.2 5.7 copy-start.17
  210.2 5.7 copy-start.4
  210.2 6.9 %copy-start.21 = (s32[32]{0:T(128)S(1)}, s32[32]{0:T(128)}, u32[]{:S(2)}) copy-start(s32[32]{0:T(128)} %neighbour_lengths_ref.3) | copy-start | bytes 388
  217.1 17.8 %copy-start.6 = (f32[1024,768]{1,0:T(8,128)}, f32[1024,768]{1,0:T(8,128)S(1)}, u32[]{:S(2)}) copy-start(f32[1024,768]{1,0:T(8,128)S(1)} %get-tuple-element.47.after_ref) | copy-start | bytes 9437188
  217.1 17.8 %copy-start.7 = (bf16[1024,768]{1,0:T(8,128)(2,1)}, bf16[1024,768]{1,0:T(8,128)(2,1)S(1)}, u32[]{:S(2)}) copy-start(bf16[1024,768]{1,0:T(8,128)(2,1)S(1)} %get-tuple-element.48.query_ref) | copy-start | bytes 4718596
  294.7 126.1 %collective-permute-start.30 = (bf16[384,6912]{1,0:T(8,128)(2,1)}, bf16[384,6912]{1,0:T(8,128)(2,1)}, u32[]{:S(2)}, u32[]{:S(2)}) collective-permute-start(bf16[384,6912]{1,0:T(8,128)(2,1)} %get-tuple-element.71), channel_id=1, source_target_pairs={{0,8},{1,9},{2,10},{3,11},{4,12},{5,13},{6,14},{7,15},{8,0},{9,1},... | collective-permute-start | bytes 15925256 | tf_op jit(solution)/shard_map/ppermute | solution.py:443
  343.4 15.5 %copy-start.13 = (bf16[1024,768]{1,0:T(8,128)(2,1)S(1)}, bf16[1024,768]{1,0:T(8,128)(2,1)}, u32[]{:S(2)}) copy-start(bf16[1024,768]{1,0:T(8,128)(2,1)} %get-tuple-element.52.query_grad_ref) | copy-start | bytes 4718596
  343.4 15.5 %copy-start.16 = (f32[8,768]{1,0:T(8,128)S(1)}, f32[8,768]{1,0:T(8,128)}, u32[]{:S(2)}) copy-start(f32[8,768]{1,0:T(8,128)} %copy-done.15) | copy-start | bytes 73732
  375.2 61.0 %collective-permute-start.25 = (bf16[384,3072]{1,0:T(8,128)(2,1)}, bf16[384,3072]{1,0:T(8,128)(2,1)}, u32[]{:S(2)}, u32[]{:S(2)}) collective-permute-start(bf16[384,3072]{1,0:T(8,128)(2,1)} %pad_maximum_fusion.3), channel_id=1, source_target_pairs={{0,8},{1,9},{2,10},{3,11},{4,12},{5,13},{6,14},{7,15},{8,0},{9,1},... | collective-permute-start | bytes 7077896 | tf_op jit(solution)/shard_map/ppermute | solution.py:443
  420.3 13.3 %collective-permute-start.20 = (bf16[384,2432]{1,0:T(8,128)(2,1)}, bf16[384,2432]{1,0:T(8,128)(2,1)S(1)}, u32[]{:S(2)}, u32[]{:S(2)}) collective-permute-start(bf16[384,2432]{1,0:T(8,128)(2,1)} %get-tuple-element.65), channel_id=1, source_target_pairs={{0,8},{1,9},{2,10},{3,11},{4,12},{5,13},{6,14},{7,15},{8,0},{9,1},... | collective-permute-start | bytes 5603336 | tf_op jit(solution)/shard_map/ppermute | solution.py:443
  420.8 12.8 %copy-start.23 = (bf16[384,2432]{1,0:T(8,128)(2,1)S(1)}, bf16[384,2432]{1,0:T(8,128)(2,1)}, u32[]{:S(2)}) copy-start(bf16[384,2432]{1,0:T(8,128)(2,1)} %get-tuple-element.64) | copy-start | bytes 5603332
  432.0 46.3 %collective-permute-start.31 = (bf16[2,2,2,24,6912]{4,3,2,1,0:T(8,128)(2,1)}, bf16[2,2,2,24,6912]{4,3,2,1,0:T(8,128)(2,1)}, u32[]{:S(2)}, u32[]{:S(2)}) collective-permute-start(bf16[2,2,2,24,6912]{4,3,2,1,0:T(8,128)(2,1)} %get-tuple-element.79), channel_id=1, source_target_pairs={{0,16},{1,17},{2,18},{3,19},{4,20},{5,21},{6,22},{7,23},{8,9},{9,8... | collective-permute-start | bytes 7962632 | tf_op jit(solution)/shard_map/ppermute | solution.py:443
  435.5 38.9 %collective-permute-start.21 = (bf16[2,2,2,24,2432]{4,3,2,1,0:T(8,128)(2,1)}, bf16[2,2,2,24,2432]{4,3,2,1,0:T(8,128)(2,1)}, u32[]{:S(2)}, u32[]{:S(2)}) collective-permute-start(bf16[2,2,2,24,2432]{4,3,2,1,0:T(8,128)(2,1)} %get-tuple-element.87), channel_id=1, source_target_pairs={{0,16},{1,17},{2,18},{3,19},{4,20},{5,21},{6,22},{7,23},{8,9},{9,8... | collective-permute-start | bytes 2801672 | tf_op jit(solution)/shard_map/ppermute | solution.py:443
  440.4 55.0 %collective-permute-start.26 = (bf16[2,2,2,24,3072]{4,3,2,1,0:T(8,128)(2,1)S(1)}, bf16[2,2,2,24,3072]{4,3,2,1,0:T(8,128)(2,1)S(1)}, u32[]{:S(2)}, u32[]{:S(2)}) collective-permute-start(bf16[2,2,2,24,3072]{4,3,2,1,0:T(8,128)(2,1)S(1)} %get-tuple-element.83), channel_id=1, source_target_pairs={{0,16},{1,17},{2,18},{3,19},{4,20},{5,21},{6,22},{7,23},{8,9},{9,8... | collective-permute-start | bytes 3538952 | tf_op jit(solution)/shard_map/ppermute | solution.py:443
  474.4 3.9 copy-start.22
  476.5 22.3 %collective-permute-start.22 = (bf16[2,2,24,2432]{3,2,1,0:T(8,128)(2,1)S(1)}, bf16[2,2,24,2432]{3,2,1,0:T(8,128)(2,1)S(1)}, u32[]{:S(2)}, u32[]{:S(2)}) collective-permute-start(bf16[2,2,24,2432]{3,2,1,0:T(8,128)(2,1)S(1)} %get-tuple-element.95), channel_id=1, source_target_pairs={{0,1},{1,0},{2,3},{3,2},{4,5},{5,4},{6,7},{7,6},{8,24},{9,25},{10,... | collective-permute-start | bytes 1400840 | tf_op jit(solution)/shard_map/ppermute | solution.py:443
  483.3 41.2 %collective-permute-start.32 = (bf16[2,2,24,6912]{3,2,1,0:T(8,128)(2,1)}, bf16[2,2,24,6912]{3,2,1,0:T(8,128)(2,1)S(1)}, u32[]{:S(2)}, u32[]{:S(2)}) collective-permute-start(bf16[2,2,24,6912]{3,2,1,0:T(8,128)(2,1)} %get-tuple-element.81), channel_id=1, source_target_pairs={{0,1},{1,0},{2,3},{3,2},{4,5},{5,4},{6,7},{7,6},{8,24},{9,25},{10,... | collective-permute-start | bytes 3981320 | tf_op jit(solution)/shard_map/ppermute | solution.py:443
  497.0 26.1 %collective-permute-start.27 = (bf16[2,2,24,3072]{3,2,1,0:T(8,128)(2,1)}, bf16[2,2,24,3072]{3,2,1,0:T(8,128)(2,1)}, u32[]{:S(2)}, u32[]{:S(2)}) collective-permute-start(bf16[2,2,24,3072]{3,2,1,0:T(8,128)(2,1)} %get-tuple-element.91), channel_id=1, source_target_pairs={{0,1},{1,0},{2,3},{3,2},{4,5},{5,4},{6,7},{7,6},{8,24},{9,25},{10,... | collective-permute-start | bytes 1769480 | tf_op jit(solution)/shard_map/ppermute | solution.py:443
  499.6 19.4 %collective-permute-start.23 = (bf16[2,24,2432]{2,1,0:T(8,128)(2,1)}, bf16[2,24,2432]{2,1,0:T(8,128)(2,1)}, u32[]{:S(2)}, u32[]{:S(2)}) collective-permute-start(bf16[2,24,2432]{2,1,0:T(8,128)(2,1)} %get-tuple-element.107), channel_id=1, source_target_pairs={{0,4},{1,5},{2,6},{3,7},{4,0},{5,1},{6,2},{7,3},{8,12},{9,13},{10,... | collective-permute-start | bytes 700424 | tf_op jit(solution)/shard_map/ppermute | solution.py:443
  499.6 2.8 copy-start.3
  520.0 7.7 %collective-permute-start.24 = (bf16[24,2432]{1,0:T(8,128)(2,1)S(1)}, bf16[24,2432]{1,0:T(8,128)(2,1)S(1)}, u32[]{:S(2)}, u32[]{:S(2)}) collective-permute-start(bf16[24,2432]{1,0:T(8,128)(2,1)S(1)} %fusion.16), channel_id=1, source_target_pairs={{0,2},{1,3},{2,0},{3,1},{4,6},{5,7},{6,4},{7,5},{8,10},{9,11},{10,... | collective-permute-start | bytes 350216 | tf_op jit(solution)/shard_map/ppermute | solution.py:443
  524.4 27.0 %collective-permute-start.28 = (bf16[2,24,3072]{2,1,0:T(8,128)(2,1)S(1)}, bf16[2,24,3072]{2,1,0:T(8,128)(2,1)S(1)}, u32[]{:S(2)}, u32[]{:S(2)}) collective-permute-start(bf16[2,24,3072]{2,1,0:T(8,128)(2,1)S(1)} %get-tuple-element.101), channel_id=1, source_target_pairs={{0,4},{1,5},{2,6},{3,7},{4,0},{5,1},{6,2},{7,3},{8,12},{9,13},{10,... | collective-permute-start | bytes 884744 | tf_op jit(solution)/shard_map/ppermute | solution.py:443
  524.8 39.6 %collective-permute-start.33 = (bf16[2,24,6912]{2,1,0:T(8,128)(2,1)S(1)}, bf16[2,24,6912]{2,1,0:T(8,128)(2,1)S(1)}, u32[]{:S(2)}, u32[]{:S(2)}) collective-permute-start(bf16[2,24,6912]{2,1,0:T(8,128)(2,1)S(1)} %get-tuple-element.89), channel_id=1, source_target_pairs={{0,4},{1,5},{2,6},{3,7},{4,0},{5,1},{6,2},{7,3},{8,12},{9,13},{10,... | collective-permute-start | bytes 1990664 | tf_op jit(solution)/shard_map/ppermute | solution.py:443
  551.4 16.1 %collective-permute-start.29 = (bf16[24,3072]{1,0:T(8,128)(2,1)S(1)}, bf16[24,3072]{1,0:T(8,128)(2,1)S(1)}, u32[]{:S(2)}, u32[]{:S(2)}) collective-permute-start(bf16[24,3072]{1,0:T(8,128)(2,1)S(1)} %fusion.13), channel_id=1, source_target_pairs={{0,2},{1,3},{2,0},{3,1},{4,6},{5,7},{6,4},{7,5},{8,10},{9,11},{10,... | collective-permute-start | bytes 442376 | tf_op jit(solution)/shard_map/ppermute | solution.py:443
  564.4 10.1 %collective-permute-start.34 = (bf16[24,6912]{1,0:T(8,128)(2,1)S(1)}, bf16[24,6912]{1,0:T(8,128)(2,1)S(1)}, u32[]{:S(2)}, u32[]{:S(2)}) collective-permute-start(bf16[24,6912]{1,0:T(8,128)(2,1)S(1)} %fusion.4), channel_id=1, source_target_pairs={{0,2},{1,3},{2,0},{3,1},{4,6},{5,7},{6,4},{7,5},{8,10},{9,11},{10,... | collective-permute-start | bytes 995336 | tf_op jit(solution)/shard_map/ppermute | solution.py:443
  (8 other events, 13.5 us)

commit v3 on v2

--- a/solution.py
+++ b/solution.py
@@ -30,6 +30,14 @@
 
 def iota(shape, axis):
     return lax.broadcasted_iota(jnp.int32, shape, axis)
+
+
+def cost(microseconds):
+    return pl.CostEstimate(flops=int(microseconds * 1.1e9), bytes_accessed=0, transcendentals=0)
+
+
+def passing(kernel, before, given, *refs):
+    return kernel(*refs[:before], *refs[before + given :])
 
 
 def split_three(values):
@@ -113,6 +121,7 @@
             jax.ShapeDtypeStruct((pairs, 8, seq_len), F32),
         ],
         compiler_params=pltpu.CompilerParams(vmem_limit_bytes=48 * 2**20),
+        cost_estimate=cost(22),
         name="self_forward",
     )(lengths, projected, projected, projected)
 
@@ -217,29 +226,33 @@
     out_ref[2] = value_grad_ref[...].astype(BF16)
 
 
-def self_backward(projected, lengths, grad, exact, logsum):
+def self_backward(projected, lengths, grad, exact, logsum, first, count, earlier):
     seq_len = projected.shape[0]
     width = projected.shape[1] // 3
     pairs = width // LANES
     column = lambda offset: pl.BlockSpec((seq_len, LANES), lambda p: (0, p + offset))
+    given = [] if earlier is None else [earlier]
     return pl.pallas_call(
-        self_backward_kernel,
-        grid=(pairs,),
+        functools.partial(passing, self_backward_kernel, 7, len(given)),
+        grid=(count,),
         in_specs=[
             pl.BlockSpec(memory_space=pltpu.SMEM),
-            column(0),
-            column(pairs),
-            column(2 * pairs),
-            column(0),
-            column(0),
-            pl.BlockSpec((1, 8, seq_len), lambda p: (p, 0, 0)),
-        ],
-        out_specs=pl.BlockSpec((3, seq_len, LANES), lambda p: (0, 0, p)),
+            column(first),
+            column(pairs + first),
+            column(2 * pairs + first),
+            column(first),
+            column(first),
+            pl.BlockSpec((1, 8, seq_len), lambda p: (p + first, 0, 0)),
+        ]
+        + [pl.BlockSpec(memory_space=pl.ANY)] * len(given),
+        out_specs=pl.BlockSpec((3, seq_len, LANES), lambda p: (0, 0, p + first)),
         out_shape=jax.ShapeDtypeStruct((3, seq_len, width), BF16),
         scratch_shapes=[pltpu.VMEM((seq_len, LANES), F32), pltpu.VMEM((seq_len, LANES), F32)],
+        input_output_aliases={7: 0} if given else {},
         compiler_params=pltpu.CompilerParams(vmem_limit_bytes=48 * 2**20),
+        cost_estimate=cost(25),
         name="self_backward",
-    )(lengths, projected, projected, projected, grad, exact, logsum)
+    )(lengths, projected, projected, projected, grad, exact, logsum, *given)
 
 
 def block_diagonal(rows):
@@ -306,6 +319,7 @@
         ),
         out_shape=jax.ShapeDtypeStruct((seq_len, width), BF16),
         compiler_params=pltpu.CompilerParams(vmem_limit_bytes=48 * 2**20),
+        cost_estimate=cost(17),
         name="cross_forward",
     )(ids, neighbour_lengths, queries, pool_keyval, pool_keyval)
 
@@ -325,8 +339,8 @@
     key_total,
     value_total,
 ):
-    span = pl.program_id(1)
-    spans = pl.num_programs(1)
+    span = pl.program_id(0)
+    spans = pl.num_programs(0)
     neigh_len = first_key_ref.shape[1]
 
     @pl.when(span == 0)
@@ -361,23 +375,25 @@
         value_out_ref[...] = value_total[...].astype(BF16)
 
 
-def cross_backward(queries, grads, pool_keyval, ids, neighbour_lengths):
+def cross_backward(queries, grads, pool_keyval, ids, neighbour_lengths, group, earlier):
     seq_len, width = queries.shape
     pool_count, neigh_len, _ = pool_keyval.shape
     spans = seq_len // SPAN
     groups = width // WIDE
-    rows = pl.BlockSpec((SPAN, WIDE), lambda g, c, ids, lens: (c, g))
+    rows = pl.BlockSpec((SPAN, WIDE), lambda c, ids, lens: (c, group))
     slot = lambda j, offset: pl.BlockSpec(
-        (1, neigh_len, WIDE), lambda g, c, ids, lens: (ids[c * NEIGH + j], 0, g + offset)
-    )
-    pool = pl.BlockSpec((pool_count, neigh_len, WIDE), lambda g, c, ids, lens: (0, 0, g))
+        (1, neigh_len, WIDE), lambda c, ids, lens: (ids[c * NEIGH + j], 0, group + offset)
+    )
+    pool = pl.BlockSpec((pool_count, neigh_len, WIDE), lambda c, ids, lens: (0, 0, group))
     pool_shape = jax.ShapeDtypeStruct((pool_count, neigh_len, width), BF16)
+    given = [] if earlier is None else list(earlier)
     return pl.pallas_call(
-        cross_backward_kernel,
+        functools.partial(passing, cross_backward_kernel, 8, len(given)),
         grid_spec=pltpu.PrefetchScalarGridSpec(
             num_scalar_prefetch=2,
-            grid=(groups, spans),
-            in_specs=[rows, rows, slot(0, 0), slot(1, 0), slot(0, groups), slot(1, groups)],
+            grid=(spans,),
+            in_specs=[rows, rows, slot(0, 0), slot(1, 0), slot(0, groups), slot(1, groups)]
+            + [pl.BlockSpec(memory_space=pl.ANY)] * len(given),
             out_specs=[rows, pool, pool],
             scratch_shapes=[
                 pltpu.VMEM((pool_count, neigh_len, WIDE), F32),
@@ -385,9 +401,11 @@
             ],
         ),
         out_shape=[jax.ShapeDtypeStruct((seq_len, width), BF16), pool_shape, pool_shape],
+        input_output_aliases={8 + i: i for i in range(len(given))},
         compiler_params=pltpu.CompilerParams(vmem_limit_bytes=56 * 2**20),
+        cost_estimate=cost(48),
         name="cross_backward",
-    )(ids, neighbour_lengths, queries, grads, pool_keyval, pool_keyval, pool_keyval, pool_keyval)
+    )(ids, neighbour_lengths, queries, grads, *[pool_keyval] * 4, *given)
 
 AXES = ("fsdp", "dp")
 
@@ -400,12 +418,25 @@
     return [1 << i for i in range(count.bit_length() - 2, -1, -1)]
 
 
-def place(side, own, other):
-    return jnp.stack([jnp.where(side == 0, own, other), jnp.where(side == 0, other, own)])
+class Line:
+    def __init__(self):
+        self.noted = []
+
+    def note(self, *values):
+        self.noted = [values[0]]
+
+    def also(self, value):
+        self.noted.append(value)
+
+    def after(self, value):
+        if not self.noted:
+            return value
+        return lax.optimization_barrier((value, *self.noted))[0]
 
 
 class Plan:
-    def __init__(self, rows):
+    def __init__(self, rows, line):
+        self.line = line
         self.inner = lax.axis_size("dp")
         self.outer = lax.axis_size("fsdp")
         self.count = self.inner * self.outer
@@ -423,16 +454,14 @@
         self.natural = [mask for mask in index_bits(self.count) if mask not in self.core]
         self.odd = self.bit(self.core[0]) if self.core else jnp.zeros((), jnp.int32)
         self.odd_word = self.odd.reshape(1)
-
-    def steps(self):
-        return list(zip(*self.orders))
+        self.steps = list(zip(*self.orders))
+        self.places = self.arrival_places()
 
     def bit(self, mask):
         return (self.me // mask) % 2
 
-    def side(self, masks):
-        even, odd = masks
-        return jnp.where(self.odd == 0, self.bit(even), self.bit(odd))
+    def by_core(self, even, odd):
+        return jnp.where(self.odd == 0, even, odd)
 
     def exchange(self, values, masks):
         even, odd = masks
@@ -445,92 +474,181 @@
     def swap(self, values):
         return self.exchange(values, (self.core[0], self.core[0])) if self.core else values
 
-
-def reorder_kernel(moves, odd_ref, in_ref, out_ref, buffer, sems):
-    for parity, pairs in enumerate(moves):
-
-        @pl.when(odd_ref[0] == parity)
-        def _():
-            for source, target in pairs:
-                pltpu.make_async_copy(
-                    in_ref.at[source], buffer.at[target], sems.at[source]
-                ).start()
-            for source, target in pairs:
-                pltpu.make_async_copy(
-                    in_ref.at[source], buffer.at[target], sems.at[source]
-                ).wait()
-
+    def weight_of(self, mask):
+        return 1 << (len(self.natural) - 1 - self.natural.index(mask))
+
+    def arrival_places(self):
+        blocks = jnp.arange(1 << len(self.natural), dtype=jnp.int32)
+        found = []
+        for order in self.orders:
+            target = jnp.zeros_like(blocks)
+            for place_at, mask in enumerate(order):
+                flag = ((blocks >> place_at) & 1) ^ self.bit(mask)
+                target = target + flag * self.weight_of(mask)
+            found.append(target)
+        return self.by_core(found[0], found[1])
+
+    def fold_places(self, step):
+        found = []
+        for order in self.orders:
+            gone = order[::-1][:step]
+            left = [mask for mask in self.natural if mask not in gone]
+            mask = order[::-1][step]
+            high = 1 << (len(left) - 1 - left.index(mask))
+            index = jnp.arange(1 << (len(left) - 1), dtype=jnp.int32)
+            kept = (index // high) * (2 * high) + index % high
+            own = self.bit(mask)
+            found.append((kept + (1 - own) * high, kept + own * high))
+        return tuple(self.by_core(found[0][i], found[1][i]) for i in range(2))
+
+
+def reorder_kernel(places_ref, in_ref, out_ref, buffer, sems):
+    blocks = in_ref.shape[0]
+
+    def copies(block):
+        return pltpu.make_async_copy(
+            in_ref.at[block], buffer.at[places_ref[block]], sems.at[block]
+        )
+
+    for block in range(blocks):
+        copies(block).start()
+    for block in range(blocks):
+        copies(block).wait()
     pltpu.sync_copy(buffer, out_ref)
 
 
 def reorder(plan, held):
     blocks = held.shape[0]
-    moves = []
-    for order in plan.orders[: plan.halves]:
-        pairs = []
-        for source in range(blocks):
-            target = 0
-            for place_at, mask in enumerate(order):
-                if (source >> place_at) & 1:
-                    target += 1 << (len(plan.natural) - 1 - plan.natural.index(mask))
-            pairs.append((source, target))
-        moves.append(pairs)
     return pl.pallas_call(
-        functools.partial(reorder_kernel, moves),
+        reorder_kernel,
         in_specs=[pl.BlockSpec(memory_space=pltpu.SMEM), pl.BlockSpec(memory_space=pl.ANY)],
         out_specs=pl.BlockSpec(memory_space=pl.ANY),
         out_shape=jax.ShapeDtypeStruct(held.shape, held.dtype),
         scratch_shapes=[pltpu.VMEM(held.shape, held.dtype), pltpu.SemaphoreType.DMA((blocks,))],
         compiler_params=pltpu.CompilerParams(vmem_limit_bytes=32 * 2**20),
         name="reorder_blocks",
-    )(plan.odd_word, held)
-
-
-def gather_halves(plan, shard):
-    columns = shard.shape[1]
-    held = shard
-    for masks in plan.steps():
-        other = plan.exchange(held, masks)
-        held = place(plan.side(masks), held, other)
-    held = reorder(plan, held.reshape((-1,) + shard.shape))
-    other = plan.swap(held)
-    shape = (plan.half_rows, columns)
-    return (held.reshape(shape), other.reshape(shape))
-
-
-def scatter_halves(plan, keep, send):
-    columns = keep.shape[1]
-    shape = (2,) * len(plan.natural) + (plan.rows, columns)
-    blocks = [keep.reshape(shape)]
-    if plan.core:
-        blocks.append(plan.swap(send).reshape(shape))
-
-    def add(parts):
-        total = parts[0].astype(F32)
-        for part in parts[1:]:
-            total = total + part.astype(F32)
-        return total.astype(BF16)
-
-    def pick(parts, axes, index):
-        chosen = []
-        for part in parts:
-            even, odd = [lax.dynamic_index_in_dim(part, index, axis, False) for axis in axes]
-            chosen.append(even if axes[0] == axes[1] else jnp.where(plan.odd == 0, even, odd))
-        return add(chosen)
-
-    layouts = [list(plan.natural), list(plan.natural)]
-    for masks in plan.steps()[::-1]:
-        axes = tuple(layouts[parity].index(masks[parity]) for parity in range(2))
-        side = plan.side(masks)
-        sent = pick(blocks, axes, 1 - side)
-        kept = pick(blocks, axes, side)
-        blocks = [kept, plan.exchange(sent, masks)]
-        for parity in range(2):
-            layouts[parity].pop(axes[parity])
-    total = blocks[0].astype(F32)
-    for part in blocks[1:]:
-        total = total + part.astype(F32)
-    return total.reshape(plan.rows, columns)
+    )(plan.places, held)
+
+
+class Gather:
+    def __init__(self, plan, shard):
+        self.plan = plan
+        self.held = shard[None]
+        self.at = 0
+        self.other = None
+        self.halves = None
+
+    def launch(self):
+        plan = self.plan
+        self.held = plan.line.after(self.held)
+        plan.line.also(self.held)
+        if self.at < len(plan.steps):
+            self.other = plan.exchange(self.held, plan.steps[self.at])
+        else:
+            self.other = plan.swap(self.held)
+
+    def land(self):
+        plan = self.plan
+        other = plan.line.after(self.other)
+        if self.at < len(plan.steps):
+            self.held = jnp.concatenate([self.held, other], axis=0)
+            self.at += 1
+            if self.at == len(plan.steps):
+                self.held = reorder(plan, self.held)
+            plan.line.note(self.held)
+        else:
+            plan.line.note(other)
+            shape = (plan.half_rows, self.held.shape[-1])
+            self.halves = (self.held.reshape(shape), other.reshape(shape))
+
+    def step(self):
+        if self.halves is None:
+            self.land()
+            if self.halves is None:
+                self.launch()
+
+    def finish(self):
+        while self.halves is None:
+            self.step()
+        return self.halves
+
+
+def fold_kernel(sent_places, kept_places, *refs):
+    half = len(refs) // 2 - 1
+    sent_in, kept_in, (sent_ref, kept_ref) = refs[:half], refs[half : 2 * half], refs[2 * half :]
+    for source, target in ((sent_in, sent_ref), (kept_in, kept_ref)):
+        total = source[0][...].astype(F32)
+        for part in source[1:]:
+            total = total + part[...].astype(F32)
+        target[...] = total.astype(BF16)
+
+
+def fold(places, parts):
+    blocks, rows, columns = parts[0].shape
+    shape = jax.ShapeDtypeStruct((blocks // 2, rows, columns), BF16)
+    out = pl.BlockSpec((1, rows, columns), lambda i, sent, kept: (i, 0, 0))
+    sent = pl.BlockSpec((1, rows, columns), lambda i, sent, kept: (sent[i], 0, 0))
+    kept = pl.BlockSpec((1, rows, columns), lambda i, sent, kept: (kept[i], 0, 0))
+    return pl.pallas_call(
+        fold_kernel,
+        grid_spec=pltpu.PrefetchScalarGridSpec(
+            num_scalar_prefetch=2,
+            grid=(blocks // 2,),
+            in_specs=[sent] * len(parts) + [kept] * len(parts),
+            out_specs=[out, out],
+        ),
+        out_shape=[shape, shape],
+        compiler_params=pltpu.CompilerParams(vmem_limit_bytes=32 * 2**20),
+        name="fold_blocks",
+    )(*places, *parts, *parts)
+
+
+class Scatter:
+    def __init__(self, plan, keep, send):
+        self.plan = plan
+        self.columns = keep.shape[1]
+        shape = (1 << len(plan.natural), plan.rows, self.columns)
+        self.kept = keep.reshape(shape)
+        self.sent = send.reshape(shape) if plan.core else None
+        self.at = -1
+        self.other = None
+        self.total = None
+
+    def launch(self):
+        plan = self.plan
+        if self.sent is None:
+            return
+        self.sent = plan.line.after(self.sent)
+        plan.line.also(self.sent)
+        if self.at < 0:
+            self.other = plan.swap(self.sent)
+        else:
+            self.other = plan.exchange(self.sent, plan.steps[::-1][self.at])
+
+    def land(self):
+        plan = self.plan
+        parts = [self.kept] if self.other is None else [self.kept, plan.line.after(self.other)]
+        self.at += 1
+        if self.at < len(plan.steps):
+            self.sent, self.kept = fold(plan.fold_places(self.at), parts)
+            plan.line.note(self.sent)
+        else:
+            total = parts[0].astype(F32)
+            for part in parts[1:]:
+                total = total + part.astype(F32)
+            self.total = total.reshape(plan.rows, self.columns)
+            plan.line.note(self.total)
+
+    def step(self):
+        if self.total is None:
+            self.land()
+            if self.total is None:
+                self.launch()
+
+    def finish(self):
+        while self.total is None:
+            self.step()
+        return self.total
 
 
 def column_copies(plan, odd, held_ref, other_ref, target, sems, start, width):
@@ -652,6 +770,7 @@
         out_shape=jax.ShapeDtypeStruct((rows, 2 * width), BF16),
         scratch_shapes=[pltpu.VMEM((width, 2 * width), BF16), copy_sems(plan)],
         compiler_params=params(40),
+        cost_estimate=cost(13),
         name="pool_project",
     )(plan.odd_word, encoded, *halves)
 
@@ -709,6 +828,7 @@
             copy_sems(plan, 2),
         ],
         compiler_params=params(40),
+        cost_estimate=cost(6),
         name="project",
     )(plan.odd_word, tokens, *halves)
 
@@ -774,6 +894,7 @@
             copy_sems(plan, 2),
         ],
         compiler_params=params(40),
+        cost_estimate=cost(6),
         name="middle",
     )(plan.odd_word, tokens, mixed, vectors, *halves)
 
@@ -799,8 +920,10 @@
     mixed_ref,
     cotangent_ref,
     vectors_ref,
-    feed_held_ref,
-    feed_other_ref,
+    up_held_ref,
+    up_other_ref,
+    down_held_ref,
+    down_other_ref,
     held_ref,
     other_ref,
     block_ref,
@@ -823,14 +946,15 @@
             return column_copies(
                 plan, odd_ref[0], held_ref, other_ref, weights.at[index], sems.at[index], out_start, width
             )
+        is_up = index < parts
         return column_copies(
             plan,
             odd_ref[0],
-            feed_held_ref,
-            feed_other_ref,
+            up_held_ref if is_up else down_held_ref,
+            up_other_ref if is_up else down_other_ref,
             weights.at[index],
             sems.at[index],
-            index * width,
+            (index if is_up else index - parts) * width,
             width,
         )
 
@@ -899,9 +1023,9 @@
         store_halves(plan, odd_ref[0], result, keep_ref, send_ref, slice(0, width))
 
 
-def feed(plan, out_start, after, mixed, cotangent, vectors, feed_halves, halves):
+def feed(plan, out_start, after, mixed, cotangent, vectors, up_halves, down_halves, halves):
     rows, width = after.shape
-    parts = feed_halves[0].shape[1] // width // 2
+    parts = up_halves[0].shape[1] // width
     terms = 2 * parts + 1
     steps = rows // ROWS
     last = steps - 1
@@ -912,7 +1036,7 @@
     return pl.pallas_call(
         functools.partial(feed_kernel, plan, out_start, steps),
         grid=(steps + terms,),
-        in_specs=[SCALAR, rows_in, rows_in, rows_in, whole] + [ANYWHERE] * 4,
+        in_specs=[SCALAR, rows_in, rows_in, rows_in, whole] + [ANYWHERE] * 6,
         out_specs=[rows_in, rows_in, rows_in, whole, slab, slab],
         out_shape=[
             jax.ShapeDtypeStruct((rows, width), BF16),
@@ -929,8 +1053,9 @@
             copy_sems(plan, terms),
         ],
         compiler_params=params(60),
+        cost_estimate=cost(58),
         name="feed_forward",
-    )(plan.odd_word, after, mixed, cotangent, vectors, *feed_halves, *halves)
+    )(plan.odd_word, after, mixed, cotangent, vectors, *up_halves, *down_halves, *halves)
 
 
 def second_kernel(
@@ -1021,6 +1146,7 @@
             copy_sems(plan, 2),
         ],
         compiler_params=params(48),
+        cost_estimate=cost(14),
         name="second_back",
     )(plan.odd_word, after, grad_in, query_grad, second_in, mixed, vectors, *halves)
 
@@ -1124,6 +1250,7 @@
             copy_sems(plan),
         ],
         compiler_params=params(56),
+        cost_estimate=cost(18),
         name="first_back",
     )(
         plan.odd_word,
@@ -1178,6 +1305,7 @@
         out_shape=[slab_shape, slab_shape],
         scratch_shapes=[pltpu.VMEM((width, width), F32), pltpu.VMEM((width, width), F32)],
         compiler_params=params(48),
+        cost_estimate=cost(15),
         name="keyval_terms",
     )(plan.odd_word, encoded, pool_keys, pool_values)
 
@@ -1198,20 +1326,23 @@
     )
 
 
-def neighbours_back(plan, pool_keys, pool_values, halves):
+def neighbours_back(plan, pool_keys, pool_values, halves, first, count, earlier):
     rows, width = pool_keys.shape
     block = 512
-    rows_in = pl.BlockSpec((block, width), lambda i: (i, 0))
+    rows_in = pl.BlockSpec((block, width), lambda i: (i + first, 0))
+    given = [] if earlier is None else [earlier]
     return pl.pallas_call(
-        functools.partial(neighbours_kernel, plan),
-        grid=(rows // block,),
-        in_specs=[SCALAR, rows_in, rows_in, ANYWHERE, ANYWHERE],
+        functools.partial(passing, functools.partial(neighbours_kernel, plan), 5, len(given)),
+        grid=(count,),
+        in_specs=[SCALAR, rows_in, rows_in, ANYWHERE, ANYWHERE] + [ANYWHERE] * len(given),
         out_specs=rows_in,
         out_shape=jax.ShapeDtypeStruct((rows, width), F32),
         scratch_shapes=[pltpu.VMEM((width, 2 * width), BF16), copy_sems(plan)],
+        input_output_aliases={5: 0} if given else {},
         compiler_params=params(40),
+        cost_estimate=cost(15),
         name="neighbours_back",
-    )(plan.odd_word, pool_keys, pool_values, *halves)
+    )(plan.odd_word, pool_keys, pool_values, *halves, *given)
 
 def local(
     tokens,
@@ -1235,98 +1366,194 @@
     cotangent,
 ):
     rows, width = cross_query.shape
-    plan = Plan(rows)
+    line = Line()
+    plan = Plan(rows, line)
+    steps = len(plan.steps)
     parts = feed_down.shape[0] // rows
     pool_count, neigh_len = neighbours.shape[:2]
     vectors = (first_gain, first_shift, second_gain, second_shift, third_gain, third_shift)
     vector_pack = jnp.pad(jnp.stack(vectors, axis=1), ((0, 0), (0, LANES - len(vectors))))
     up_shard = feed_up.reshape(rows, plan.count, parts, rows).swapaxes(1, 2).reshape(feed_up.shape)
     down_shard = feed_down.reshape(parts, rows, width).swapaxes(0, 1).reshape(rows, parts * width)
-
-    keyval_halves = gather_halves(plan, cross_keyval)
-    project_halves = gather_halves(plan, jnp.concatenate([self_input, vector_pack], axis=1))
-    middle_halves = gather_halves(
-        plan, jnp.concatenate([self_output, cross_query, cross_output], axis=1)
-    )
-    feed_halves = gather_halves(plan, jnp.concatenate([up_shard, down_shard], axis=1))
-
     rows_in = tokens[0]
     encoded = neighbours.reshape(pool_count * neigh_len, width)
     ids = neighbour_ids.reshape(-1)
-    pool_keyval = pool_project(plan, encoded, keyval_halves)
+
+    def advance(*chunks):
+        for chunk in chunks:
+            chunk.step()
+
+    def run(kernel, first, *rest):
+        results = kernel(line.after(first), *rest)
+        line.note(results[0] if isinstance(results, (tuple, list)) else results)
+        return results
+
+    keyval = Gather(plan, cross_keyval)
+    start = Gather(plan, jnp.concatenate([self_input, vector_pack], axis=1))
+    middle_part = Gather(plan, jnp.concatenate([self_output, cross_query, cross_output], axis=1))
+    up = Gather(plan, up_shard)
+    down = Gather(plan, down_shard)
+
+    keyval.launch()
+    start.launch()
+    advance(keyval)
+    advance(keyval, start)
+    middle_part.launch()
+    up.launch()
+    down.launch()
+    advance(keyval, start)
+    advance(keyval, start, middle_part)
+    advance(start, middle_part, up)
+    keyval_halves = keyval.finish()
+    pool_keyval = run(functools.partial(pool_project, plan), encoded, keyval_halves)
     pool_keyval = pool_keyval.reshape(pool_count, neigh_len, 2 * width)
-    first_in, projected, vector_rows = project(plan, rows_in, project_halves)
-    self_mixed, self_exact, logsum = self_forward(projected, lengths)
-    after_self, second_in, cross_queries = middle(
-        plan, (0, width), rows_in, self_mixed, vector_rows, middle_halves
-    )
-    cross_mixed = cross_forward(cross_queries, pool_keyval, ids, neighbour_lengths)
-    block_out, after_cross_grad, mixed_grad, third_terms, feed_keep, feed_send = feed(
-        plan,
-        2 * width,
-        after_self,
+    start_halves = start.finish()
+    advance(middle_part, up, down)
+    first_in, projected, vector_rows = run(
+        lambda values: project(plan, values, start_halves), rows_in
+    )
+    advance(middle_part, up, down)
+    self_mixed, self_exact, logsum = run(self_forward, projected, lengths)
+    middle_halves = middle_part.finish()
+    advance(up, down)
+    after_self, second_in, cross_queries = run(
+        lambda values: middle(plan, (0, width), rows_in, values, vector_rows, middle_halves),
+        self_mixed,
+    )
+    up_halves = up.finish()
+    cross_mixed = run(cross_forward, cross_queries, pool_keyval, ids, neighbour_lengths)
+    down_halves = down.finish()
+    block_out, after_cross_grad, mixed_grad, third_terms, feed_keep, feed_send = run(
+        lambda values: feed(
+            plan,
+            2 * width,
+            after_self,
+            values,
+            cotangent[0],
+            vector_rows,
+            up_halves,
+            down_halves,
+            middle_halves,
+        ),
         cross_mixed,
-        cotangent[0],
-        vector_rows,
-        feed_halves,
-        middle_halves,
-    )
-    feed_sum = scatter_halves(plan, feed_keep, feed_send)
-
-    query_grad, pool_keys, pool_values = cross_backward(
-        cross_queries, mixed_grad, pool_keyval, ids, neighbour_lengths
-    )
+    )
+    feed_sum = Scatter(plan, feed_keep, feed_send)
+    feed_sum.launch()
+
+    crossed = None
+    for group in range(width // WIDE):
+        crossed = run(
+            cross_backward,
+            cross_queries,
+            mixed_grad,
+            pool_keyval,
+            ids,
+            neighbour_lengths,
+            group,
+            crossed,
+        )
+        if group == 0:
+            advance(feed_sum)
+    advance(feed_sum)
+    query_grad, pool_keys, pool_values = crossed
     pool_keys = pool_keys.reshape(pool_count * neigh_len, width)
     pool_values = pool_values.reshape(pool_count * neigh_len, width)
-    keyval_keep, keyval_send = keyval_terms(plan, encoded, pool_keys, pool_values)
-    after_self_grad, attend_grad, second_terms, second_keep, second_send = second_back(
-        plan,
-        (0, width),
-        after_self,
-        after_cross_grad,
+    keyval_keep, keyval_send = run(
+        lambda values: keyval_terms(plan, encoded, values, pool_values), pool_keys
+    )
+    advance(feed_sum)
+    after_self_grad, attend_grad, second_terms, second_keep, second_send = run(
+        lambda values: second_back(
+            plan,
+            (0, width),
+            after_self,
+            after_cross_grad,
+            values,
+            second_in,
+            self_mixed,
+            vector_rows,
+            middle_halves,
+        ),
         query_grad,
-        second_in,
-        self_mixed,
-        vector_rows,
-        middle_halves,
-    )
-    middle_sum = scatter_halves(
+    )
+    middle_sum = Scatter(
         plan,
         jnp.concatenate([keyval_keep, second_keep], axis=1),
         jnp.concatenate([keyval_send, second_send], axis=1),
     )
-    projected_grad = self_backward(projected, lengths, attend_grad, self_exact, logsum)
-    tokens_grad, first_keep, first_send = first_back(
-        plan,
-        rows_in,
-        after_self_grad,
+    middle_sum.launch()
+    pairs = width // LANES
+    projected_grad = None
+    for turn in range(2):
+        projected_grad = run(
+            lambda values: self_backward(
+                projected,
+                lengths,
+                values,
+                self_exact,
+                logsum,
+                turn * (pairs // 2),
+                pairs // 2,
+                projected_grad,
+            ),
+            attend_grad,
+        )
+        advance(middle_sum, feed_sum)
+    tokens_grad, first_keep, first_send = run(
+        lambda values: first_back(
+            plan,
+            rows_in,
+            after_self_grad,
+            values,
+            first_in,
+            vector_rows,
+            second_terms,
+            third_terms,
+            start_halves,
+        ),
         projected_grad,
-        first_in,
-        vector_rows,
-        second_terms,
-        third_terms,
-        project_halves,
-    )
-    first_sum = scatter_halves(plan, first_keep, first_send)
-    neighbours_grad = neighbours_back(plan, pool_keys, pool_values, keyval_halves)
-
-    down_grad = feed_sum[:, : parts * width].reshape(rows, parts, width).swapaxes(0, 1)
-    up_grad = feed_sum[:, parts * width : 2 * parts * width]
+    )
+    first_sum = Scatter(plan, first_keep, first_send)
+    first_sum.launch()
+    advance(middle_sum)
+    blocks = pool_keys.shape[0] // 512
+    neighbours_grad = None
+    for turn in range(2):
+        advance(first_sum)
+        neighbours_grad = run(
+            lambda values: neighbours_back(
+                plan,
+                values,
+                pool_values,
+                keyval_halves,
+                turn * (blocks // 2),
+                blocks // 2,
+                neighbours_grad,
+            ),
+            pool_keys,
+        )
+        advance(middle_sum)
+    feed_total = feed_sum.finish()
+    middle_total = middle_sum.finish()
+    first_total = first_sum.finish()
+
+    down_grad = feed_total[:, : parts * width].reshape(rows, parts, width).swapaxes(0, 1)
+    up_grad = feed_total[:, parts * width : 2 * parts * width]
     up_grad = up_grad.reshape(rows, parts, plan.count, rows).swapaxes(1, 2)
-    vector_grads = [first_sum[:, 3 * width + i] for i in range(len(vectors))]
+    vector_grads = [first_total[:, 3 * width + i] for i in range(len(vectors))]
     return (
         block_out[None],
         tokens_grad[None],
         neighbours_grad.reshape(neighbours.shape),
         vector_grads[0],
         vector_grads[1],
-        first_sum[:, : 3 * width],
-        middle_sum[:, 3 * width :],
+        first_total[:, : 3 * width],
+        middle_total[:, 3 * width :],
         vector_grads[2],
         vector_grads[3],
-        middle_sum[:, 2 * width : 3 * width],
-        middle_sum[:, : 2 * width],
-        feed_sum[:, 2 * parts * width :],
+        middle_total[:, 2 * width : 3 * width],
+        middle_total[:, : 2 * width],
+        feed_total[:, 2 * parts * width :],
         vector_grads[4],
         vector_grads[5],
         up_grad.reshape(feed_up.shape),

time: 592 us -> 467 us (0.79)
  waiting for transfers between devices: 181 us -> 72.1 us
  other arithmetic: 35.6 us -> 4.82 us
  Pallas kernels: 277 us -> 303 us
  starting transfers between devices: 57.6 us -> 42.4 us
  local copies, waits for them, and re-layouts: 27.4 us -> 35.2 us
    ppermute x35 -> x40, waiting for transfers between devices: 181 us -> 72.1 us  [exchange(): return lax.ppermute(values, AXES, pairs)]
    pallas_call x7 -> x24, Pallas kernels: 103 us -> 133 us  [the longest x3 55 us: cross_backward(): pl.pallas_call(functools.partial(passing, cross_backward_kernel, 8, len(g...]
    convert_element_type x12 -> x0, other arithmetic: 29.3 us -> none  [add(): return total.astype(BF16)]
    ppermute x35 -> x40, starting transfers between devices: 57.6 us -> 42.4 us  [exchange(): return lax.ppermute(values, AXES, pairs)]
    unnamed x80 -> x103, local copies, waits for them, and re-layouts: 14.5 us -> 16.4 us
  transfers between devices with their start and end apart: 35 -> 40, of which waited for: 18 -> 16; matrix products, arithmetic and copies ran while one was open for 7% -> 5% of each run, Pallas kernels for 38% -> 45%
where the time goes in v3:
time: 467 us; the launch traced here: 460 us
  Pallas kernels  303 us (65%)
  waiting for transfers between devices  72.1 us (15%)
  starting transfers between devices  42.4 us (9%)
  local copies, waits for them, and re-layouts  35.2 us (8%)
  other arithmetic  4.82 us (1%)
    ppermute x40, waiting for transfers between devices, exchange(): return lax.ppermute(values, AXES, pairs)  72.1 us
    pallas_call x1, Pallas kernels, feed(): pl.pallas_call(functools.partial(feed_kernel, plan, out_start, steps), gr...  58.5 us
    pallas_call x3, Pallas kernels, cross_backward(): pl.pallas_call(functools.partial(passing, cross_backward_kernel, 8, len(g...  55 us
    ppermute x40, starting transfers between devices, exchange(): return lax.ppermute(values, AXES, pairs)  42.4 us
    pallas_call x2, Pallas kernels, self_backward(): pl.pallas_call(functools.partial(passing, self_backward_kernel, 7, len(gi...  27.4 us
    pallas_call x1, Pallas kernels, self_forward(): pl.pallas_call(self_forward_kernel, grid=(pairs,), in_specs=[pl.BlockSpec...  21.9 us
    pallas_call x1, Pallas kernels, first_back(): pl.pallas_call(functools.partial(first_kernel, plan, steps), grid=(steps,...  18.7 us
    pallas_call x2, Pallas kernels, neighbours_back(): pl.pallas_call(functools.partial(passing, functools.partial(neighbours_ke...  17.7 us
  transfers between devices with their start and end apart: 40, of which 16 were waited for; matrix products, arithmetic and copies ran while one was open for 5% of the time, Pallas kernels for 45%

profile of v3, /device:TPU:0, one launch (start us, length us, event | category | flops | bytes accessed | tf_op | source)
XLA Modules:
  0.0 459.9 jit_solution(13825814953383396773)
XLA Ops:
  0.6 3.1 collective-permute-start.1
  7.5 2.1 reshape.131
  11.2 3.0 collective-permute-start.2
  14.2 6.4 %collective-permute-done.2 = bf16[2,24,1536]{2,1,0:T(8,128)(2,1)S(1)} collective-permute-done((bf16[2,24,1536]{2,1,0:T(8,128)(2,1)S(1)}, bf16[2,24,1536]{2,1,0:T(8,128)(2,1)S(1)}, u32[]{:S(2)}, u32[]{:S(2)}) %collective-permute-start.2) | collective-permute-done | bytes 147488 | tf_op jit(solution)/shard_map/ppermute | solution.py:472
  21.5 3.4 collective-permute-start.6
  24.9 1.5 collective-permute-start.7
  26.6 2.0 collective-permute-start.3
  28.6 3.0 collective-permute-done.7
  31.7 1.6 collective-permute-start.9
  33.2 2.4 collective-permute-done.6
  35.6 1.6 collective-permute-start.8
  37.2 8.5 %collective-permute-done.9 = bf16[8,24,1536]{2,1,0:T(8,128)(2,1)S(1)} collective-permute-done((bf16[8,24,1536]{2,1,0:T(8,128)(2,1)S(1)}, bf16[8,24,1536]{2,1,0:T(8,128)(2,1)S(1)}, u32[]{:S(2)}, u32[]{:S(2)}) %collective-permute-start.9) | collective-permute-done | bytes 589856 | tf_op jit(solution)/shard_map/ppermute | solution.py:472
  45.9 2.7 reorder_blocks.5
  48.7 1.6 collective-permute-start.11
  51.1 11.2 %collective-permute-done.11 = bf16[8,24,2432]{2,1,0:T(8,128)(2,1)S(1)} collective-permute-done((bf16[8,24,2432]{2,1,0:T(8,128)(2,1)S(1)}, bf16[8,24,2432]{2,1,0:T(8,128)(2,1)S(1)}, u32[]{:S(2)}, u32[]{:S(2)}) %collective-permute-start.11) | collective-permute-done | bytes 933920 | tf_op jit(solution)/shard_map/ppermute | solution.py:472
  62.5 3.3 reorder_blocks.6
  66.0 1.6 collective-permute-start.13
  68.4 12.9 %pool_project.1 = bf16[4096,1536]{1,0:T(8,128)(2,1)} custom-call(s32[1]{0:T(128)} %bitcast.odd_ref.refs_0_, bf16[4096,768]{1,0:T(8,128)(2,1)S(1)} %bitcast.76, bf16[384,1536]{1,0:T(8,128)(2,1)S(1)} %bitcast.70, bf16[384,1536]{1,0:T(8,128)(2,1)S(1)} %bitcast.85), custom_call_target="tpu_custom_call" | custom-call | flops 14300000256 | tf_op jit(solution)/shard_map/pool_project/pallas_call | solution.py:765
  81.4 1.6 collective-permute-start.18
  83.8 1.3 collective-permute-start.17
  86.0 5.7 %project.1 = (bf16[1024,768]{1,0:T(8,128)(2,1)S(1)}, bf16[1024,2304]{1,0:T(8,128)(2,1)S(1)}, f32[8,768]{1,0:T(8,128)S(1)}) custom-call(s32[1]{0:T(128)} %bitcast.odd_ref.refs_0_, bf16[1024,768]{1,0:T(8,128)(2,1)S(1)} %bitcast.83, bf16[384,2432]{1,0:T(8,128)(2,1)S(1)} %bitcast.65, bf16[384,2432]{1,0:T(8,128)(2,1)S(1)} %bitcast.77), custom_call_target="tpu_custom_call" | custom-call | flops 6600000000 | tf_op jit(solution)/shard_map/project/pallas_call | solution.py:811
  91.7 2.1 copy-done.17
  93.9 6.9 %collective-permute-done.18 = bf16[8,24,2304]{2,1,0:T(8,128)(2,1)S(1)} collective-permute-done((bf16[8,24,2304]{2,1,0:T(8,128)(2,1)S(1)}, bf16[8,24,2304]{2,1,0:T(8,128)(2,1)S(1)}, u32[]{:S(2)}, u32[]{:S(2)}) %collective-permute-start.18) | collective-permute-done | bytes 884768 | tf_op jit(solution)/shard_map/ppermute | solution.py:472
  101.0 3.4 reorder_blocks.7
  104.5 1.6 collective-permute-start.20
  106.1 21.9 %self_forward.1 = (bf16[1024,768]{1,0:T(8,128)(2,1)S(1)}, f32[1024,768]{1,0:T(8,128)S(1)}, f32[6,8,1024]{2,1,0:T(8,128)S(1)}) custom-call(s32[1]{0:T(128)S(6)} %copy.95.length_ref.refs_0_, bf16[1024,2304]{1,0:T(8,128)(2,1)} %copy-done.17, bf16[1024,2304]{1,0:T(8,128)(2,1)} %copy-done.17, bf16[1024,2304]{1,0:T(8,128)(2,1)} %copy-done.17), custom_call_target="tpu_custom_call" | custom-call | flops 24199999488 | tf_op jit(solution)/shard_map/self_forward/pallas_call | solution.py:104
  128.0 1.7 copy-done.26
  131.6 4.0 reorder_blocks.8
  136.6 9.1 %collective-permute-done.19 = bf16[4,24,3072]{2,1,0:T(8,128)(2,1)} collective-permute-done((bf16[4,24,3072]{2,1,0:T(8,128)(2,1)S(1)}, bf16[4,24,3072]{2,1,0:T(8,128)(2,1)}, u32[]{:S(2)}, u32[]{:S(2)}) %collective-permute-start.19) | collective-permute-done | bytes 589856 | tf_op jit(solution)/shard_map/ppermute | solution.py:472
  147.5 1.5 copy-done.11
  149.0 1.4 copy-done.13
  150.4 1.4 copy-done.20
  151.8 5.6 %middle.1 = (f32[1024,768]{1,0:T(8,128)S(1)}, bf16[1024,768]{1,0:T(8,128)(2,1)S(1)}, bf16[1024,768]{1,0:T(8,128)(2,1)S(1)}) custom-call(s32[1]{0:T(128)} %bitcast.odd_ref.refs_0_, bf16[1024,768]{1,0:T(8,128)(2,1)S(1)} %bitcast.84, bf16[1024,768]{1,0:T(8,128)(2,1)S(1)} %copy-done.20, f32[8,768]{1,0:T(8,128)S(1)} %get-tuple-element.221.vectors_ref, ...), custom_call_target="tpu_custom_call" | custom-call | flops 6600000000 | tf_op jit(solution)/shard_map/middle/pallas_call | solution.py:874
  157.4 1.7 copy-done.18
  160.3 17.2 %cross_forward.1.mixed_ref = bf16[1024,768]{1,0:T(8,128)(2,1)S(1)} custom-call(s32[32]{0:T(128)S(1)} %reshape.139.ids_ref.refs_0_, s32[32]{0:T(128)S(1)} %copy-done.16, bf16[1024,768]{1,0:T(8,128)(2,1)S(1)} %get-tuple-element.245.query_ref.refs_2_, bf16[32,128,1536]{2,1,0:T(8,128)(2,1)} %bitcast.111, bf16[32,128,1536]{2,1,0:T(8,128)(2,1)} %bitcast.112), custom_call_target="tpu_custom_call" | custom-call | flops 18699999232 | tf_op jit(solution)/shard_map/cross_forward/pallas_call | solution.py:312
  178.6 4.0 reorder_blocks.9
  182.7 4.5 collective-permute-done.24
  187.2 1.4 copy-done.37
  188.6 58.5 %feed_forward.1 = (bf16[1024,768]{1,0:T(8,128)(2,1)}, f32[1024,768]{1,0:T(8,128)}, bf16[1024,768]{1,0:T(8,128)(2,1)}, f32[8,768]{1,0:T(8,128)}, bf16[384,6912]{1,0:T(8,128)(2,1)}, /*index=5*/bf16[384,6912]{1,0:T(8,128)(2,1)}) custom-call(s32[1]{0:T(128)} %bitcast.odd_ref.refs_0_, f32[1024,768]{1,0:T(8,128)} %copy-done.18, bf16[1024,768]{1,0:T(8,128)(2,1)} %copy-done.24, ...), custom_call_target="tpu_custom_call" | custom-call | flops 63800000512 | tf_op jit(solution)/shard_map/feed_forward/pallas_call | solution.py:1036
  247.4 18.5 %cross_backward.3 = (bf16[1024,768]{1,0:T(8,128)(2,1)}, bf16[32,128,768]{2,1,0:T(8,128)(2,1)}, bf16[32,128,768]{2,1,0:T(8,128)(2,1)}) custom-call(s32[32]{0:T(128)} %copy-done.8, s32[32]{0:T(128)} %refs_1_.5, bf16[1024,768]{1,0:T(8,128)(2,1)} %copy-done.22, bf16[1024,768]{1,0:T(8,128)(2,1)} %get-tuple-element.236.refs_3_, bf16[32,128,1536]{2,1,0:T(8,128)(2,1)} %bitcast.113, ...), custom_call_target="tpu_custom_call" | custom-call | flops 52800000000 | tf_op jit(solution)/shard_map/cross_backward/pallas_call | solution.py:390
  265.9 7.2 %fold_blocks.12 = (bf16[8,24,6912]{2,1,0:T(8,128)(2,1)}, bf16[8,24,6912]{2,1,0:T(8,128)(2,1)S(1)}) custom-call(s32[8]{0:T(128)S(1)} %get-tuple-element.335.sent_places, s32[8]{0:T(128)S(1)} %get-tuple-element.334.kept_places, bf16[16,24,6912]{2,1,0:T(8,128)(2,1)S(1)} %bitcast.59, bf16[16,24,6912]{2,1,0:T(8,128)(2,1)} %collective-permute-done.25.refs_1_.refs_3_, ...), custom_call_target="tpu_custom_call" | custom-call | tf_op jit(solution)/shard_map/fold_blocks/pallas_call | solution.py:592
  273.1 1.4 collective-permute-start.26
  274.5 18.4 %cross_backward.4 = (bf16[1024,768]{1,0:T(8,128)(2,1)}, bf16[32,128,768]{2,1,0:T(8,128)(2,1)}, bf16[32,128,768]{2,1,0:T(8,128)(2,1)}) custom-call(s32[32]{0:T(128)} %copy-done.8, s32[32]{0:T(128)} %refs_1_.5, bf16[1024,768]{1,0:T(8,128)(2,1)} %copy-done.22, ...), custom_call_target="tpu_custom_call", output_to_operand_aliasing={{0}: (8, {}), {1}: (9, {}), {2}: (10, {})} | custom-call | flops 52800000000 | tf_op jit(solution)/shard_map/cross_backward/pallas_call | solution.py:390
  292.9 18.1 %cross_backward.5 = (bf16[1024,768]{1,0:T(8,128)(2,1)}, bf16[32,128,768]{2,1,0:T(8,128)(2,1)}, bf16[32,128,768]{2,1,0:T(8,128)(2,1)}) custom-call(s32[32]{0:T(128)} %copy-done.8, s32[32]{0:T(128)} %refs_1_.5, bf16[1024,768]{1,0:T(8,128)(2,1)} %copy-done.22, ...), custom_call_target="tpu_custom_call", output_to_operand_aliasing={{0}: (8, {}), {1}: (9, {}), {2}: (10, {})} | custom-call | flops 52800000000 | tf_op jit(solution)/shard_map/cross_backward/pallas_call | solution.py:390
  313.0 15.2 %keyval_terms.1 = (bf16[384,1536]{1,0:T(8,128)(2,1)S(1)}, bf16[384,1536]{1,0:T(8,128)(2,1)S(1)}) custom-call(s32[1]{0:T(128)} %bitcast.odd_ref.refs_0_, bf16[4096,768]{1,0:T(8,128)(2,1)} %bitcast.73, bf16[4096,768]{1,0:T(8,128)(2,1)} %bitcast.88, bf16[4096,768]{1,0:T(8,128)(2,1)} %bitcast.126), custom_call_target="tpu_custom_call" | custom-call | flops 16499999744 | tf_op jit(solution)/shard_map/keyval_terms/pallas_call | solution.py:1300
  328.1 1.9 collective-permute-done.27.refs_1_.refs_3_
  331.0 1.5 collective-permute-start.28
  332.5 14.0 %second_back.1 = (f32[1024,768]{1,0:T(8,128)}, bf16[1024,768]{1,0:T(8,128)(2,1)S(1)}, f32[8,768]{1,0:T(8,128)S(1)}, bf16[384,1536]{1,0:T(8,128)(2,1)S(1)}, bf16[384,1536]{1,0:T(8,128)(2,1)S(1)}) custom-call(s32[1]{0:T(128)} %bitcast.odd_ref.refs_0_, f32[1024,768]{1,0:T(8,128)} %copy-done.18, f32[1024,768]{1,0:T(8,128)} %get-tuple-element.231.grad_in_ref, ...), custom_call_target="tpu_custom_call" | custom-call | flops 15399999488 | tf_op jit(solution)/shard_map/second_back/pallas_call | solution.py:1129
  346.6 1.7 pad_maximum_fusion.3
  349.3 13.8 %self_backward.2.refs_7_ = bf16[3,1024,768]{2,1,0:T(8,128)(2,1)} custom-call(s32[1]{0:T(128)S(6)} %copy.95.length_ref.refs_0_, bf16[1024,2304]{1,0:T(8,128)(2,1)} %copy-done.17, bf16[1024,2304]{1,0:T(8,128)(2,1)} %copy-done.17, bf16[1024,2304]{1,0:T(8,128)(2,1)} %copy-done.17, bf16[1024,768]{1,0:T(8,128)(2,1)S(1)} %get-tuple-element.279.refs_4_, ...), custom_call_target="tpu_custom_call" | custom-call | flops 27499999232 | tf_op jit(solution)/shard_map/self_backward/pallas_call | solution.py:235
  365.3 1.3 collective-permute-start.31
  366.6 13.6 %self_backward.3.projected_grad_ref = bf16[3,1024,768]{2,1,0:T(8,128)(2,1)} custom-call(s32[1]{0:T(128)S(6)} %copy.95.length_ref.refs_0_, bf16[1024,2304]{1,0:T(8,128)(2,1)} %copy-done.17, bf16[1024,2304]{1,0:T(8,128)(2,1)} %copy-done.17, bf16[1024,2304]{1,0:T(8,128)(2,1)} %copy-done.17, ...), custom_call_target="tpu_custom_call", output_to_operand_aliasing={{}: (7, {})} | custom-call | flops 27499999232 | tf_op jit(solution)/shard_map/self_backward/pallas_call | solution.py:235
  380.2 1.3 collective-permute-done.31.refs_1_.refs_3_
  383.3 18.7 %first_back.1 = (f32[1024,768]{1,0:T(8,128)}, bf16[384,2432]{1,0:T(8,128)(2,1)}, bf16[384,2432]{1,0:T(8,128)(2,1)}) custom-call(s32[1]{0:T(128)} %bitcast.odd_ref.refs_0_, bf16[1024,768]{1,0:T(8,128)(2,1)} %bitcast.82, f32[1024,768]{1,0:T(8,128)} %get-tuple-element.263.grad_in_ref, bf16[3,1024,768]{2,1,0:T(8,128)(2,1)} %self_backward.3.projected_grad_ref, ...), custom_call_target="tpu_custom_call" | custom-call | flops 19800000512 | tf_op jit(solution)/shard_map/first_back/pallas_call | solution.py:1228
  402.0 1.6 collective-permute-start.33
  403.6 8.4 %collective-permute-done.33.refs_1_.refs_3_ = bf16[4,24,3072]{2,1,0:T(8,128)(2,1)S(1)} collective-permute-done((bf16[4,24,3072]{2,1,0:T(8,128)(2,1)S(1)}, bf16[4,24,3072]{2,1,0:T(8,128)(2,1)S(1)}, u32[]{:S(2)}, u32[]{:S(2)}) %collective-permute-start.33) | collective-permute-done | bytes 589856 | tf_op jit(solution)/shard_map/ppermute | solution.py:472
  415.9 8.9 %neighbours_back.2.refs_5_ = f32[4096,768]{1,0:T(8,128)} custom-call(s32[1]{0:T(128)} %bitcast.odd_ref.refs_0_, bf16[4096,768]{1,0:T(8,128)(2,1)S(1)} %bitcast.91, bf16[4096,768]{1,0:T(8,128)(2,1)} %bitcast.127, bf16[384,1536]{1,0:T(8,128)(2,1)S(1)} %bitcast.71, bf16[384,1536]{1,0:T(8,128)(2,1)S(1)} %bitcast.86), custom_call_target="tpu_custom_call" | custom-call | flops 16499999744 | tf_op jit(solution)/shard_map/neighbours_back/pallas_call | solution.py:1334
  424.7 3.8 collective-permute-done.35.refs_1_.refs_3_
  429.6 1.4 collective-permute-start.36
  431.1 8.8 %neighbours_back.3 = f32[4096,768]{1,0:T(8,128)} custom-call(s32[1]{0:T(128)} %bitcast.odd_ref.refs_0_, bf16[4096,768]{1,0:T(8,128)(2,1)S(1)} %bitcast.92, bf16[4096,768]{1,0:T(8,128)(2,1)} %bitcast.128, bf16[384,1536]{1,0:T(8,128)(2,1)S(1)} %bitcast.72, bf16[384,1536]{1,0:T(8,128)(2,1)S(1)} %bitcast.87, ...), custom_call_target="tpu_custom_call", output_to_operand_aliasing={{}: (5, {})} | custom-call | flops 16499999744 | tf_op jit(solution)/shard_map/neighbours_back/pallas_call | solution.py:1334
  441.0 1.9 collective-permute-start.38
  445.6 2.4 copy.69
  448.0 4.0 reshape.158
  455.1 3.0 collective-permute-done.39
  (205 shorter events, 37.9 us)
Async XLA Ops:
  0.6 10.5 %collective-permute-start.1 = (bf16[1,24,1536]{2,1,0:T(8,128)(2,1)}, bf16[1,24,1536]{2,1,0:T(8,128)(2,1)S(1)}, u32[]{:S(2)}, u32[]{:S(2)}) collective-permute-start(bf16[1,24,1536]{2,1,0:T(8,128)(2,1)} %bitcast.99), channel_id=1, source_target_pairs={{0,2},{1,3},{2,0},{3,1},{4,6},{5,7},{6,4},{7,5},{8,10},{9,11},{10,... | collective-permute-start | bytes 221192 | tf_op jit(solution)/shard_map/ppermute | solution.py:472
  5.5 15.1 %collective-permute-start = (bf16[1,24,2432]{2,1,0:T(8,128)(2,1)S(1)}, bf16[1,24,2432]{2,1,0:T(8,128)(2,1)S(1)}, u32[]{:S(2)}, u32[]{:S(2)}) collective-permute-start(bf16[1,24,2432]{2,1,0:T(8,128)(2,1)S(1)} %fusion.2), channel_id=1, source_target_pairs={{0,2},{1,3},{2,0},{3,1},{4,6},{5,7},{6,4},{7,5},{8,10},{9,11},{10,... | collective-permute-start | bytes 350216 | tf_op jit(solution)/shard_map/ppermute | solution.py:472
  7.3 3.7 copy-start.33
  7.3 3.7 copy-start.34
  11.2 9.4 %collective-permute-start.2 = (bf16[2,24,1536]{2,1,0:T(8,128)(2,1)S(1)}, bf16[2,24,1536]{2,1,0:T(8,128)(2,1)S(1)}, u32[]{:S(2)}, u32[]{:S(2)}) collective-permute-start(bf16[2,24,1536]{2,1,0:T(8,128)(2,1)S(1)} %pad_maximum_fusion.7), channel_id=1, source_target_pairs={{0,4},{1,5},{2,6},{3,7},{4,0},{5,1},{6,2},{7,3},{8,12},{9,13},{10,... | collective-permute-start | bytes 442376 | tf_op jit(solution)/shard_map/ppermute | solution.py:472
  20.7 29.7 %collective-permute-start.5 = (bf16[1,24,2304]{2,1,0:T(8,128)(2,1)S(1)}, bf16[1,24,2304]{2,1,0:T(8,128)(2,1)S(1)}, u32[]{:S(2)}, u32[]{:S(2)}) collective-permute-start(bf16[1,24,2304]{2,1,0:T(8,128)(2,1)S(1)} %maximum_bitcast_fusion), channel_id=1, source_target_pairs={{0,2},{1,3},{2,0},{3,1},{4,6},{5,7},{6,4},{7,5},{8,10},{9,11},{10,... | collective-permute-start | bytes 331784 | tf_op jit(solution)/shard_map/ppermute | solution.py:472
  21.5 14.1 %collective-permute-start.6 = (bf16[2,24,2432]{2,1,0:T(8,128)(2,1)S(1)}, bf16[2,24,2432]{2,1,0:T(8,128)(2,1)S(1)}, u32[]{:S(2)}, u32[]{:S(2)}) collective-permute-start(bf16[2,24,2432]{2,1,0:T(8,128)(2,1)S(1)} %constant_dynamic-update-slice_fusion.2), channel_id=1, source_target_pairs={{0,4},{1,5},{2,6},{3,7},{4,0},{5,1},{6,2},{7,3},{8,12},{9,13},{10,... | collective-permute-start | bytes 700424 | tf_op jit(solution)/shard_map/ppermute | solution.py:472
  24.9 6.7 %collective-permute-start.7 = (bf16[4,24,1536]{2,1,0:T(8,128)(2,1)S(1)}, bf16[4,24,1536]{2,1,0:T(8,128)(2,1)S(1)}, u32[]{:S(2)}, u32[]{:S(2)}) collective-permute-start(bf16[4,24,1536]{2,1,0:T(8,128)(2,1)S(1)} %constant_dynamic-update-slice_fusion), channel_id=1, source_target_pairs={{0,1},{1,0},{2,3},{3,2},{4,5},{5,4},{6,7},{7,6},{8,24},{9,25},{10,... | collective-permute-start | bytes 884744 | tf_op jit(solution)/shard_map/ppermute | solution.py:472
  26.5 41.1 %collective-permute-start.4 = (bf16[1,24,3072]{2,1,0:T(8,128)(2,1)S(1)}, bf16[1,24,3072]{2,1,0:T(8,128)(2,1)S(1)}, u32[]{:S(2)}, u32[]{:S(2)}) collective-permute-start(bf16[1,24,3072]{2,1,0:T(8,128)(2,1)S(1)} %broadcast_in_dim_reshape.7), channel_id=1, source_target_pairs={{0,2},{1,3},{2,0},{3,1},{4,6},{5,7},{6,4},{7,5},{8,10},{9,11},{10,... | collective-permute-start | bytes 442376 | tf_op jit(solution)/shard_map/ppermute | solution.py:472
  26.6 58.6 %collective-permute-start.3 = (bf16[1,24,3072]{2,1,0:T(8,128)(2,1)S(1)}, bf16[1,24,3072]{2,1,0:T(8,128)(2,1)S(1)}, u32[]{:S(2)}, u32[]{:S(2)}) collective-permute-start(bf16[1,24,3072]{2,1,0:T(8,128)(2,1)S(1)} %broadcast_in_dim_reshape.6), channel_id=1, source_target_pairs={{0,2},{1,3},{2,0},{3,1},{4,6},{5,7},{6,4},{7,5},{8,10},{9,11},{10,... | collective-permute-start | bytes 442376 | tf_op jit(solution)/shard_map/ppermute | solution.py:472
  31.7 14.1 %collective-permute-start.9 = (bf16[8,24,1536]{2,1,0:T(8,128)(2,1)S(1)}, bf16[8,24,1536]{2,1,0:T(8,128)(2,1)S(1)}, u32[]{:S(2)}, u32[]{:S(2)}) collective-permute-start(bf16[8,24,1536]{2,1,0:T(8,128)(2,1)S(1)} %constant_dynamic-update-slice_fusion.4), channel_id=1, source_target_pairs={{0,16},{1,17},{2,18},{3,19},{4,20},{5,21},{6,22},{7,23},{8,9},{9,8... | collective-permute-start | bytes 1769480 | tf_op jit(solution)/shard_map/ppermute | solution.py:472
  35.6 13.0 %collective-permute-start.8 = (bf16[4,24,2432]{2,1,0:T(8,128)(2,1)S(1)}, bf16[4,24,2432]{2,1,0:T(8,128)(2,1)S(1)}, u32[]{:S(2)}, u32[]{:S(2)}) collective-permute-start(bf16[4,24,2432]{2,1,0:T(8,128)(2,1)S(1)} %constant_dynamic-update-slice_fusion.6), channel_id=1, source_target_pairs={{0,1},{1,0},{2,3},{3,2},{4,5},{5,4},{6,7},{7,6},{8,24},{9,25},{10,... | collective-permute-start | bytes 1400840 | tf_op jit(solution)/shard_map/ppermute | solution.py:472
  45.9 22.4 %slice-start.2 = ((s8[6291456]{0:T(1024)(128)(4,1)}), s8[4194304]{0:T(1024)(128)(4,1)S(1)}, s32[]{:S(2)}) async-start(s8[6291456]{0:T(1024)(128)(4,1)} %bitcast.74), calls=%async_computation.2 | async-start | bytes 8388608
  48.6 19.7 %copy-start.6 = (bf16[16,24,1536]{2,1,0:T(8,128)(2,1)}, bf16[16,24,1536]{2,1,0:T(8,128)(2,1)S(1)}, u32[]{:S(2)}) copy-start(bf16[16,24,1536]{2,1,0:T(8,128)(2,1)S(1)} %reorder_blocks.5) | copy-start | bytes 3538948
  48.7 13.6 %collective-permute-start.11 = (bf16[8,24,2432]{2,1,0:T(8,128)(2,1)S(1)}, bf16[8,24,2432]{2,1,0:T(8,128)(2,1)S(1)}, u32[]{:S(2)}, u32[]{:S(2)}) collective-permute-start(bf16[8,24,2432]{2,1,0:T(8,128)(2,1)S(1)} %constant_dynamic-update-slice_fusion.8), channel_id=1, source_target_pairs={{0,16},{1,17},{2,18},{3,19},{4,20},{5,21},{6,22},{7,23},{8,9},{9,8... | collective-permute-start | bytes 2801672 | tf_op jit(solution)/shard_map/ppermute | solution.py:472
  50.3 18.0 %collective-permute-start.15 = (bf16[16,24,1536]{2,1,0:T(8,128)(2,1)S(1)}, bf16[16,24,1536]{2,1,0:T(8,128)(2,1)S(1)}, u32[]{:S(2)}, u32[]{:S(2)}) collective-permute-start(bf16[16,24,1536]{2,1,0:T(8,128)(2,1)S(1)} %reorder_blocks.5), channel_id=1, source_target_pairs={{0,8},{1,9},{2,10},{3,11},{4,12},{5,13},{6,14},{7,15},{8,0},{9,1},... | collective-permute-start | bytes 3538952 | tf_op jit(solution)/shard_map/ppermute | solution.py:472
  50.4 15.5 %collective-permute-start.10 = (bf16[2,24,2304]{2,1,0:T(8,128)(2,1)S(1)}, bf16[2,24,2304]{2,1,0:T(8,128)(2,1)S(1)}, u32[]{:S(2)}, u32[]{:S(2)}) collective-permute-start(bf16[2,24,2304]{2,1,0:T(8,128)(2,1)S(1)} %constant_dynamic-update-slice_fusion.10), channel_id=1, source_target_pairs={{0,4},{1,5},{2,6},{3,7},{4,0},{5,1},{6,2},{7,3},{8,12},{9,13},{10,... | collective-permute-start | bytes 663560 | tf_op jit(solution)/shard_map/ppermute | solution.py:472
  51.1 17.3 %slice-start.3 = ((s8[6291456]{0:T(1024)(128)(4,1)}), s8[2097152]{0:T(1024)(128)(4,1)S(1)}, s32[]{:S(2)}) async-start(s8[6291456]{0:T(1024)(128)(4,1)} %bitcast.74), calls=%async_computation.3 | async-start | bytes 4194304
  65.8 20.1 %copy-start.3 = (bf16[16,24,2432]{2,1,0:T(8,128)(2,1)}, bf16[16,24,2432]{2,1,0:T(8,128)(2,1)S(1)}, u32[]{:S(2)}) copy-start(bf16[16,24,2432]{2,1,0:T(8,128)(2,1)S(1)} %reorder_blocks.6) | copy-start | bytes 5603332
  65.8 15.4 %collective-permute-start.14 = (bf16[16,24,2432]{2,1,0:T(8,128)(2,1)S(1)}, bf16[16,24,2432]{2,1,0:T(8,128)(2,1)S(1)}, u32[]{:S(2)}, u32[]{:S(2)}) collective-permute-start(bf16[16,24,2432]{2,1,0:T(8,128)(2,1)S(1)} %reorder_blocks.6), channel_id=1, source_target_pairs={{0,8},{1,9},{2,10},{3,11},{4,12},{5,13},{6,14},{7,15},{8,0},{9,1},... | collective-permute-start | bytes 5603336 | tf_op jit(solution)/shard_map/ppermute | solution.py:472
  66.0 15.4 %collective-permute-start.13 = (bf16[4,24,2304]{2,1,0:T(8,128)(2,1)S(1)}, bf16[4,24,2304]{2,1,0:T(8,128)(2,1)S(1)}, u32[]{:S(2)}, u32[]{:S(2)}) collective-permute-start(bf16[4,24,2304]{2,1,0:T(8,128)(2,1)S(1)} %constant_dynamic-update-slice_fusion.12), channel_id=1, source_target_pairs={{0,1},{1,0},{2,3},{3,2},{4,5},{5,4},{6,7},{7,6},{8,24},{9,25},{10,... | collective-permute-start | bytes 1327112 | tf_op jit(solution)/shard_map/ppermute | solution.py:472
  67.6 16.2 %collective-permute-start.12 = (bf16[2,24,3072]{2,1,0:T(8,128)(2,1)S(1)}, bf16[2,24,3072]{2,1,0:T(8,128)(2,1)S(1)}, u32[]{:S(2)}, u32[]{:S(2)}) collective-permute-start(bf16[2,24,3072]{2,1,0:T(8,128)(2,1)S(1)} %constant_dynamic-update-slice_fusion.14), channel_id=1, source_target_pairs={{0,4},{1,5},{2,6},{3,7},{4,0},{5,1},{6,2},{7,3},{8,12},{9,13},{10,... | collective-permute-start | bytes 884744 | tf_op jit(solution)/shard_map/ppermute | solution.py:472
  68.3 13.0 %copy-start.14 = (bf16[16,24,1536]{2,1,0:T(8,128)(2,1)}, bf16[16,24,1536]{2,1,0:T(8,128)(2,1)S(1)}, u32[]{:S(2)}) copy-start(bf16[16,24,1536]{2,1,0:T(8,128)(2,1)S(1)} %collective-permute-done.15) | copy-start | bytes 3538948
  81.3 4.7 %copy-start.12 = (bf16[1,1024,768]{2,1,0:T(8,128)(2,1)S(1)}, bf16[1,1024,768]{2,1,0:T(8,128)(2,1)}, u32[]{:S(2)}) copy-start(bf16[1,1024,768]{2,1,0:T(8,128)(2,1)} %param.19) | copy-start | bytes 4718596
  81.3 10.4 %copy-start.9 = (bf16[16,24,2432]{2,1,0:T(8,128)(2,1)}, bf16[16,24,2432]{2,1,0:T(8,128)(2,1)S(1)}, u32[]{:S(2)}) copy-start(bf16[16,24,2432]{2,1,0:T(8,128)(2,1)S(1)} %collective-permute-done.14) | copy-start | bytes 5603332
  81.4 19.4 %collective-permute-start.18 = (bf16[8,24,2304]{2,1,0:T(8,128)(2,1)S(1)}, bf16[8,24,2304]{2,1,0:T(8,128)(2,1)S(1)}, u32[]{:S(2)}, u32[]{:S(2)}) collective-permute-start(bf16[8,24,2304]{2,1,0:T(8,128)(2,1)S(1)} %constant_dynamic-update-slice_fusion.16), channel_id=1, source_target_pairs={{0,16},{1,17},{2,18},{3,19},{4,20},{5,21},{6,22},{7,23},{8,9},{9,8... | collective-permute-start | bytes 2654216 | tf_op jit(solution)/shard_map/ppermute | solution.py:472
  83.8 20.6 %collective-permute-start.17 = (bf16[4,24,3072]{2,1,0:T(8,128)(2,1)S(1)}, bf16[4,24,3072]{2,1,0:T(8,128)(2,1)S(1)}, u32[]{:S(2)}, u32[]{:S(2)}) collective-permute-start(bf16[4,24,3072]{2,1,0:T(8,128)(2,1)S(1)} %constant_dynamic-update-slice_fusion.18), channel_id=1, source_target_pairs={{0,1},{1,0},{2,3},{3,2},{4,5},{5,4},{6,7},{7,6},{8,24},{9,25},{10,... | collective-permute-start | bytes 1769480 | tf_op jit(solution)/shard_map/ppermute | solution.py:472
  85.2 20.8 %collective-permute-start.16 = (bf16[2,24,3072]{2,1,0:T(8,128)(2,1)S(1)}, bf16[2,24,3072]{2,1,0:T(8,128)(2,1)S(1)}, u32[]{:S(2)}, u32[]{:S(2)}) collective-permute-start(bf16[2,24,3072]{2,1,0:T(8,128)(2,1)S(1)} %constant_dynamic-update-slice_fusion.20), channel_id=1, source_target_pairs={{0,4},{1,5},{2,6},{3,7},{4,0},{5,1},{6,2},{7,3},{8,12},{9,13},{10,... | collective-permute-start | bytes 884744 | tf_op jit(solution)/shard_map/ppermute | solution.py:472
  93.8 7.1 %copy-start.23 = (bf16[1024,768]{1,0:T(8,128)(2,1)}, bf16[1024,768]{1,0:T(8,128)(2,1)S(1)}, u32[]{:S(2)}) copy-start(bf16[1024,768]{1,0:T(8,128)(2,1)S(1)} %get-tuple-element.206.first_in_ref) | copy-start | bytes 4718596
  93.8 53.7 %copy-start.28 = (f32[8,768]{1,0:T(8,128)}, f32[8,768]{1,0:T(8,128)S(1)}, u32[]{:S(2)}) copy-start(f32[8,768]{1,0:T(8,128)S(1)} %get-tuple-element.221.vectors_ref) | copy-start | bytes 73732
  104.4 23.7 %copy-start.4 = (bf16[16,24,2304]{2,1,0:T(8,128)(2,1)}, bf16[16,24,2304]{2,1,0:T(8,128)(2,1)S(1)}, u32[]{:S(2)}) copy-start(bf16[16,24,2304]{2,1,0:T(8,128)(2,1)S(1)} %reorder_blocks.7) | copy-start | bytes 5308420
  104.4 25.4 %collective-permute-start.21 = (bf16[16,24,2304]{2,1,0:T(8,128)(2,1)S(1)}, bf16[16,24,2304]{2,1,0:T(8,128)(2,1)S(1)}, u32[]{:S(2)}, u32[]{:S(2)}) collective-permute-start(bf16[16,24,2304]{2,1,0:T(8,128)(2,1)S(1)} %reorder_blocks.7), channel_id=1, source_target_pairs={{0,8},{1,9},{2,10},{3,11},{4,12},{5,13},{6,14},{7,15},{8,0},{9,1},... | collective-permute-start | bytes 5308424 | tf_op jit(solution)/shard_map/ppermute | solution.py:472
  104.5 25.3 %collective-permute-start.20 = (bf16[8,24,3072]{2,1,0:T(8,128)(2,1)S(1)}, bf16[8,24,3072]{2,1,0:T(8,128)(2,1)S(1)}, u32[]{:S(2)}, u32[]{:S(2)}) collective-permute-start(bf16[8,24,3072]{2,1,0:T(8,128)(2,1)S(1)} %constant_dynamic-update-slice_fusion.22), channel_id=1, source_target_pairs={{0,16},{1,17},{2,18},{3,19},{4,20},{5,21},{6,22},{7,23},{8,9},{9,8... | collective-permute-start | bytes 3538952 | tf_op jit(solution)/shard_map/ppermute | solution.py:472
  131.6 4.8 %copy-start.36 = (s32[1,16,2]{1,2,0:T(2,128)S(1)}, s32[1,16,2]{1,2,0:T(2,128)}, u32[]{:S(2)}) copy-start(s32[1,16,2]{1,2,0:T(2,128)} %param.22) | copy-start | bytes 388
  135.5 21.9 %copy-start.1 = (bf16[16,24,3072]{2,1,0:T(8,128)(2,1)}, bf16[16,24,3072]{2,1,0:T(8,128)(2,1)S(1)}, u32[]{:S(2)}) copy-start(bf16[16,24,3072]{2,1,0:T(8,128)(2,1)S(1)} %reorder_blocks.8) | copy-start | bytes 7077892
  135.6 24.7 %collective-permute-start.22 = (bf16[16,24,3072]{2,1,0:T(8,128)(2,1)S(1)}, bf16[16,24,3072]{2,1,0:T(8,128)(2,1)}, u32[]{:S(2)}, u32[]{:S(2)}) collective-permute-start(bf16[16,24,3072]{2,1,0:T(8,128)(2,1)S(1)} %reorder_blocks.8), channel_id=1, source_target_pairs={{0,8},{1,9},{2,10},{3,11},{4,12},{5,13},{6,14},{7,15},{8,0},{9,1},... | collective-permute-start | bytes 7077896 | tf_op jit(solution)/shard_map/ppermute | solution.py:472
  135.6 10.1 %collective-permute-start.19 = (bf16[4,24,3072]{2,1,0:T(8,128)(2,1)S(1)}, bf16[4,24,3072]{2,1,0:T(8,128)(2,1)}, u32[]{:S(2)}, u32[]{:S(2)}) collective-permute-start(bf16[4,24,3072]{2,1,0:T(8,128)(2,1)S(1)} %constant_dynamic-update-slice_fusion.24), channel_id=1, source_target_pairs={{0,1},{1,0},{2,3},{3,2},{4,5},{5,4},{6,7},{7,6},{8,24},{9,25},{10,... | collective-permute-start | bytes 1769480 | tf_op jit(solution)/shard_map/ppermute | solution.py:472
  136.5 23.8 %copy-start.8 = (s32[32]{0:T(128)}, s32[32]{0:T(128)S(1)}, u32[]{:S(2)}) copy-start(s32[32]{0:T(128)S(1)} %reshape.139.ids_ref.refs_0_) | copy-start | bytes 388
  136.5 10.9 %copy-start.5 = (bf16[16,24,2304]{2,1,0:T(8,128)(2,1)S(1)}, bf16[16,24,2304]{2,1,0:T(8,128)(2,1)}, u32[]{:S(2)}) copy-start(bf16[16,24,2304]{2,1,0:T(8,128)(2,1)} %copy-done.4) | copy-start | bytes 5308420
  146.8 30.7 %collective-permute-start.23 = (bf16[8,24,3072]{2,1,0:T(8,128)(2,1)S(1)}, bf16[8,24,3072]{2,1,0:T(8,128)(2,1)S(1)}, u32[]{:S(2)}, u32[]{:S(2)}) collective-permute-start(bf16[8,24,3072]{2,1,0:T(8,128)(2,1)S(1)} %constant_dynamic-update-slice_fusion.26), channel_id=1, source_target_pairs={{0,16},{1,17},{2,18},{3,19},{4,20},{5,21},{6,22},{7,23},{8,9},{9,8... | collective-permute-start | bytes 3538952 | tf_op jit(solution)/shard_map/ppermute | solution.py:472
  151.8 8.5 %copy-start.16 = (s32[32]{0:T(128)S(1)}, s32[32]{0:T(128)}, u32[]{:S(2)}) copy-start(s32[32]{0:T(128)} %refs_1_.5) | copy-start | bytes 388
  160.3 17.2 %copy-start.22 = (bf16[1024,768]{1,0:T(8,128)(2,1)}, bf16[1024,768]{1,0:T(8,128)(2,1)S(1)}, u32[]{:S(2)}) copy-start(bf16[1024,768]{1,0:T(8,128)(2,1)S(1)} %get-tuple-element.245.query_ref.refs_2_) | copy-start | bytes 4718596
  182.6 6.0 %copy-start.2 = (bf16[16,24,3072]{2,1,0:T(8,128)(2,1)}, bf16[16,24,3072]{2,1,0:T(8,128)(2,1)S(1)}, u32[]{:S(2)}) copy-start(bf16[16,24,3072]{2,1,0:T(8,128)(2,1)S(1)} %reorder_blocks.9) | copy-start | bytes 7077892
  182.6 4.6 %collective-permute-start.24 = (bf16[16,24,3072]{2,1,0:T(8,128)(2,1)S(1)}, bf16[16,24,3072]{2,1,0:T(8,128)(2,1)S(1)}, u32[]{:S(2)}, u32[]{:S(2)}) collective-permute-start(bf16[16,24,3072]{2,1,0:T(8,128)(2,1)S(1)} %reorder_blocks.9), channel_id=1, source_target_pairs={{0,8},{1,9},{2,10},{3,11},{4,12},{5,13},{6,14},{7,15},{8,0},{9,1},... | collective-permute-start | bytes 7077896 | tf_op jit(solution)/shard_map/ppermute | solution.py:472
  247.2 18.7 %collective-permute-start.25 = (bf16[16,24,6912]{2,1,0:T(8,128)(2,1)}, bf16[16,24,6912]{2,1,0:T(8,128)(2,1)}, u32[]{:S(2)}, u32[]{:S(2)}) collective-permute-start(bf16[16,24,6912]{2,1,0:T(8,128)(2,1)} %bitcast.107), channel_id=1, source_target_pairs={{0,8},{1,9},{2,10},{3,11},{4,12},{5,13},{6,14},{7,15},{8,0},{9,1},... | collective-permute-start | bytes 15925256 | tf_op jit(solution)/shard_map/ppermute | solution.py:472
  247.4 18.5 %slice-start = ((s8[5308416]{0:T(1024)(128)(4,1)}), s8[4194304]{0:T(1024)(128)(4,1)S(1)}, s32[]{:S(2)}) async-start(s8[5308416]{0:T(1024)(128)(4,1)} %bitcast.57), calls=%async_computation | async-start | bytes 8388608
  247.4 18.5 %slice-start.1 = ((s8[5308416]{0:T(1024)(128)(4,1)}), s8[1114112]{0:T(1024)(128)(4,1)S(1)}, s32[]{:S(2)}) async-start(s8[5308416]{0:T(1024)(128)(4,1)} %bitcast.57), calls=%async_computation.1 | async-start | bytes 2228224
  273.1 37.9 %collective-permute-start.26 = (bf16[8,24,6912]{2,1,0:T(8,128)(2,1)}, bf16[8,24,6912]{2,1,0:T(8,128)(2,1)S(1)}, u32[]{:S(2)}, u32[]{:S(2)}) collective-permute-start(bf16[8,24,6912]{2,1,0:T(8,128)(2,1)} %get-tuple-element.240), channel_id=1, source_target_pairs={{0,16},{1,17},{2,18},{3,19},{4,20},{5,21},{6,22},{7,23},{8,9},{9,8... | collective-permute-start | bytes 7962632 | tf_op jit(solution)/shard_map/ppermute | solution.py:472
  312.2 17.8 %collective-permute-start.27 = (bf16[4,24,6912]{2,1,0:T(8,128)(2,1)S(1)}, bf16[4,24,6912]{2,1,0:T(8,128)(2,1)S(1)}, u32[]{:S(2)}, u32[]{:S(2)}) collective-permute-start(bf16[4,24,6912]{2,1,0:T(8,128)(2,1)S(1)} %get-tuple-element.253), channel_id=1, source_target_pairs={{0,1},{1,0},{2,3},{3,2},{4,5},{5,4},{6,7},{7,6},{8,24},{9,25},{10,... | collective-permute-start | bytes 3981320 | tf_op jit(solution)/shard_map/ppermute | solution.py:472
  331.0 33.7 %collective-permute-start.28 = (bf16[2,24,6912]{2,1,0:T(8,128)(2,1)S(1)}, bf16[2,24,6912]{2,1,0:T(8,128)(2,1)S(1)}, u32[]{:S(2)}, u32[]{:S(2)}) collective-permute-start(bf16[2,24,6912]{2,1,0:T(8,128)(2,1)S(1)} %get-tuple-element.260), channel_id=1, source_target_pairs={{0,4},{1,5},{2,6},{3,7},{4,0},{5,1},{6,2},{7,3},{8,12},{9,13},{10,... | collective-permute-start | bytes 1990664 | tf_op jit(solution)/shard_map/ppermute | solution.py:472
  348.3 15.1 %collective-permute-start.29 = (bf16[16,24,3072]{2,1,0:T(8,128)(2,1)}, bf16[16,24,3072]{2,1,0:T(8,128)(2,1)S(1)}, u32[]{:S(2)}, u32[]{:S(2)}) collective-permute-start(bf16[16,24,3072]{2,1,0:T(8,128)(2,1)} %bitcast.35), channel_id=1, source_target_pairs={{0,8},{1,9},{2,10},{3,11},{4,12},{5,13},{6,14},{7,15},{8,0},{9,1},... | collective-permute-start | bytes 7077896 | tf_op jit(solution)/shard_map/ppermute | solution.py:472
  364.9 17.5 %collective-permute-start.30 = (bf16[1,24,6912]{2,1,0:T(8,128)(2,1)S(1)}, bf16[1,24,6912]{2,1,0:T(8,128)(2,1)S(1)}, u32[]{:S(2)}, u32[]{:S(2)}) collective-permute-start(bf16[1,24,6912]{2,1,0:T(8,128)(2,1)S(1)} %get-tuple-element.278), channel_id=1, source_target_pairs={{0,2},{1,3},{2,0},{3,1},{4,6},{5,7},{6,4},{7,5},{8,10},{9,11},{10,... | collective-permute-start | bytes 995336 | tf_op jit(solution)/shard_map/ppermute | solution.py:472
  365.3 16.2 %collective-permute-start.31 = (bf16[8,24,3072]{2,1,0:T(8,128)(2,1)S(1)}, bf16[8,24,3072]{2,1,0:T(8,128)(2,1)S(1)}, u32[]{:S(2)}, u32[]{:S(2)}) collective-permute-start(bf16[8,24,3072]{2,1,0:T(8,128)(2,1)S(1)} %get-tuple-element.275), channel_id=1, source_target_pairs={{0,16},{1,17},{2,18},{3,19},{4,20},{5,21},{6,22},{7,23},{8,9},{9,8... | collective-permute-start | bytes 3538952 | tf_op jit(solution)/shard_map/ppermute | solution.py:472
  381.5 34.4 %slice-start.4 = ((s8[6291456]{0:T(1024)(128)(4,1)}), s8[4194304]{0:T(1024)(128)(4,1)S(1)}, s32[]{:S(2)}) async-start(s8[6291456]{0:T(1024)(128)(4,1)} %bitcast.89), calls=%async_computation.4 | async-start | bytes 8388608
  383.3 32.6 %slice-start.5 = ((s8[6291456]{0:T(1024)(128)(4,1)}), s8[2097152]{0:T(1024)(128)(4,1)S(1)}, s32[]{:S(2)}) async-start(s8[6291456]{0:T(1024)(128)(4,1)} %bitcast.89), calls=%async_computation.5 | async-start | bytes 4194304
  401.9 12.1 %copy-start = (bf16[384,2432]{1,0:T(8,128)(2,1)S(1)}, bf16[384,2432]{1,0:T(8,128)(2,1)}, u32[]{:S(2)}) copy-start(bf16[384,2432]{1,0:T(8,128)(2,1)} %get-tuple-element.290) | copy-start | bytes 5603332
  402.0 12.0 %collective-permute-start.32 = (bf16[16,24,2432]{2,1,0:T(8,128)(2,1)}, bf16[16,24,2432]{2,1,0:T(8,128)(2,1)S(1)}, u32[]{:S(2)}, u32[]{:S(2)}) collective-permute-start(bf16[16,24,2432]{2,1,0:T(8,128)(2,1)} %bitcast.109), channel_id=1, source_target_pairs={{0,8},{1,9},{2,10},{3,11},{4,12},{5,13},{6,14},{7,15},{8,0},{9,1},... | collective-permute-start | bytes 5603336 | tf_op jit(solution)/shard_map/ppermute | solution.py:472
  402.0 9.9 %collective-permute-start.33 = (bf16[4,24,3072]{2,1,0:T(8,128)(2,1)S(1)}, bf16[4,24,3072]{2,1,0:T(8,128)(2,1)S(1)}, u32[]{:S(2)}, u32[]{:S(2)}) collective-permute-start(bf16[4,24,3072]{2,1,0:T(8,128)(2,1)S(1)} %get-tuple-element.284), channel_id=1, source_target_pairs={{0,1},{1,0},{2,3},{3,2},{4,5},{5,4},{6,7},{7,6},{8,24},{9,25},{10,... | collective-permute-start | bytes 1769480 | tf_op jit(solution)/shard_map/ppermute | solution.py:472
  412.7 15.8 %collective-permute-start.35 = (bf16[2,24,3072]{2,1,0:T(8,128)(2,1)S(1)}, bf16[2,24,3072]{2,1,0:T(8,128)(2,1)S(1)}, u32[]{:S(2)}, u32[]{:S(2)}) collective-permute-start(bf16[2,24,3072]{2,1,0:T(8,128)(2,1)S(1)} %get-tuple-element.296), channel_id=1, source_target_pairs={{0,4},{1,5},{2,6},{3,7},{4,0},{5,1},{6,2},{7,3},{8,12},{9,13},{10,... | collective-permute-start | bytes 884744 | tf_op jit(solution)/shard_map/ppermute | solution.py:472
  415.1 13.6 %collective-permute-start.34 = (bf16[8,24,2432]{2,1,0:T(8,128)(2,1)S(1)}, bf16[8,24,2432]{2,1,0:T(8,128)(2,1)S(1)}, u32[]{:S(2)}, u32[]{:S(2)}) collective-permute-start(bf16[8,24,2432]{2,1,0:T(8,128)(2,1)S(1)} %get-tuple-element.300), channel_id=1, source_target_pairs={{0,16},{1,17},{2,18},{3,19},{4,20},{5,21},{6,22},{7,23},{8,9},{9,8... | collective-permute-start | bytes 2801672 | tf_op jit(solution)/shard_map/ppermute | solution.py:472
  428.6 11.4 %collective-permute-start.37 = (bf16[1,24,3072]{2,1,0:T(8,128)(2,1)S(1)}, bf16[1,24,3072]{2,1,0:T(8,128)(2,1)S(1)}, u32[]{:S(2)}, u32[]{:S(2)}) collective-permute-start(bf16[1,24,3072]{2,1,0:T(8,128)(2,1)S(1)} %get-tuple-element.305), channel_id=1, source_target_pairs={{0,2},{1,3},{2,0},{3,1},{4,6},{5,7},{6,4},{7,5},{8,10},{9,11},{10,... | collective-permute-start | bytes 442376 | tf_op jit(solution)/shard_map/ppermute | solution.py:472
  429.6 10.4 %collective-permute-start.36 = (bf16[4,24,2432]{2,1,0:T(8,128)(2,1)S(1)}, bf16[4,24,2432]{2,1,0:T(8,128)(2,1)S(1)}, u32[]{:S(2)}, u32[]{:S(2)}) collective-permute-start(bf16[4,24,2432]{2,1,0:T(8,128)(2,1)S(1)} %get-tuple-element.308), channel_id=1, source_target_pairs={{0,1},{1,0},{2,3},{3,2},{4,5},{5,4},{6,7},{7,6},{8,24},{9,25},{10,... | collective-permute-start | bytes 1400840 | tf_op jit(solution)/shard_map/ppermute | solution.py:472
  441.0 12.2 %collective-permute-start.38 = (bf16[2,24,2432]{2,1,0:T(8,128)(2,1)S(1)}, bf16[2,24,2432]{2,1,0:T(8,128)(2,1)S(1)}, u32[]{:S(2)}, u32[]{:S(2)}) collective-permute-start(bf16[2,24,2432]{2,1,0:T(8,128)(2,1)S(1)} %get-tuple-element.316), channel_id=1, source_target_pairs={{0,4},{1,5},{2,6},{3,7},{4,0},{5,1},{6,2},{7,3},{8,12},{9,13},{10,... | collective-permute-start | bytes 700424 | tf_op jit(solution)/shard_map/ppermute | solution.py:472
  453.2 4.9 %collective-permute-start.39 = (bf16[1,24,2432]{2,1,0:T(8,128)(2,1)S(1)}, bf16[1,24,2432]{2,1,0:T(8,128)(2,1)S(1)}, u32[]{:S(2)}, u32[]{:S(2)}) collective-permute-start(bf16[1,24,2432]{2,1,0:T(8,128)(2,1)S(1)} %get-tuple-element.320), channel_id=1, source_target_pairs={{0,2},{1,3},{2,0},{3,1},{4,6},{5,7},{6,4},{7,5},{8,10},{9,11},{10,... | collective-permute-start | bytes 350216 | tf_op jit(solution)/shard_map/ppermute | solution.py:472
  (20 other events, 40.1 us)
